TPU v7x, 128 devices: a whole 4x4x4 slice. The times are simulated.
128 devices in a mesh: group: 8 (over x_lo, y), ctx: 16 (over z, x_hi, core).
Axes of the slice: x: 4 (x_hi: 2, x_lo: 2; x = x_hi * 2 + x_lo), y: 4, z: 4, core: 2. Of those that a mesh axis runs over, the one named last changes fastest.
Arguments:
- query_latent: bfloat16 [80, 2, 1536], P('group'), may hold values from -6 to 6
- w_query: bfloat16 [1536, 12288], P(None, 'ctx'), may hold values from -0.15625 to 0.15625
- w_key_up: bfloat16 [64, 128, 512], P('ctx'), may hold values from -0.5 to 0.5
- w_value_up: bfloat16 [64, 512, 128], P('ctx'), may hold values from -0.25 to 0.25
- cache: bfloat16 [16, 12288, 576], P('group', 'ctx'), may hold values from -1900 to 1900
- fresh: bfloat16 [8, 8, 12288, 576], P('group', None, 'ctx'), may hold values from -1900 to 1900, as said below
- new_latent: bfloat16 [80, 2, 576], P('group'), may hold values from -6 to 6
- lengths: int32 [80], P('group'), may hold values from 1 to 12288
- fresh_slot: int32 [8, 8], P('group'), may hold values from 0 to 7, each once within a row
- positions: int32 [80, 2], P('group'), may hold values from 0 to 65535
Outputs:
- attended: bfloat16 [80, 2, 8192], P('group', None, 'ctx')
Inputs may be any that keep to these rules, and one draw needn't show every extreme that they name: `fresh`: latent cache entries. Each row of fresh_slot names every one of the 8 received slots once.
All inputs are finite; a program needn't handle non-finite values.
Results may differ from a plain program's by a relative error of at most 0.04.
Values may be sent and summed in bfloat16 or wider, within the bound.
No kernel may reach another device: no remote copies, remote signals or barrier semaphores. Data moves between devices by JAX's collectives and lax.ppermute only.
A program may use at most 128 MiB of HBM per device.

v0:
```python
import jax
import jax.numpy as jnp
from jax import lax
from jax.sharding import PartitionSpec as P

LAT = 512
ROPE = 64
NOPE = 128


def combined_all(part, axis, combine):
    gathered = jax.tree.map(lambda a: lax.all_gather(a, axis), part)

    def take(source):
        return jax.tree.map(lambda a: lax.dynamic_index_in_dim(a, source, 0, False), gathered)

    return lax.fori_loop(
        1, lax.axis_size(axis), lambda source, state: combine(state, take(source)), take(0)
    )


def rotate(values, where_at):
    half = values.shape[-1] // 2
    freqs = 50000.0 ** (-jnp.arange(half, dtype=jnp.float32) / half)
    angles = where_at.astype(jnp.float32)[..., None] * freqs
    cosine = jnp.cos(angles)
    sine = jnp.sin(angles)
    first = values[..., :half]
    second = values[..., half:]
    return jnp.concatenate([first * cosine - second * sine, second * cosine + first * sine], -1)


def local_softmax(queries, keys, row_lengths, offset, score_scale):
    scores = (
        jnp.einsum("rqw,rtw->rqt", queries, keys, preferred_element_type=jnp.float32) * score_scale
    )
    places = offset + jnp.arange(keys.shape[1], dtype=jnp.int32)
    live = places[None, None, :] < row_lengths[:, None, None]
    scores = jnp.where(live, scores, -1e30)
    highest = jnp.max(scores, -1)
    weights = jnp.where(live, jnp.exp(scores - highest[..., None]), 0.0)
    total = jnp.sum(weights, -1)
    summed = jnp.einsum(
        "rqt,rtl->rql",
        weights.astype(jnp.bfloat16),
        keys[..., :LAT],
        preferred_element_type=jnp.float32,
    )
    return (highest, total, summed)


def joined(first, second):
    highest = jnp.maximum(first[0], second[0])
    fade_first = jnp.exp(first[0] - highest)
    fade_second = jnp.exp(second[0] - highest)
    total = first[1] * fade_first + second[1] * fade_second
    summed = first[2] * fade_first[..., None] + second[2] * fade_second[..., None]
    return (highest, total, summed)


def local(
    query_latent,
    w_query,
    w_key_up,
    w_value_up,
    cache,
    fresh,
    new_latent,
    lengths,
    fresh_slot,
    positions,
):
    rows = query_latent.shape[0]
    tokens = cache.shape[1]
    width = cache.shape[2]
    heads_here = w_key_up.shape[0]
    shards = lax.axis_size("ctx")
    heads = heads_here * shards
    score_scale = (NOPE + ROPE) ** (-0.5)
    offset = lax.axis_index("ctx") * tokens
    qfull = jnp.dot(query_latent.reshape(rows * 2, -1), w_query, preferred_element_type=jnp.float32)
    qfull = qfull.astype(jnp.bfloat16).reshape(rows, 2, heads_here, NOPE + ROPE)
    latent_query = jnp.einsum(
        "rshn,hnl->rshl", qfull[..., :NOPE], w_key_up, preferred_element_type=jnp.float32
    )
    rotated = rotate(qfull[..., NOPE:].astype(jnp.float32), positions[:, :, None])
    own_query = jnp.concatenate([latent_query, rotated], -1).astype(jnp.bfloat16)
    all_query = lax.all_gather(own_query, "ctx", axis=2, tiled=True)
    all_query = all_query.reshape(rows, 2 * heads, width)
    received = lax.all_to_all(fresh, "group", split_axis=1, concat_axis=0, tiled=True)
    received = received.reshape(-1, tokens, width)
    picked = jnp.take(received, fresh_slot[0], axis=0)
    keys = jnp.concatenate([cache, picked], 0)
    highest, total, summed = local_softmax(all_query, keys, lengths, offset, score_scale)
    highest = highest.reshape(rows, 2, heads)
    total = total.reshape(rows, 2, heads)
    summed = summed.reshape(rows, 2, heads, LAT)
    highest, total, summed = combined_all((highest, total, summed), "ctx", joined)
    first_head = lax.axis_index("ctx") * heads_here
    highest = lax.dynamic_slice_in_dim(highest, first_head, heads_here, 2)
    total = lax.dynamic_slice_in_dim(total, first_head, heads_here, 2)
    summed = lax.dynamic_slice_in_dim(summed, first_head, heads_here, 2)
    new_keys = jnp.concatenate(
        [
            new_latent[..., :LAT].astype(jnp.float32),
            rotate(new_latent[..., LAT:].astype(jnp.float32), positions),
        ],
        -1,
    ).astype(jnp.bfloat16)
    new_scores = (
        jnp.einsum("rshw,rjw->rshj", own_query, new_keys, preferred_element_type=jnp.float32)
        * score_scale
    )
    allowed = (jnp.arange(2, dtype=jnp.int32)[None, :] <= jnp.arange(2, dtype=jnp.int32)[:, None])[
        None, :, None, :
    ]
    new_scores = jnp.where(allowed, new_scores, -1e30)
    top = jnp.maximum(highest, jnp.max(new_scores, -1))
    new_weights = jnp.where(allowed, jnp.exp(new_scores - top[..., None]), 0.0)
    fade = jnp.exp(highest - top)
    total = total * fade + jnp.sum(new_weights, -1)
    summed = summed * fade[..., None] + jnp.einsum(
        "rshj,rjl->rshl",
        new_weights.astype(jnp.bfloat16),
        new_keys[..., :LAT],
        preferred_element_type=jnp.float32,
    )
    latent_out = (summed / total[..., None]).astype(jnp.bfloat16)
    attended = jnp.einsum(
        "rshl,hlv->rshv", latent_out, w_value_up, preferred_element_type=jnp.float32
    )
    return attended.astype(jnp.bfloat16).reshape(rows, 2, -1)


def solution(mesh):
    placed = (
        P("group", None, None),
        P(None, "ctx"),
        P("ctx", None, None),
        P("ctx", None, None),
        P("group", "ctx", None),
        P("group", None, "ctx", None),
        P("group", None, None),
        P("group"),
        P("group", None),
        P("group", None),
    )
    return jax.shard_map(
        local, mesh=mesh, in_specs=placed, out_specs=P("group", None, "ctx"), check_vma=False
    )
```

profile of v0, /device:TPU:0, one launch (start us, length us, event | category | flops | bytes accessed | tf_op | source)
XLA Modules:
  0.0 426.8 jit_solution(15259516055967524165)
XLA Ops:
  6.5 5.8 %all-to-all-start = ((bf16[1,8,768,576]{2,3,0,1:T(8,128)(2,1)}), bf16[1,8,768,576]{2,3,0,1:T(8,128)(2,1)}, u32[]{:S(2)}, u32[]{:S(2)}) async-start(bf16[1,8,768,576]{2,3,0,1:T(8,128)(2,1)} %bitcast.64), calls=%async_computation | async-start | bytes 14155776 | tf_op jit(solution)/shard_map/all_to_all | solution.py:90
  13.8 0.7 copy.35
  14.8 53.9 %all-gather.3.cloned.1.call-done = bf16[10,2,64,576]{3,1,0,2:T(2,128)(2,1)} async-done(((bf16[10,2,4,576]{3,1,0,2:T(2,128)(2,1)}), bf16[10,2,64,576]{3,1,0,2:T(2,128)(2,1)}) %all-gather.3.cloned.1.call-update) | async-done | bytes 1474576 | tf_op jit(solution)/shard_map/all_gather | solution.py:88
  68.7 1.7 copy.36
  70.4 25.8 %all-to-all-done = bf16[1,8,768,576]{2,3,0,1:T(8,128)(2,1)} async-done(((bf16[1,8,768,576]{2,3,0,1:T(8,128)(2,1)}), bf16[1,8,768,576]{2,3,0,1:T(8,128)(2,1)}, u32[]{:S(2)}, u32[]{:S(2)}) %all-to-all-start) | async-done | bytes 7077920 | tf_op jit(solution)/shard_map/all_to_all | solution.py:90
  96.2 7.0 %gather_fusion = bf16[8,768,576]{1,2,0:T(8,128)(2,1)} fusion(bf16[8,768,576]{1,2,0:T(8,128)(2,1)} %bitcast.9, s32[1024]{0:T(1024)S(1)} %pad_clamp_fusion), kind=kCustom, calls=%fused_computation | custom fusion | bytes 14155808 | tf_op jit(solution)/shard_map/jit(_take)/gather | solution.py:92
  103.1 3.8 broadcast_select_fusion
  106.9 4.0 fusion.11
  111.0 6.0 %fusion.7 = f32[10,128,512]{2,1,0:T(8,128)} fusion(bf16[8,768,576]{1,2,0:T(8,128)(2,1)S(1)} %broadcast_select_fusion, bf16[2,768,576]{1,2,0:T(8,128)(2,1)S(1)} %copy-done.9, f32[10,128,768]{2,1,0:T(8,128)S(1)} %get-tuple-element.213, f32[10,128]{1,0:T(8,128)S(1)} %get-tuple-element.212, pred[10,768]{1,0:T(8,128)(4,1)S(1)} %broadcast_compare_fusion), kind=kOutput, calls=%fused_computation.13 | convolution fusion | flops 1027276800 | bytes 15413760 | tf_op jit(solution)/shard_map/rqt,rtl->rql/dot_general | solution.py:43
  117.0 0.7 fusion.47
  117.8 3.4 fusion.13
  121.2 26.5 %all_gather.14 = f32[16,10,2,64]{3,2,1,0:T(2,128)S(1)} all-gather(f32[1,10,2,64]{3,2,1,0:T(2,128)S(1)} %all_gather_reshape.10), channel_id=1, replica_groups=mesh['group'=8,'ctx'=16] {'ctx'}, dimensions={0}, use_global_device_ids=true | all-gather | bytes 87040 | tf_op jit(solution)/shard_map/all_gather | solution.py:12
  147.8 20.9 %all_gather.13 = f32[16,10,2,64]{3,2,1,0:T(2,128)S(1)} all-gather(f32[1,10,2,64]{3,2,1,0:T(2,128)S(1)} %all_gather_reshape.9), channel_id=1, replica_groups=mesh['group'=8,'ctx'=16] {'ctx'}, dimensions={0}, use_global_device_ids=true | all-gather | bytes 87040 | tf_op jit(solution)/shard_map/all_gather | solution.py:12
  168.7 176.8 %all-gather.5.cloned.1.call-done = f32[16,10,2,64,512]{4,3,2,1,0:T(8,128)} async-done(((f32[1,10,2,64,512]{4,3,2,1,0:T(8,128)}), f32[16,10,2,64,512]{4,3,2,1,0:T(8,128)}) %all-gather.5.cloned.1.call-update) | async-done | bytes 41943056 | tf_op jit(solution)/shard_map/all_gather | solution.py:12
  345.5 3.6 slice_bitcast_fusion
  349.1 68.2 %while.19 = (s32[]{:T(128)}, f32[10,2,64]{2,1,0:T(2,128)S(1)}, f32[10,2,64]{2,1,0:T(2,128)S(1)}, f32[10,2,64,512]{3,2,1,0:T(8,128)}, f32[16,10,2,64]{3,2,1,0:T(2...) while((s32[]{:T(128)}, f32[10,2,64]{2,1,0:T(2,128)S(1)}, ...), condition=%wide.region_3.4_spmd, body=%wide.region_2.3_spmd.sunk | while | flops 1973765 | bytes 7915663 | solution.py:17
  349.1 4.6 %fusion.54 = f32[10,2,64,512]{3,2,1,0:T(8,128)} fusion(f32[16,10,2,64,512]{4,3,2,1,0:T(8,128)} %get-tuple-element.293, s32[]{:T(128)S(6)} %select_n.95, f32[10,2,64,512]{3,2,1,0:T(8,128)} %get-tuple-element.280, f32[10,2,64]{2,1,0:T(2,128)S(1)} %get-tuple-element.265, f32[10,2,64]{2,1,0:T(2,128)S(1)} %get-tuple-element.266), kind=kLoop, calls=%fused_computation.2.clone.1 | loop fusion | flops 1966080 | bytes 7874564 | tf_op jit(solution)/shard_map/while/body/eval_jaxpr/add | solution.py:57
  353.7 4.5 %fusion.54 = f32[10,2,64,512]{3,2,1,0:T(8,128)} fusion(f32[16,10,2,64,512]{4,3,2,1,0:T(8,128)} %get-tuple-element.293, s32[]{:T(128)S(6)} %select_n.95, f32[10,2,64,512]{3,2,1,0:T(8,128)} %get-tuple-element.280, f32[10,2,64]{2,1,0:T(2,128)S(1)} %get-tuple-element.265, f32[10,2,64]{2,1,0:T(2,128)S(1)} %get-tuple-element.266), kind=kLoop, calls=%fused_computation.2.clone.1 | loop fusion | flops 1966080 | bytes 7874564 | tf_op jit(solution)/shard_map/while/body/eval_jaxpr/add | solution.py:57
  358.3 4.5 %fusion.54 = f32[10,2,64,512]{3,2,1,0:T(8,128)} fusion(f32[16,10,2,64,512]{4,3,2,1,0:T(8,128)} %get-tuple-element.293, s32[]{:T(128)S(6)} %select_n.95, f32[10,2,64,512]{3,2,1,0:T(8,128)} %get-tuple-element.280, f32[10,2,64]{2,1,0:T(2,128)S(1)} %get-tuple-element.265, f32[10,2,64]{2,1,0:T(2,128)S(1)} %get-tuple-element.266), kind=kLoop, calls=%fused_computation.2.clone.1 | loop fusion | flops 1966080 | bytes 7874564 | tf_op jit(solution)/shard_map/while/body/eval_jaxpr/add | solution.py:57
  362.8 4.5 %fusion.54 = f32[10,2,64,512]{3,2,1,0:T(8,128)} fusion(f32[16,10,2,64,512]{4,3,2,1,0:T(8,128)} %get-tuple-element.293, s32[]{:T(128)S(6)} %select_n.95, f32[10,2,64,512]{3,2,1,0:T(8,128)} %get-tuple-element.280, f32[10,2,64]{2,1,0:T(2,128)S(1)} %get-tuple-element.265, f32[10,2,64]{2,1,0:T(2,128)S(1)} %get-tuple-element.266), kind=kLoop, calls=%fused_computation.2.clone.1 | loop fusion | flops 1966080 | bytes 7874564 | tf_op jit(solution)/shard_map/while/body/eval_jaxpr/add | solution.py:57
  367.4 4.5 %fusion.54 = f32[10,2,64,512]{3,2,1,0:T(8,128)} fusion(f32[16,10,2,64,512]{4,3,2,1,0:T(8,128)} %get-tuple-element.293, s32[]{:T(128)S(6)} %select_n.95, f32[10,2,64,512]{3,2,1,0:T(8,128)} %get-tuple-element.280, f32[10,2,64]{2,1,0:T(2,128)S(1)} %get-tuple-element.265, f32[10,2,64]{2,1,0:T(2,128)S(1)} %get-tuple-element.266), kind=kLoop, calls=%fused_computation.2.clone.1 | loop fusion | flops 1966080 | bytes 7874564 | tf_op jit(solution)/shard_map/while/body/eval_jaxpr/add | solution.py:57
  371.9 4.5 %fusion.54 = f32[10,2,64,512]{3,2,1,0:T(8,128)} fusion(f32[16,10,2,64,512]{4,3,2,1,0:T(8,128)} %get-tuple-element.293, s32[]{:T(128)S(6)} %select_n.95, f32[10,2,64,512]{3,2,1,0:T(8,128)} %get-tuple-element.280, f32[10,2,64]{2,1,0:T(2,128)S(1)} %get-tuple-element.265, f32[10,2,64]{2,1,0:T(2,128)S(1)} %get-tuple-element.266), kind=kLoop, calls=%fused_computation.2.clone.1 | loop fusion | flops 1966080 | bytes 7874564 | tf_op jit(solution)/shard_map/while/body/eval_jaxpr/add | solution.py:57
  376.5 4.5 %fusion.54 = f32[10,2,64,512]{3,2,1,0:T(8,128)} fusion(f32[16,10,2,64,512]{4,3,2,1,0:T(8,128)} %get-tuple-element.293, s32[]{:T(128)S(6)} %select_n.95, f32[10,2,64,512]{3,2,1,0:T(8,128)} %get-tuple-element.280, f32[10,2,64]{2,1,0:T(2,128)S(1)} %get-tuple-element.265, f32[10,2,64]{2,1,0:T(2,128)S(1)} %get-tuple-element.266), kind=kLoop, calls=%fused_computation.2.clone.1 | loop fusion | flops 1966080 | bytes 7874564 | tf_op jit(solution)/shard_map/while/body/eval_jaxpr/add | solution.py:57
  381.0 4.5 %fusion.54 = f32[10,2,64,512]{3,2,1,0:T(8,128)} fusion(f32[16,10,2,64,512]{4,3,2,1,0:T(8,128)} %get-tuple-element.293, s32[]{:T(128)S(6)} %select_n.95, f32[10,2,64,512]{3,2,1,0:T(8,128)} %get-tuple-element.280, f32[10,2,64]{2,1,0:T(2,128)S(1)} %get-tuple-element.265, f32[10,2,64]{2,1,0:T(2,128)S(1)} %get-tuple-element.266), kind=kLoop, calls=%fused_computation.2.clone.1 | loop fusion | flops 1966080 | bytes 7874564 | tf_op jit(solution)/shard_map/while/body/eval_jaxpr/add | solution.py:57
  385.5 4.5 %fusion.54 = f32[10,2,64,512]{3,2,1,0:T(8,128)} fusion(f32[16,10,2,64,512]{4,3,2,1,0:T(8,128)} %get-tuple-element.293, s32[]{:T(128)S(6)} %select_n.95, f32[10,2,64,512]{3,2,1,0:T(8,128)} %get-tuple-element.280, f32[10,2,64]{2,1,0:T(2,128)S(1)} %get-tuple-element.265, f32[10,2,64]{2,1,0:T(2,128)S(1)} %get-tuple-element.266), kind=kLoop, calls=%fused_computation.2.clone.1 | loop fusion | flops 1966080 | bytes 7874564 | tf_op jit(solution)/shard_map/while/body/eval_jaxpr/add | solution.py:57
  390.1 4.5 %fusion.54 = f32[10,2,64,512]{3,2,1,0:T(8,128)} fusion(f32[16,10,2,64,512]{4,3,2,1,0:T(8,128)} %get-tuple-element.293, s32[]{:T(128)S(6)} %select_n.95, f32[10,2,64,512]{3,2,1,0:T(8,128)} %get-tuple-element.280, f32[10,2,64]{2,1,0:T(2,128)S(1)} %get-tuple-element.265, f32[10,2,64]{2,1,0:T(2,128)S(1)} %get-tuple-element.266), kind=kLoop, calls=%fused_computation.2.clone.1 | loop fusion | flops 1966080 | bytes 7874564 | tf_op jit(solution)/shard_map/while/body/eval_jaxpr/add | solution.py:57
  394.6 4.5 %fusion.54 = f32[10,2,64,512]{3,2,1,0:T(8,128)} fusion(f32[16,10,2,64,512]{4,3,2,1,0:T(8,128)} %get-tuple-element.293, s32[]{:T(128)S(6)} %select_n.95, f32[10,2,64,512]{3,2,1,0:T(8,128)} %get-tuple-element.280, f32[10,2,64]{2,1,0:T(2,128)S(1)} %get-tuple-element.265, f32[10,2,64]{2,1,0:T(2,128)S(1)} %get-tuple-element.266), kind=kLoop, calls=%fused_computation.2.clone.1 | loop fusion | flops 1966080 | bytes 7874564 | tf_op jit(solution)/shard_map/while/body/eval_jaxpr/add | solution.py:57
  399.2 4.5 %fusion.54 = f32[10,2,64,512]{3,2,1,0:T(8,128)} fusion(f32[16,10,2,64,512]{4,3,2,1,0:T(8,128)} %get-tuple-element.293, s32[]{:T(128)S(6)} %select_n.95, f32[10,2,64,512]{3,2,1,0:T(8,128)} %get-tuple-element.280, f32[10,2,64]{2,1,0:T(2,128)S(1)} %get-tuple-element.265, f32[10,2,64]{2,1,0:T(2,128)S(1)} %get-tuple-element.266), kind=kLoop, calls=%fused_computation.2.clone.1 | loop fusion | flops 1966080 | bytes 7874564 | tf_op jit(solution)/shard_map/while/body/eval_jaxpr/add | solution.py:57
  403.7 4.5 %fusion.54 = f32[10,2,64,512]{3,2,1,0:T(8,128)} fusion(f32[16,10,2,64,512]{4,3,2,1,0:T(8,128)} %get-tuple-element.293, s32[]{:T(128)S(6)} %select_n.95, f32[10,2,64,512]{3,2,1,0:T(8,128)} %get-tuple-element.280, f32[10,2,64]{2,1,0:T(2,128)S(1)} %get-tuple-element.265, f32[10,2,64]{2,1,0:T(2,128)S(1)} %get-tuple-element.266), kind=kLoop, calls=%fused_computation.2.clone.1 | loop fusion | flops 1966080 | bytes 7874564 | tf_op jit(solution)/shard_map/while/body/eval_jaxpr/add | solution.py:57
  408.3 4.5 %fusion.54 = f32[10,2,64,512]{3,2,1,0:T(8,128)} fusion(f32[16,10,2,64,512]{4,3,2,1,0:T(8,128)} %get-tuple-element.293, s32[]{:T(128)S(6)} %select_n.95, f32[10,2,64,512]{3,2,1,0:T(8,128)} %get-tuple-element.280, f32[10,2,64]{2,1,0:T(2,128)S(1)} %get-tuple-element.265, f32[10,2,64]{2,1,0:T(2,128)S(1)} %get-tuple-element.266), kind=kLoop, calls=%fused_computation.2.clone.1 | loop fusion | flops 1966080 | bytes 7874564 | tf_op jit(solution)/shard_map/while/body/eval_jaxpr/add | solution.py:57
  412.8 4.5 %fusion.54 = f32[10,2,64,512]{3,2,1,0:T(8,128)} fusion(f32[16,10,2,64,512]{4,3,2,1,0:T(8,128)} %get-tuple-element.293, s32[]{:T(128)S(6)} %select_n.95, f32[10,2,64,512]{3,2,1,0:T(8,128)} %get-tuple-element.280, f32[10,2,64]{2,1,0:T(2,128)S(1)} %get-tuple-element.265, f32[10,2,64]{2,1,0:T(2,128)S(1)} %get-tuple-element.266), kind=kLoop, calls=%fused_computation.2.clone.1 | loop fusion | flops 1966080 | bytes 7874564 | tf_op jit(solution)/shard_map/while/body/eval_jaxpr/add | solution.py:57
  417.6 1.4 fusion.22
  (75 shorter events, 3.4 us)
Async XLA Ops:
  6.5 5.9 %copy-start = (bf16[1536,768]{1,0:T(8,128)(2,1)S(1)}, bf16[1536,768]{1,0:T(8,128)(2,1)}, u32[]{:S(2)}) copy-start(bf16[1536,768]{1,0:T(8,128)(2,1)} %param.13) | copy-start | bytes 7077892
  6.5 5.8 %copy-start.5 = (bf16[10,2,1536]{2,1,0:T(2,128)(2,1)S(1)}, bf16[10,2,1536]{2,1,0:T(2,128)(2,1)}, u32[]{:S(2)}) copy-start(bf16[10,2,1536]{2,1,0:T(2,128)(2,1)} %param.12) | copy-start | bytes 184324
  6.5 6.5 %copy-start.7 = (s32[10,2]{0,1:T(2,128)S(1)}, s32[10,2]{0,1:T(2,128)}, u32[]{:S(2)}) copy-start(s32[10,2]{0,1:T(2,128)} %param.21) | copy-start | bytes 244
  6.5 6.6 %copy-start.6 = (bf16[10,2,576]{2,1,0:T(2,128)(2,1)S(1)}, bf16[10,2,576]{2,1,0:T(2,128)(2,1)}, u32[]{:S(2)}) copy-start(bf16[10,2,576]{2,1,0:T(2,128)(2,1)} %param.18) | copy-start | bytes 69124
  6.5 7.0 %copy-start.3 = (bf16[4,128,512]{2,1,0:T(8,128)(2,1)S(1)}, bf16[4,128,512]{2,1,0:T(8,128)(2,1)}, u32[]{:S(2)}) copy-start(bf16[4,128,512]{2,1,0:T(8,128)(2,1)} %param.14) | copy-start | bytes 1572868
  6.5 89.6 %all-to-all-start = ((bf16[1,8,768,576]{2,3,0,1:T(8,128)(2,1)}), bf16[1,8,768,576]{2,3,0,1:T(8,128)(2,1)}, u32[]{:S(2)}, u32[]{:S(2)}) async-start(bf16[1,8,768,576]{2,3,0,1:T(8,128)(2,1)} %bitcast.64), calls=%async_computation | async-start | bytes 14155776 | tf_op jit(solution)/shard_map/all_to_all | solution.py:90
  12.3 2.3 copy-start.10
  12.3 2.4 copy-start.8
  12.3 56.4 %all-gather.3.cloned.1.call-start = ((), (), s32[]{:S(2)}) async-start(), calls=%async_computation.1 | async-start | bytes 1740800 | tf_op jit(solution)/shard_map/all_gather | solution.py:88
  14.6 330.9 %all-gather.5.cloned.1.call-start = ((), (), s32[]{:S(2)}) async-start(), calls=%async_computation.2 | async-start | bytes 44564480 | tf_op jit(solution)/shard_map/all_gather | solution.py:12
  106.9 4.1 copy-start.9
  110.9 6.0 %copy-start.2 = (f32[10,128,768]{2,1,0:T(8,128)}, f32[10,128,768]{2,1,0:T(8,128)S(1)}, u32[]{:S(2)}) copy-start(f32[10,128,768]{2,1,0:T(8,128)S(1)} %get-tuple-element.213) | copy-start | bytes 11796484
  111.0 6.1 %slice-start = ((bf16[10,2,576]{2,1,0:T(2,128)(2,1)}), bf16[10,2,512]{2,1,0:T(2,128)(2,1)S(1)}, s32[]{:S(2)}) async-start(bf16[10,2,576]{2,1,0:T(2,128)(2,1)} %param.18), calls=%async_computation.3 | async-start | bytes 40960 | tf_op jit(solution)/shard_map/slice | solution.py:105
  349.1 70.0 %copy-start.4 = (bf16[4,512,128]{2,1,0:T(8,128)(2,1)S(1)}, bf16[4,512,128]{2,1,0:T(8,128)(2,1)}, u32[]{:S(2)}) copy-start(bf16[4,512,128]{2,1,0:T(8,128)(2,1)} %param.15) | copy-start | bytes 1572868
  417.3 2.6 copy-start.1
Sparse Core Ops, SparseCore 0:
  15.6 53.0 all-gather.2
  117.1 228.3 all-gather.4
where the time goes:
time: 428 us; the launch traced here: 427 us
  waiting for transfers between devices  256 us (60%)
  other arithmetic  76.2 us (18%)
  blocking collectives  47.5 us (11%)
  local copies, waits for them, and re-layouts  14.1 us (3%)
  between operations  13.7 us (3%)
  matrix products  13 us (3%)
  starting transfers between devices  5.84 us (1%)
    all_gather x1, waiting for transfers between devices, combined_all(): gathered = jax.tree.map(lambda a: lax.all_gather(a, axis), part)  177 us
    add x15, other arithmetic, joined(): first[2] * fade_first[..., None] + second[2] * fade_second[..., None]  67.7 us
    all_gather x1, waiting for transfers between devices, local(): all_query = lax.all_gather(own_query, 'ctx', axis=2, tiled=True)  53.9 us
    all_gather x2, blocking collectives, combined_all(): gathered = jax.tree.map(lambda a: lax.all_gather(a, axis), part)  47.5 us
    all_to_all x1, waiting for transfers between devices, local(): lax.all_to_all(fresh, 'group', split_axis=1, concat_axis=0, tiled=True)  25.8 us
  transfers between devices with their start and end apart: 3, of which 3 were waited for; matrix products, arithmetic and copies ran while one was open for 2% of the time, Pallas kernels for 0%

commit v1 on v0

v1 whole, which is shorter than its diff:
```python
import functools
import math

import jax
import jax.numpy as jnp
import numpy as np
from jax import lax
from jax.experimental import pallas as pl
from jax.experimental.pallas import tpu as pltpu
from jax.sharding import Mesh
from jax.sharding import PartitionSpec as P

LAT = 512
ROPE = 64
NOPE = 128
HEAD = NOPE + ROPE
WIDE = 640
SCALE = HEAD ** (-0.5)
NONE = -1e30
BF = jnp.bfloat16
F32 = jnp.float32

HALF_PI = (1.5703125, 0.0004825592041015625, 1.2676710047e-06)


def dot(a, b, contract=((1,), (0,))):
    return lax.dot_general(a, b, (contract, ((), ())), preferred_element_type=F32)


def iota(shape, dim):
    return lax.broadcasted_iota(jnp.int32, shape, dim)


def cos_sin(angle):
    turns = jnp.floor(angle * (2.0 / math.pi) + 0.5)
    rest = angle - turns * HALF_PI[0]
    rest = rest - turns * HALF_PI[1]
    rest = rest - turns * HALF_PI[2]
    sq = rest * rest
    sine = rest + rest * sq * (
        -1.6666654611e-1 + sq * (8.3321608736e-3 + sq * -1.9515295891e-4)
    )
    cosine = 1.0 - 0.5 * sq + sq * sq * (
        4.166664568298827e-2 + sq * (-1.388731625493765e-3 + sq * 2.443315711809948e-5)
    )
    quarter = turns.astype(jnp.int32) & 3
    swapped = (quarter & 1) == 1
    first = jnp.where(swapped, sine, cosine)
    second = jnp.where(swapped, cosine, sine)
    first = jnp.where((quarter == 1) | (quarter == 2), -first, first)
    second = jnp.where(quarter >= 2, -second, second)
    return first, second


def rope(values, cosine, signed_sine):
    half = ROPE // 2
    swapped = jnp.concatenate([values[:, half:], values[:, :half]], 1)
    return values * cosine + swapped * signed_sine


def per_row(ref, rows, width):
    count = 32
    at = iota((count, 1), 0)
    out = jnp.zeros((count, 1), jnp.int32)
    for r in range(rows):
        if width is None:
            out = jnp.where(at // 2 == r, ref[r], out)
        else:
            for s in range(width):
                out = jnp.where(at == r * width + s, ref[r, s], out)
    return out


def angles_of(pos_ref, freq_ref, rows):
    at = per_row(pos_ref, rows, 2).astype(F32)
    cosine, sine = cos_sin(at * freq_ref[...])
    signed = jnp.where(iota((1, ROPE), 1) < ROPE // 2, -1.0, 1.0) * sine
    return cosine, signed


def row_of(slot_ref, slots, resident, shape, dim, per):
    at = iota(shape, dim)
    slot = at // per
    out = slot - slots
    for j in range(slots):
        out = jnp.where(slot == slot_ref[0, j], resident + j, out)
    return out


def project_kernel(heads, slots, copies, slot_ref, len_ref, pos_ref, ql_ref, wq_ref, wk_ref, freq_ref,
                   out_ref, res_ref, own_ref, rows_ref, all_ref):
    rows = ql_ref.shape[0]
    resident = rows - slots
    rows_ref[...] = jnp.zeros_like(rows_ref)
    for r in range(rows):
        rows_ref[2 * r : 2 * r + 2, :] = ql_ref[r].astype(F32)
    qfull = dot(rows_ref[...].astype(BF), wq_ref[...]).astype(BF)
    cosine, signed = angles_of(pos_ref, freq_ref, rows)
    length = per_row(len_ref, rows, None)
    lane = iota((1, WIDE - LAT - ROPE), 1)
    meta = jnp.where(lane == 0, (length // 128).astype(F32), jnp.where(lane == 1, (length % 128).astype(F32), 0.0))
    for h in range(heads):
        part = qfull[:, h * HEAD : (h + 1) * HEAD]
        all_ref[h * 32 : (h + 1) * 32, :LAT] = dot(part[:, :NOPE], wk_ref[h]).astype(BF)
        tail = jnp.concatenate([rope(part[:, NOPE:].astype(F32), cosine, signed), meta], 1)
        all_ref[h * 32 : (h + 1) * 32, LAT:] = tail.astype(BF)
    piece = 2 * heads
    count = rows * piece
    row = row_of(slot_ref, slots, resident, (count, 1), 0, piece)
    inner = iota((count, 1), 0) % piece
    source = (inner // 2) * 32 + 2 * row + inner % 2
    select = jnp.where(iota((count, heads * 32), 1) == source, 1.0, 0.0).astype(BF)
    own = dot(select, all_ref[...])
    own_ref[...] = own.astype(BF)
    for p in range(slots):
        one = own[p * piece : (p + 1) * piece]
        two = jnp.concatenate([one, one], 0).astype(BF)
        for k in range(0, copies, 2):
            at = (p * copies + k) * piece
            out_ref[at : at + 2 * piece, :] = two
    last = own[slots * piece :].astype(BF)
    for k in range(copies):
        at = k * resident * piece
        res_ref[at : at + resident * piece, :] = last


def own_keys_kernel(slots, slot_ref, pos_ref, nl_ref, freq_ref, own_ref, out_ref, stat_ref, keys_ref):
    rows = nl_ref.shape[0]
    resident = rows - slots
    count = own_ref.shape[0]
    piece = count // rows
    keys_ref[...] = jnp.zeros_like(keys_ref)
    for r in range(rows):
        keys_ref[2 * r : 2 * r + 2, :] = nl_ref[r].astype(F32)
    cosine, signed = angles_of(pos_ref, freq_ref, rows)
    latent = keys_ref[:, :LAT].astype(BF)
    turned = rope(keys_ref[:, LAT:], cosine, signed).astype(BF)
    scores = dot(own_ref[:, :LAT], latent, ((1,), (1,)))
    scores = scores + dot(own_ref[:, LAT : LAT + ROPE], turned, ((1,), (1,)))
    scores = scores * SCALE
    row = row_of(slot_ref, slots, resident, (count, 1), 0, piece)
    step = iota((count, 1), 0) % 2
    key = iota((1, 32), 1)
    allowed = (key // 2 == row) & (key % 2 <= step)
    highest = jnp.max(jnp.where(allowed, scores, NONE), 1, keepdims=True)
    weights = jnp.where(allowed, jnp.exp(scores - highest), 0.0)
    total = jnp.sum(weights, 1, keepdims=True)
    out_ref[...] = dot(weights.astype(BF), latent)
    lane = iota((1, 128), 1)
    stat_ref[...] = jnp.where(lane == 0, highest, total)


def parts_of(value):
    first = value.astype(BF).astype(F32)
    second = (value - first).astype(BF).astype(F32)
    return first, second, value - first - second


def with_stats(highest, total):
    lane = iota((1, 128), 1)
    out = 0.0
    for at, part in enumerate(parts_of(highest) + parts_of(total)):
        out = jnp.where(lane == at, part, out)
    return out.astype(BF)


def stats_of(tail):
    tail = tail.astype(F32)
    highest = tail[:, 0:1] + tail[:, 1:2] + tail[:, 2:3]
    total = tail[:, 3:4] + tail[:, 4:5] + tail[:, 5:6]
    return highest, total


def attend(queries, keys, offset):
    length = queries[:, LAT + ROPE : LAT + ROPE + 2].astype(F32)
    length = (length[:, 0:1] * 128.0 + length[:, 1:2]).astype(jnp.int32)
    scores = dot(queries[:, : LAT + ROPE], keys, ((1,), (1,))) * SCALE
    live = iota((1, keys.shape[0]), 1) < length - offset
    highest = jnp.max(jnp.where(live, scores, NONE), 1, keepdims=True)
    weights = jnp.where(live, jnp.exp(scores - highest), 0.0)
    total = jnp.sum(weights, 1, keepdims=True)
    summed = dot(weights.astype(BF), keys[:, :LAT])
    return highest, total, summed / jnp.maximum(total, 1e-30)


def attend_new_kernel(offset_ref, own_ref, other_ref, keys_ref, send_ref, keep_ref, stat_ref):
    half = own_ref.shape[0]
    queries = jnp.concatenate([other_ref[...], own_ref[...]], 0)
    highest, total, mean = attend(queries, keys_ref[0], offset_ref[0])
    send_ref[:, :LAT] = mean[:half].astype(BF)
    send_ref[:, LAT:] = with_stats(highest[:half], total[:half])
    keep_ref[...] = mean[half:]
    lane = iota((1, 128), 1)
    stat_ref[...] = jnp.where(lane == 0, highest[half:], total[half:])


def attend_resident_kernel(piece, offset_ref, own_ref, other_ref, keys_ref, send_ref, keep_ref, stat_ref):
    rows = keys_ref.shape[0]
    half = own_ref.shape[0]
    copies = half // rows // piece
    lane = iota((1, 128), 1)
    results = []
    for i in range(rows):
        at = [(k * rows + i) * piece for k in range(copies)]
        queries = [ref[a : a + piece, :] for ref in (other_ref, own_ref) for a in at]
        results.append(attend(jnp.concatenate(queries, 0), keys_ref[i], offset_ref[0]))
    n = copies * piece
    for k in range(copies):
        parts = [tuple(x[k * piece : (k + 1) * piece] for x in one) for one in results]
        highest, total, mean = (jnp.concatenate(x, 0) for x in zip(*parts))
        span = slice(k * rows * piece, (k + 1) * rows * piece)
        send_ref[span, :LAT] = mean.astype(BF)
        send_ref[span, LAT:] = with_stats(highest, total)
        parts = [tuple(x[n + k * piece : n + (k + 1) * piece] for x in one) for one in results]
        highest, total, mean = (jnp.concatenate(x, 0) for x in zip(*parts))
        keep_ref[span, :] = mean
        stat_ref[span, :] = jnp.where(lane == 0, highest, total)


def join_kernel(got_ref, keep_ref, stat_ref, out_ref):
    far_highest, far_total = stats_of(got_ref[:, LAT:])
    highest, total = stat_ref[:, 0:1], stat_ref[:, 1:2]
    top = jnp.maximum(far_highest, highest)
    far_total = far_total * jnp.exp(far_highest - top)
    total = total * jnp.exp(highest - top)
    both = total + far_total
    scale = 1.0 / jnp.maximum(both, 1e-30)
    mean = got_ref[:, :LAT].astype(F32) * (far_total * scale) + keep_ref[...] * (total * scale)
    out_ref[:, :LAT] = mean.astype(BF)
    out_ref[:, LAT:] = with_stats(top, both)


def finish_kernel(slots, slot_ref, new_ref, res_ref, own_ref, stat_ref, wv_ref, out_ref):
    heads = wv_ref.shape[0]
    piece = 2 * heads
    rows = out_ref.shape[0]
    resident = rows - slots
    copies = new_ref.shape[0] // slots // piece

    def merged(ref, start, stride, n, own_at):
        spans = [slice(start + k * stride, start + k * stride + n) for k in range(copies)]
        stats = [stats_of(ref[s, LAT:]) for s in spans]
        stats.append((stat_ref[own_at : own_at + n, 0:1], stat_ref[own_at : own_at + n, 1:2]))
        top = functools.reduce(jnp.maximum, [h for h, _ in stats])
        fades = [jnp.exp(h - top) for h, _ in stats]
        total = sum(f * t for f, (_, t) in zip(fades, stats))
        summed = own_ref[own_at : own_at + n, :] * fades[-1]
        for s, f, (_, t) in zip(spans, fades, stats):
            summed = summed + ref[s, :LAT].astype(F32) * (f * t)
        return (summed / total).astype(BF)

    latent = [merged(new_ref, p * copies * piece, piece, piece, p * piece) for p in range(slots)]
    latent.append(merged(res_ref, 0, resident * piece, resident * piece, slots * piece))
    latent = jnp.concatenate(latent, 0)
    count = rows * piece
    inner = iota((count, 1), 0) % piece
    values = []
    for h in range(heads):
        one = dot(latent, wv_ref[h])
        values.append(jnp.where(inner // 2 == h, one, 0.0).astype(BF))
    values = jnp.concatenate(values, 1)
    row = row_of(slot_ref, slots, resident, (1, count), 1, piece)
    target = 2 * row + iota((1, count), 1) % 2
    select = jnp.where(iota((32, count), 0) == target, 1.0, 0.0).astype(BF)
    out = dot(select, values)
    for r in range(rows):
        out_ref[r] = out[2 * r : 2 * r + 2].astype(BF)


VMEM = pl.BlockSpec(memory_space=pltpu.VMEM)
SMEM = pl.BlockSpec(memory_space=pltpu.SMEM)


def shape(dims, dtype):
    return jax.ShapeDtypeStruct(dims, dtype)


def local(query_latent, w_query, w_key_up, w_value_up, cache, fresh, new_latent, lengths, fresh_slot, positions):
    rows, _, depth = query_latent.shape
    heads = w_key_up.shape[0]
    slots = fresh_slot.shape[1]
    resident = rows - slots
    tokens = cache.shape[1]
    copies = lax.axis_size("zx")
    piece = 2 * heads
    half = copies * piece
    params = pltpu.CompilerParams(vmem_limit_bytes=32 * 1024 * 1024)
    freqs = 50000.0 ** (-np.arange(ROPE // 2, dtype=np.float64) / (ROPE // 2))
    freqs = jnp.asarray(np.concatenate([freqs, freqs]).astype(np.float32)[None])
    offset = ((lax.axis_index("zx") * lax.axis_size("core") + lax.axis_index("core")) * tokens).reshape(1)

    out_q, res_q, own_q = pl.pallas_call(
        functools.partial(project_kernel, heads, slots, copies),
        out_shape=(
            shape((slots * half, WIDE), BF),
            shape((resident * half, WIDE), BF),
            shape((rows * piece, WIDE), BF),
        ),
        in_specs=[SMEM] * 3 + [VMEM] * 4,
        out_specs=[VMEM] * 3,
        scratch_shapes=[pltpu.VMEM((32, depth), F32), pltpu.VMEM((heads * 32, WIDE), BF)],
        compiler_params=params,
        name="project",
    )(fresh_slot, lengths, positions, query_latent, w_query, w_key_up, freqs)

    own_out, own_stat = pl.pallas_call(
        functools.partial(own_keys_kernel, slots),
        out_shape=(shape((rows * piece, LAT), F32), shape((rows * piece, 128), F32)),
        in_specs=[SMEM] * 2 + [VMEM] * 3,
        out_specs=[VMEM] * 2,
        scratch_shapes=[pltpu.VMEM((32, LAT + ROPE), F32)],
        compiler_params=params,
        name="own_keys",
    )(fresh_slot, positions, new_latent, freqs, own_q)

    def exchange(x, axes, n):
        return lax.all_to_all(x.reshape(n, -1, WIDE), axes, 0, 0, tiled=True).reshape(-1, WIDE)

    def swap(x):
        return lax.ppermute(x, "core", [(0, 1), (1, 0)])

    res_own = exchange(res_q, "zx", copies)
    new_own = exchange(out_q, ("group", "zx"), slots * copies)
    res_other = swap(res_own)
    new_other = swap(new_own)

    res_send, res_keep, res_stat = pl.pallas_call(
        functools.partial(attend_resident_kernel, piece),
        out_shape=(
            shape((resident * half, WIDE), BF),
            shape((resident * half, LAT), F32),
            shape((resident * half, 128), F32),
        ),
        in_specs=[SMEM] + [VMEM] * 3,
        out_specs=[VMEM] * 3,
        compiler_params=params,
        name="attend_resident",
    )(offset, res_own, res_other, cache)

    new_send, new_keep, new_stat = pl.pallas_call(
        attend_new_kernel,
        grid=(slots,),
        out_shape=(
            shape((slots * half, WIDE), BF),
            shape((slots * half, LAT), F32),
            shape((slots * half, 128), F32),
        ),
        in_specs=[
            SMEM,
            pl.BlockSpec((half, WIDE), lambda i: (i, 0)),
            pl.BlockSpec((half, WIDE), lambda i: (i, 0)),
            pl.BlockSpec((1, tokens, LAT + ROPE), lambda i: (i, 0, 0)),
        ],
        out_specs=[
            pl.BlockSpec((half, WIDE), lambda i: (i, 0)),
            pl.BlockSpec((half, LAT), lambda i: (i, 0)),
            pl.BlockSpec((half, 128), lambda i: (i, 0)),
        ],
        compiler_params=params,
        name="attend_new",
    )(offset, new_own, new_other, fresh[0])

    def join(got, keep, stat):
        return pl.pallas_call(
            join_kernel,
            out_shape=shape(got.shape, BF),
            in_specs=[VMEM] * 3,
            out_specs=VMEM,
            compiler_params=params,
            name="join_cores",
        )(got, keep, stat)

    res_back = exchange(join(swap(res_send), res_keep, res_stat), "zx", copies)
    new_back = exchange(join(swap(new_send), new_keep, new_stat), ("group", "zx"), slots * copies)

    return pl.pallas_call(
        functools.partial(finish_kernel, slots),
        out_shape=shape((rows, 2, heads * 128), BF),
        in_specs=[SMEM] + [VMEM] * 5,
        out_specs=VMEM,
        compiler_params=params,
        name="finish",
    )(fresh_slot, new_back, res_back, own_out, own_stat, w_value_up)


def solution(mesh):
    groups, shards = mesh.devices.shape
    split = Mesh(mesh.devices.reshape(groups, shards // 2, 2), ("group", "zx", "core"))
    ctx = ("zx", "core")
    placed = (
        P("group", None, None),
        P(None, ctx),
        P(ctx, None, None),
        P(ctx, None, None),
        P("group", ctx, None),
        P("group", None, ctx, None),
        P("group", None, None),
        P("group"),
        P("group", None),
        P("group", None),
    )
    return jax.shard_map(
        local, mesh=split, in_specs=placed, out_specs=P("group", None, ctx), check_vma=False
    )
```

time: 428 us -> 109 us (0.25)
  waiting for transfers between devices: 256 us -> 20.1 us
  other arithmetic: 76.2 us -> 0 us
  Pallas kernels: 0 us -> 19.5 us
  between operations: 13.7 us -> 0.1 us
  matrix products: 13 us -> 0 us
  blocking collectives: 47.5 us -> 37.1 us
  local copies, waits for them, and re-layouts: 14.1 us -> 22.3 us
    all_gather x2 -> x0, waiting for transfers between devices: 231 us -> none  [the longest x1 177 us: combined_all(): gathered = jax.tree.map(lambda a: lax.all_gather(a, axis), part)]
    add x32 -> x0, other arithmetic: 68.3 us -> none  [the longest x15 67.7 us: joined(): first[2] * fade_first[..., None] + second[2] * fade_second[..., None]]
    all_gather x2 -> x0, blocking collectives: 47.5 us -> none  [combined_all(): gathered = jax.tree.map(lambda a: lax.all_gather(a, axis), part)]
    all_to_all x0 -> x2, blocking collectives: none -> 37.1 us  [exchange(): lax.all_to_all(x.reshape(n, -1, WIDE), axes, 0, 0, tiled=True)]
    unnamed x22 -> x25, local copies, waits for them, and re-layouts: 0.05 us -> 22.3 us
    pallas_call x0 -> x7, Pallas kernels: none -> 19.5 us  [the longest x1 8.38 us: local(): pl.pallas_call(attend_new_kernel, grid=(slots,), out_shape=(shape((slots...]
    dot_general x7 -> x0, matrix products: 13 us -> none  [the longest x1 6.01 us: local_softmax(): jnp.einsum('rqt,rtl->rql', weights.astype(jnp.bfloat16), keys[..., :LAT],...]
    gather x1 -> x0, local copies, waits for them, and re-layouts: 6.95 us -> none  [local(): picked = jnp.take(received, fresh_slot[0], axis=0)]
  transfers between devices with their start and end apart: 3 -> 6, of which waited for: 3 -> 3; matrix products, arithmetic and copies ran while one was open for 2% -> 12% of each run, Pallas kernels for 0% -> 7%
where the time goes in v1:
time: 109 us; the launch traced here: 108 us
  blocking collectives  37.1 us (34%)
  local copies, waits for them, and re-layouts  22.3 us (20%)
  waiting for transfers between devices  20.1 us (18%)
  Pallas kernels  19.5 us (18%)
  starting transfers between devices  9.26 us (8%)
    all_to_all x2, blocking collectives, exchange(): lax.all_to_all(x.reshape(n, -1, WIDE), axes, 0, 0, tiled=True)  37.1 us
    unnamed x25, local copies, waits for them, and re-layouts  22.3 us
    all_to_all x2, waiting for transfers between devices, exchange(): lax.all_to_all(x.reshape(n, -1, WIDE), axes, 0, 0, tiled=True)  19 us
    pallas_call x1, Pallas kernels, local(): pl.pallas_call(attend_new_kernel, grid=(slots,), out_shape=(shape((slots...  8.38 us
    all_to_all x2, starting transfers between devices, exchange(): lax.all_to_all(x.reshape(n, -1, WIDE), axes, 0, 0, tiled=True)  8.15 us
    pallas_call x2, Pallas kernels, join(): pl.pallas_call(join_kernel, out_shape=shape(got.shape, BF), in_specs=[VME...  3.93 us
    pallas_call x1, Pallas kernels, local(): pl.pallas_call(functools.partial(attend_resident_kernel, piece), out_shap...  2.55 us
  transfers between devices with their start and end apart: 6, of which 3 were waited for; matrix products, arithmetic and copies ran while one was open for 12% of the time, Pallas kernels for 7%

profile of v1, /device:TPU:0, one launch (start us, length us, event | category | flops | bytes accessed | tf_op | source)
XLA Modules:
  0.0 108.4 jit_solution(16644526204994759722)
XLA Ops:
  0.0 0.8 copy.12.pos_ref
  0.8 1.7 %copy-done.1 = bf16[1536,768]{1,0:T(8,128)(2,1)S(1)} copy-done((bf16[1536,768]{1,0:T(8,128)(2,1)S(1)}, bf16[1536,768]{1,0:T(8,128)(2,1)}, u32[]{:S(2)}) %copy-start.1) | copy-done | bytes 2359320
  2.4 1.0 copy-done.3
  3.5 0.8 copy-done.4
  4.3 0.7 copy-done.6
  5.0 0.7 copy-done.8
  5.6 0.7 copy-done.10
  6.3 1.6 %project.1 = (bf16[512,640]{1,0:T(8,128)(2,1)S(1)}, bf16[128,640]{1,0:T(8,128)(2,1)S(1)}, bf16[80,640]{1,0:T(8,128)(2,1)S(1)}) custom-call(s32[1,8]{1,0:T(1,128)S(1)} %copy-done.6, s32[10]{0:T(128)S(1)} %copy-done.10, s32[10,2]{1,0:T(8,128)S(1)} %copy.12.pos_ref, bf16[10,2,1536]{2,1,0:T(2,128)(2,1)S(1)} %copy-done.4, bf16[1536,768]{1,0:T(8,128)(2,1)S(1)} %copy-done.1, ...), custom_call_target="tpu_custom_call" | custom-call | tf_op jit(solution)/shard_map/project/pallas_call | solution.py:292
  7.9 25.9 %all_to_all.20 = bf16[64,8,640]{2,1,0:T(8,128)(2,1)S(1)} all-to-all(bf16[64,8,640]{2,1,0:T(8,128)(2,1)S(1)} %bitcast.16), channel_id=1, replica_groups=mesh['group'=8,'zx'=8,'core'=2] {'group','zx'}, dimensions={0} | all-to-all | bytes 1310720 | tf_op jit(solution)/shard_map/all_to_all | solution.py:317
  33.8 0.0 collective-permute-start
  33.8 10.1 %copy.13 = bf16[1,8,768,576]{3,2,1,0:T(8,128)(2,1)} copy(bf16[1,8,768,576]{2,3,1,0:T(8,128)(2,1)} %param.16) | data formatting | bytes 14155776 | tf_op args[5]
  43.9 0.0 collective-permute-done.other_ref
  43.9 3.2 %copy-done = bf16[1,8,768,576]{3,2,1,0:T(8,128)(2,1)S(1)} copy-done((bf16[1,8,768,576]{3,2,1,0:T(8,128)(2,1)S(1)}, bf16[1,8,768,576]{3,2,1,0:T(8,128)(2,1)}, u32[]{:S(2)}) %copy-start) | copy-done | bytes 7077912
  47.1 8.4 %attend_new.1 = (bf16[512,640]{1,0:T(8,128)(2,1)}, f32[512,512]{1,0:T(8,128)S(1)}, f32[512,128]{1,0:T(8,128)S(1)}) custom-call(s32[1]{0:T(128)} %bitcast.offset_ref, bf16[512,640]{1,0:T(8,128)(2,1)S(1)} %bitcast.12, bf16[512,640]{1,0:T(8,128)(2,1)S(1)} %collective-permute-done.other_ref, bf16[8,768,576]{2,1,0:T(8,128)(2,1)S(1)} %bitcast.10), custom_call_target="tpu_custom_call" | custom-call | tf_op jit(solution)/shard_map/attend_new/pallas_call | solution.py:340
  55.5 0.5 collective-permute-start.1
  56.0 11.2 %all_to_all.21 = bf16[8,16,640]{2,1,0:T(8,128)(2,1)S(1)} all-to-all(bf16[8,16,640]{2,1,0:T(8,128)(2,1)S(1)} %bitcast.18), channel_id=1, replica_groups=mesh['group'=8,'zx'=8,'core'=2] {'zx'}, dimensions={0} | all-to-all | bytes 327680 | tf_op jit(solution)/shard_map/all_to_all | solution.py:317
  67.3 0.0 collective-permute-start.2
  67.3 2.7 %copy.14.keys_ref = bf16[2,768,576]{2,1,0:T(8,128)(2,1)S(1)} copy(bf16[2,768,576]{1,2,0:T(8,128)(2,1)} %param.15) | data formatting | bytes 3538944 | tf_op args[4]
  70.0 0.0 collective-permute-done.2.other_ref
  70.0 2.6 %attend_resident.1 = (bf16[128,640]{1,0:T(8,128)(2,1)S(1)}, f32[128,512]{1,0:T(8,128)S(1)}, f32[128,128]{1,0:T(8,128)S(1)}) custom-call(s32[1]{0:T(128)} %bitcast.offset_ref, bf16[128,640]{1,0:T(8,128)(2,1)S(1)} %bitcast.15, bf16[128,640]{1,0:T(8,128)(2,1)} %collective-permute-done.2.other_ref, bf16[2,768,576]{2,1,0:T(8,128)(2,1)S(1)} %copy.14.keys_ref), custom_call_target="tpu_custom_call" | custom-call | tf_op jit(solution)/shard_map/attend_resident/pallas_call | solution.py:327
  72.6 0.6 collective-permute-start.3
  73.2 1.0 collective-permute-done.3.got_ref
  74.2 1.1 %join_cores.3 = bf16[128,640]{1,0:T(8,128)(2,1)} custom-call(bf16[128,640]{1,0:T(8,128)(2,1)S(1)} %collective-permute-done.3.got_ref, f32[128,512]{1,0:T(8,128)S(1)} %get-tuple-element.22.keep_ref, f32[128,128]{1,0:T(8,128)S(1)} %get-tuple-element.23.stat_ref), custom_call_target="tpu_custom_call" | custom-call | tf_op jit(solution)/shard_map/join_cores/pallas_call | solution.py:364
  75.3 3.5 %all-to-all-start.3 = ((bf16[8,16,640]{2,1,0:T(8,128)(2,1)}), bf16[8,16,640]{2,1,0:T(8,128)(2,1)S(1)}, u32[]{:S(2)}, u32[]{:S(2)}) async-start(bf16[8,16,640]{2,1,0:T(8,128)(2,1)} %bitcast.8), calls=%async_computation.3 | async-start | bytes 327680 | tf_op jit(solution)/shard_map/all_to_all | solution.py:317
  78.8 0.0 collective-permute-done.1.got_ref
  78.9 2.8 %join_cores.2 = bf16[512,640]{1,0:T(8,128)(2,1)} custom-call(bf16[512,640]{1,0:T(8,128)(2,1)} %collective-permute-done.1.got_ref, f32[512,512]{1,0:T(8,128)S(1)} %get-tuple-element.18.keep_ref, f32[512,128]{1,0:T(8,128)S(1)} %get-tuple-element.19.stat_ref), custom_call_target="tpu_custom_call" | custom-call | tf_op jit(solution)/shard_map/join_cores/pallas_call | solution.py:364
  81.7 5.7 %all-to-all-done.3 = bf16[8,16,640]{2,1,0:T(8,128)(2,1)S(1)} async-done(((bf16[8,16,640]{2,1,0:T(8,128)(2,1)}), bf16[8,16,640]{2,1,0:T(8,128)(2,1)S(1)}, u32[]{:S(2)}, u32[]{:S(2)}) %all-to-all-start.3) | async-done | bytes 163872 | tf_op jit(solution)/shard_map/all_to_all | solution.py:317
  87.4 4.6 %all-to-all-start.1 = ((bf16[64,8,640]{2,1,0:T(8,128)(2,1)}), bf16[64,8,640]{2,1,0:T(8,128)(2,1)S(1)}, u32[]{:S(2)}, u32[]{:S(2)}) async-start(bf16[64,8,640]{2,1,0:T(8,128)(2,1)} %bitcast.4), calls=%async_computation.1 | async-start | bytes 1310720 | tf_op jit(solution)/shard_map/all_to_all | solution.py:317
  92.0 0.0 copy-done.5
  92.1 1.2 %own_keys.1 = (f32[80,512]{1,0:T(8,128)S(1)}, f32[80,128]{1,0:T(8,128)S(1)}) custom-call(s32[1,8]{1,0:T(1,128)S(1)} %copy-done.7, s32[10,2]{1,0:T(8,128)S(1)} %copy.12.pos_ref, bf16[10,2,576]{2,1,0:T(2,128)(2,1)S(1)} %copy-done.5, f32[1,64]{1,0:T(1,128)S(1)} %copy-done.9, bf16[80,640]{1,0:T(8,128)(2,1)S(1)} %get-tuple-element.24.own_ref), custom_call_target="tpu_custom_call" | custom-call | tf_op jit(solution)/shard_map/own_keys/pallas_call | solution.py:306
  93.2 13.3 %all-to-all-done.1 = bf16[64,8,640]{2,1,0:T(8,128)(2,1)S(1)} async-done(((bf16[64,8,640]{2,1,0:T(8,128)(2,1)}), bf16[64,8,640]{2,1,0:T(8,128)(2,1)S(1)}, u32[]{:S(2)}, u32[]{:S(2)}) %all-to-all-start.1) | async-done | bytes 655392 | tf_op jit(solution)/shard_map/all_to_all | solution.py:317
  106.6 1.9 %finish.1 = bf16[10,2,512]{2,1,0:T(2,128)(2,1)} custom-call(s32[1,8]{1,0:T(1,128)S(1)} %copy-done.7, bf16[512,640]{1,0:T(8,128)(2,1)S(1)} %bitcast.13, bf16[128,640]{1,0:T(8,128)(2,1)S(1)} %bitcast.17, f32[80,512]{1,0:T(8,128)S(1)} %get-tuple-element.25.own_ref, f32[80,128]{1,0:T(8,128)S(1)} %get-tuple-element.26.stat_ref, bf16[4,512,128]{2,1,0:T(8,128)(2,1)S(1)} %copy-done.2), custom_call_target="tpu_custom_call" | custom-call | tf_op jit(solution)/shard_map/finish/pallas_call | solution.py:376
  (14 shorter events, 0.0 us)
Async XLA Ops:
  0.8 1.7 %copy-start.1 = (bf16[1536,768]{1,0:T(8,128)(2,1)S(1)}, bf16[1536,768]{1,0:T(8,128)(2,1)}, u32[]{:S(2)}) copy-start(bf16[1536,768]{1,0:T(8,128)(2,1)} %wq_ref.1) | copy-start | bytes 7077892
  2.4 1.0 copy-start.3
  3.5 0.8 copy-start.4
  4.3 0.7 copy-start.6
  5.0 0.7 copy-start.8
  5.6 0.7 copy-start.10
  33.8 10.1 %collective-permute-start = (bf16[512,640]{1,0:T(8,128)(2,1)S(1)}, bf16[512,640]{1,0:T(8,128)(2,1)S(1)}, u32[]{:S(2)}, u32[]{:S(2)}) collective-permute-start(bf16[512,640]{1,0:T(8,128)(2,1)S(1)} %bitcast.11), channel_id=1, source_target_pairs={{0,1},{1,0},{2,3},{3,2},{4,5},{5,4},{6,7},{7,6},{8,9},{9,8},{10,11... | collective-permute-start | bytes 1966088 | tf_op jit(solution)/shard_map/ppermute | solution.py:320
  43.9 3.2 %copy-start = (bf16[1,8,768,576]{3,2,1,0:T(8,128)(2,1)S(1)}, bf16[1,8,768,576]{3,2,1,0:T(8,128)(2,1)}, u32[]{:S(2)}) copy-start(bf16[1,8,768,576]{3,2,1,0:T(8,128)(2,1)} %copy.13) | copy-start | bytes 21233668
  55.5 23.3 %collective-permute-start.1 = (bf16[512,640]{1,0:T(8,128)(2,1)}, bf16[512,640]{1,0:T(8,128)(2,1)}, u32[]{:S(2)}, u32[]{:S(2)}) collective-permute-start(bf16[512,640]{1,0:T(8,128)(2,1)} %get-tuple-element.17), channel_id=1, source_target_pairs={{0,1},{1,0},{2,3},{3,2},{4,5},{5,4},{6,7},{7,6},{8,9},{9,8},{10,11... | collective-permute-start | bytes 1966088 | tf_op jit(solution)/shard_map/ppermute | solution.py:320
  67.3 2.8 %collective-permute-start.2 = (bf16[128,640]{1,0:T(8,128)(2,1)S(1)}, bf16[128,640]{1,0:T(8,128)(2,1)}, u32[]{:S(2)}, u32[]{:S(2)}) collective-permute-start(bf16[128,640]{1,0:T(8,128)(2,1)S(1)} %bitcast.14), channel_id=1, source_target_pairs={{0,1},{1,0},{2,3},{3,2},{4,5},{5,4},{6,7},{7,6},{8,9},{9,8},{10,11... | collective-permute-start | bytes 491528 | tf_op jit(solution)/shard_map/ppermute | solution.py:320
  72.6 1.6 %collective-permute-start.3 = (bf16[128,640]{1,0:T(8,128)(2,1)S(1)}, bf16[128,640]{1,0:T(8,128)(2,1)S(1)}, u32[]{:S(2)}, u32[]{:S(2)}) collective-permute-start(bf16[128,640]{1,0:T(8,128)(2,1)S(1)} %get-tuple-element.21), channel_id=1, source_target_pairs={{0,1},{1,0},{2,3},{3,2},{4,5},{5,4},{6,7},{7,6},{8,9},{9,8},{10,11... | collective-permute-start | bytes 491528 | tf_op jit(solution)/shard_map/ppermute | solution.py:320
  74.2 17.8 %copy-start.5 = (bf16[10,2,576]{2,1,0:T(2,128)(2,1)S(1)}, bf16[10,2,576]{2,1,0:T(2,128)(2,1)}, u32[]{:S(2)}) copy-start(bf16[10,2,576]{2,1,0:T(2,128)(2,1)} %nl_ref.1) | copy-start | bytes 69124
  74.2 17.8 %copy-start.7 = (s32[1,8]{1,0:T(1,128)S(1)}, s32[1,8]{1,0:T(1,128)}, u32[]{:S(2)}) copy-start(s32[1,8]{1,0:T(1,128)} %slot_ref.5) | copy-start | bytes 100
  74.2 17.8 %copy-start.9 = (f32[1,64]{1,0:T(1,128)S(1)}, f32[1,64]{1,0:T(1,128)}, u32[]{:S(2)}) copy-start(f32[1,64]{1,0:T(1,128)} %constant.14.clone.freq_ref) | copy-start | bytes 772
  75.3 31.2 %copy-start.2 = (bf16[4,512,128]{2,1,0:T(8,128)(2,1)S(1)}, bf16[4,512,128]{2,1,0:T(8,128)(2,1)}, u32[]{:S(2)}) copy-start(bf16[4,512,128]{2,1,0:T(8,128)(2,1)} %wv_ref.1) | copy-start | bytes 1572868
  75.3 12.1 %all-to-all-start.3 = ((bf16[8,16,640]{2,1,0:T(8,128)(2,1)}), bf16[8,16,640]{2,1,0:T(8,128)(2,1)S(1)}, u32[]{:S(2)}, u32[]{:S(2)}) async-start(bf16[8,16,640]{2,1,0:T(8,128)(2,1)} %bitcast.8), calls=%async_computation.3 | async-start | bytes 327680 | tf_op jit(solution)/shard_map/all_to_all | solution.py:317
  87.4 19.2 %all-to-all-start.1 = ((bf16[64,8,640]{2,1,0:T(8,128)(2,1)}), bf16[64,8,640]{2,1,0:T(8,128)(2,1)S(1)}, u32[]{:S(2)}, u32[]{:S(2)}) async-start(bf16[64,8,640]{2,1,0:T(8,128)(2,1)} %bitcast.4), calls=%async_computation.1 | async-start | bytes 1310720 | tf_op jit(solution)/shard_map/all_to_all | solution.py:317

commit v2 on v1

v2 whole, which is shorter than its diff:
```python
import functools
import math

import jax
import jax.numpy as jnp
import numpy as np
from jax import lax
from jax.experimental import pallas as pl
from jax.experimental.pallas import tpu as pltpu
from jax.sharding import Mesh
from jax.sharding import PartitionSpec as P

LAT = 512
ROPE = 64
NOPE = 128
HEAD = NOPE + ROPE
WIDE = 640
SCALE = HEAD ** (-0.5)
NONE = -1e30
BF = jnp.bfloat16
F32 = jnp.float32

HALF_PI = (1.5703125, 0.0004825592041015625, 1.2676710047e-06)


def dot(a, b, contract=((1,), (0,))):
    return lax.dot_general(a, b, (contract, ((), ())), preferred_element_type=F32)


def iota(shape, dim):
    return lax.broadcasted_iota(jnp.int32, shape, dim)


def cos_sin(angle):
    turns = jnp.floor(angle * (2.0 / math.pi) + 0.5)
    rest = angle - turns * HALF_PI[0]
    rest = rest - turns * HALF_PI[1]
    rest = rest - turns * HALF_PI[2]
    sq = rest * rest
    sine = rest + rest * sq * (
        -1.6666654611e-1 + sq * (8.3321608736e-3 + sq * -1.9515295891e-4)
    )
    cosine = 1.0 - 0.5 * sq + sq * sq * (
        4.166664568298827e-2 + sq * (-1.388731625493765e-3 + sq * 2.443315711809948e-5)
    )
    quarter = turns.astype(jnp.int32) & 3
    swapped = (quarter & 1) == 1
    first = jnp.where(swapped, sine, cosine)
    second = jnp.where(swapped, cosine, sine)
    first = jnp.where((quarter == 1) | (quarter == 2), -first, first)
    second = jnp.where(quarter >= 2, -second, second)
    return first, second


def rope(values, cosine, signed_sine):
    half = ROPE // 2
    swapped = jnp.concatenate([values[:, half:], values[:, :half]], 1)
    return values * cosine + swapped * signed_sine


def per_row(get, rows, width):
    at = iota((32, 1), 0)
    out = jnp.zeros((32, 1), jnp.int32)
    for r in range(rows):
        for s in range(width):
            out = jnp.where(at // (2 // width) == r * width + s, get(r, s), out)
    return out


def angles_of(pos_ref, freq_ref, rows):
    at = per_row(lambda r, s: pos_ref[s, r], rows, 2).astype(F32)
    cosine, sine = cos_sin(at * freq_ref[...])
    signed = jnp.where(iota((1, ROPE), 1) < ROPE // 2, -1.0, 1.0) * sine
    return cosine, signed


def row_of(slot_ref, slots, resident, shape, dim, per):
    at = iota(shape, dim)
    slot = at // per
    out = slot - slots
    for j in range(slots):
        out = jnp.where(slot == slot_ref[0, j], resident + j, out)
    return out


def project_kernel(heads, slots, copies, slot_ref, len_ref, pos_ref, ql_ref, wq_hbm, wk_hbm, freq_ref,
                   out_ref, res_ref, own_ref, rows_ref, all_ref, wq_ref, wk_ref, sems):
    rows = ql_ref.shape[0]
    resident = rows - slots
    chunks = wq_ref.shape[0]
    step = wq_ref.shape[1]
    loads = [
        pltpu.make_async_copy(wq_hbm.at[pl.ds(c * step, step)], wq_ref.at[c], sems.at[c]) for c in range(chunks)
    ]
    loads.append(pltpu.make_async_copy(wk_hbm, wk_ref, sems.at[chunks]))
    for load in loads:
        load.start()
    rows_ref[...] = jnp.zeros_like(rows_ref)
    for r in range(rows):
        rows_ref[2 * r : 2 * r + 2, :] = ql_ref[r].astype(F32)
    cosine, signed = angles_of(pos_ref, freq_ref, rows)
    length = per_row(lambda r, s: len_ref[r], rows, 1)
    lane = iota((1, WIDE - LAT - ROPE), 1)
    meta = jnp.where(lane == 0, (length // 128).astype(F32), jnp.where(lane == 1, (length % 128).astype(F32), 0.0))
    piece = 2 * heads
    count = rows * piece
    row = row_of(slot_ref, slots, resident, (count, 1), 0, piece)
    inner = iota((count, 1), 0) % piece
    source = (inner // 2) * 32 + 2 * row + inner % 2
    select = jnp.where(iota((count, heads * 32), 1) == source, 1.0, 0.0).astype(BF)
    qfull = 0.0
    for c in range(chunks):
        loads[c].wait()
        qfull = qfull + dot(rows_ref[:, c * step : (c + 1) * step].astype(BF), wq_ref[c])
    qfull = qfull.astype(BF)
    loads[chunks].wait()
    for h in range(heads):
        part = qfull[:, h * HEAD : (h + 1) * HEAD]
        all_ref[h * 32 : (h + 1) * 32, :LAT] = dot(part[:, :NOPE], wk_ref[h]).astype(BF)
        tail = jnp.concatenate([rope(part[:, NOPE:].astype(F32), cosine, signed), meta], 1)
        all_ref[h * 32 : (h + 1) * 32, LAT:] = tail.astype(BF)
    own = dot(select, all_ref[...])
    own_ref[...] = own.astype(BF)
    for p in range(slots):
        one = own[p * piece : (p + 1) * piece]
        two = jnp.concatenate([one, one], 0).astype(BF)
        for k in range(0, copies, 2):
            at = (p * copies + k) * piece
            out_ref[at : at + 2 * piece, :] = two
    res_ref[...] = own[slots * piece :].astype(BF)


def own_keys_kernel(slots, slot_ref, pos_ref, nl_ref, freq_ref, own_ref, out_ref, stat_ref, keys_ref):
    rows = nl_ref.shape[0]
    resident = rows - slots
    count = own_ref.shape[0]
    piece = count // rows
    keys_ref[...] = jnp.zeros_like(keys_ref)
    for r in range(rows):
        keys_ref[2 * r : 2 * r + 2, :] = nl_ref[r].astype(F32)
    cosine, signed = angles_of(pos_ref, freq_ref, rows)
    latent = keys_ref[:, :LAT].astype(BF)
    turned = rope(keys_ref[:, LAT:], cosine, signed).astype(BF)
    scores = dot(own_ref[:, :LAT], latent, ((1,), (1,)))
    scores = scores + dot(own_ref[:, LAT : LAT + ROPE], turned, ((1,), (1,)))
    scores = scores * SCALE
    row = row_of(slot_ref, slots, resident, (count, 1), 0, piece)
    step = iota((count, 1), 0) % 2
    key = iota((1, 32), 1)
    allowed = (key // 2 == row) & (key % 2 <= step)
    highest = jnp.max(jnp.where(allowed, scores, NONE), 1, keepdims=True)
    weights = jnp.where(allowed, jnp.exp(scores - highest), 0.0)
    total = jnp.sum(weights, 1, keepdims=True)
    out_ref[...] = dot(weights.astype(BF), latent)
    stat_ref[:, :128] = jnp.broadcast_to(highest, (count, 128))
    stat_ref[:, 128:] = jnp.broadcast_to(total, (count, 128))


def parts_of(value):
    first = value.astype(BF).astype(F32)
    second = (value - first).astype(BF).astype(F32)
    return first, second, value - first - second


def with_stats(highest, total):
    lane = iota((1, 128), 1)
    out = 0.0
    for at, part in enumerate(parts_of(highest) + parts_of(total)):
        out = jnp.where(lane == at, part, out)
    return out.astype(BF)


def stats_of(tail):
    at = iota((128, 256), 0)
    pick = jnp.where((at < 6) & (at // 3 == iota((128, 256), 1) // 128), 1.0, 0.0).astype(BF)
    both = dot(tail, pick)
    return both[:, :128], both[:, 128:]


def spread(value):
    return jnp.concatenate([value] * (LAT // 128), -1)


def softmax_part(scores, length):
    scores = jnp.where(iota((1, scores.shape[1]), 1) < length, scores, NONE)
    highest = jnp.max(scores, 1, keepdims=True)
    weights = jnp.exp((scores - jnp.maximum(highest, 0.1 * NONE)) * SCALE)
    return highest * SCALE, jnp.sum(weights, 1, keepdims=True), weights.astype(BF)


def attend_kernel(piece, offset_ref, fresh_hbm, cache_hbm, new_own, new_other, *refs):
    send_ref, keep_ref, stat_ref, keys_ref, sems = refs[-5:]
    blocks = refs[:-5]
    res_other, res_own = blocks[: len(blocks) // 2], blocks[len(blocks) // 2 :]
    slots, resident = fresh_hbm.shape[0], cache_hbm.shape[0]
    rows = slots + resident
    half = new_own.shape[0] // slots
    loads = [pltpu.make_async_copy(fresh_hbm.at[i], keys_ref.at[i], sems.at[i]) for i in range(slots)]
    loads += [
        pltpu.make_async_copy(cache_hbm.at[i], keys_ref.at[slots + i], sems.at[slots + i]) for i in range(resident)
    ]
    for load in loads:
        load.start()
    arrived = 0

    def queries_of(i):
        if i < slots:
            span = slice(i * half, (i + 1) * half)
            return jnp.concatenate([new_other[span, :], new_own[span, :]], 0)
        at = (i - slots) * piece
        step = resident * piece
        return jnp.concatenate(
            [ref[k + at : k + at + piece, :] for ref in res_other + res_own for k in range(0, ref.shape[0], step)], 0
        )

    def scores_of(i):
        queries = queries_of(i)
        length = queries[:, LAT + ROPE : LAT + ROPE + 2].astype(F32)
        length = (length[:, 0:1] * 128.0 + length[:, 1:2]).astype(jnp.int32) - offset_ref[0]
        return dot(queries[:, : LAT + ROPE], keys_ref[i]), length

    loads[0].wait()
    arrived = 1
    ahead = scores_of(0)
    for i in range(rows):
        scores, length = ahead
        if i + 1 < rows:
            if i + 1 == arrived:
                upto = min(rows, arrived + i + 2)
                for load in loads[arrived:upto]:
                    load.wait()
                arrived = upto
            ahead = scores_of(i + 1)
        highest, total, weights = softmax_part(scores, length)
        mean = dot(weights, keys_ref[i, :LAT, :], ((1,), (1,))) * (1.0 / jnp.maximum(total, 1e-30))
        stats = with_stats(highest, total)
        span = slice(i * half, (i + 1) * half)
        send_ref[span, :LAT] = mean[:half].astype(BF)
        send_ref[span, LAT:] = stats[:half]
        keep_ref[span, :] = mean[half:]
        stat_ref[span, :] = stats[half:]


def joined(got, keep, stat):
    far_highest, far_total = stats_of(got[:, LAT:])
    highest, total = stats_of(stat)
    top = jnp.maximum(far_highest, highest)
    far_total = far_total * jnp.exp(far_highest - top)
    total = total * jnp.exp(highest - top)
    both = total + far_total
    scale = 1.0 / jnp.maximum(both, 1e-30)
    mean = got[:, :LAT].astype(F32) * spread(far_total * scale) + keep * spread(total * scale)
    return mean.astype(BF), with_stats(top, both)


def join_kernel(slots, piece, got_ref, keep_ref, stat_ref, new_ref, *res_refs):
    mean, stats = joined(got_ref[...], keep_ref[...], stat_ref[...])
    count = new_ref.shape[0]
    half = count // slots
    new_ref[:, :LAT] = mean[:count]
    new_ref[:, LAT:] = stats[:count]
    resident = got_ref.shape[0] // half - slots
    block = 0
    for ref in res_refs:
        for k in range(0, ref.shape[0], resident * piece):
            for i in range(resident):
                at = count + i * half + block * piece
                span = slice(k + i * piece, k + (i + 1) * piece)
                ref[span, :LAT] = mean[at : at + piece]
                ref[span, LAT:] = stats[at : at + piece]
            block += 1


def merged(means, tails, own, own_highest, own_total):
    copies, n = means.shape[:2]
    highest, total = (x.reshape(copies, n, 128) for x in stats_of(tails.reshape(copies * n, 128)))
    top = jnp.maximum(jnp.max(highest, 0), own_highest)
    share = total * jnp.exp(highest - top[None])
    own_fade = jnp.exp(own_highest - top)
    scale = 1.0 / (jnp.sum(share, 0) + own_total * own_fade)
    summed = own * spread(own_fade * scale)
    share = share * scale[None]
    for k in range(copies):
        summed = summed + means[k].astype(F32) * spread(share[k])
    return summed.astype(BF)


def finish_kernel(slots, slot_ref, new_ref, own_ref, stat_ref, wv_ref, *refs):
    out_ref = refs[-1]
    heads = wv_ref.shape[0]
    piece = 2 * heads
    rows = out_ref.shape[0]
    resident = rows - slots
    n = resident * piece
    copies = new_ref.shape[0] // slots // piece
    mine = copies // 2 + 1
    parts = [ref[:n, :] for ref in refs[:mine]] + [ref[n:, :] for ref in refs[mine:-1]]

    def own_of(at, n):
        return own_ref[at : at + n, :], stat_ref[at : at + n, :128], stat_ref[at : at + n, 128:]

    half = copies * piece
    latent = []
    for p in range(slots):
        block = new_ref[p * half : (p + 1) * half, :].reshape(copies, piece, WIDE)
        latent.append(merged(block[..., :LAT], block[..., LAT:], *own_of(p * piece, piece)))
    block = jnp.stack(parts)
    latent.append(merged(block[..., :LAT], block[..., LAT:], *own_of(slots * piece, resident * piece)))
    latent = jnp.concatenate(latent, 0)
    count = rows * piece
    inner = iota((count, 1), 0) % piece
    values = []
    for h in range(heads):
        one = dot(latent, wv_ref[h])
        values.append(jnp.where(inner // 2 == h, one, 0.0).astype(BF))
    values = jnp.concatenate(values, 1)
    row = row_of(slot_ref, slots, resident, (1, count), 1, piece)
    target = 2 * row + iota((1, count), 1) % 2
    select = jnp.where(iota((32, count), 0) == target, 1.0, 0.0).astype(BF)
    out = dot(select, values)
    for r in range(rows):
        out_ref[r] = out[2 * r : 2 * r + 2].astype(BF)


VMEM = pl.BlockSpec(memory_space=pltpu.VMEM)
SMEM = pl.BlockSpec(memory_space=pltpu.SMEM)
ANY = pl.BlockSpec(memory_space=pl.ANY)


def shape(dims, dtype):
    return jax.ShapeDtypeStruct(dims, dtype)


def params(mebibytes):
    return pltpu.CompilerParams(vmem_limit_bytes=mebibytes * 1024 * 1024)


def cost(flops, moved):
    return pl.CostEstimate(flops=flops, bytes_accessed=moved, transcendentals=0)


def local(query_latent, w_query, w_key_up, w_value_up, cache, fresh, new_latent, lengths, fresh_slot, positions):
    rows, _, depth = query_latent.shape
    heads = w_key_up.shape[0]
    slots = fresh_slot.shape[1]
    resident = rows - slots
    tokens = cache.shape[1]
    copies = lax.axis_size("zx")
    piece = 2 * heads
    half = copies * piece
    chunks = 4
    freqs = 50000.0 ** (-np.arange(ROPE // 2, dtype=np.float64) / (ROPE // 2))
    freqs = jnp.asarray(np.concatenate([freqs, freqs]).astype(np.float32)[None])
    place = lax.axis_index("zx")
    offset = ((place * lax.axis_size("core") + lax.axis_index("core")) * tokens).reshape(1)
    positions = positions.T
    cache = jnp.swapaxes(cache, 1, 2)
    fresh = jnp.swapaxes(fresh[0], 1, 2)

    def in_hbm(x):
        return pltpu.with_memory_space_constraint(x, pltpu.HBM)

    out_q, res_q, own_q = pl.pallas_call(
        functools.partial(project_kernel, heads, slots, copies),
        out_shape=(
            shape((slots * half, WIDE), BF),
            shape((resident * piece, WIDE), BF),
            shape((rows * piece, WIDE), BF),
        ),
        in_specs=[SMEM] * 3 + [VMEM, ANY, ANY, VMEM],
        out_specs=[VMEM] * 3,
        scratch_shapes=[
            pltpu.VMEM((32, depth), F32),
            pltpu.VMEM((heads * 32, WIDE), BF),
            pltpu.VMEM((chunks, depth // chunks, heads * HEAD), BF),
            pltpu.VMEM((heads, NOPE, LAT), BF),
            pltpu.SemaphoreType.DMA((chunks + 1,)),
        ],
        compiler_params=params(16),
        name="project",
    )(*map(in_hbm, (fresh_slot, lengths, positions, query_latent, w_query, w_key_up, freqs)))

    own_out, own_stat = pl.pallas_call(
        functools.partial(own_keys_kernel, slots),
        out_shape=(shape((rows * piece, LAT), F32), shape((rows * piece, 256), F32)),
        in_specs=[SMEM] * 2 + [VMEM] * 3,
        out_specs=[VMEM] * 2,
        scratch_shapes=[pltpu.VMEM((32, LAT + ROPE), F32)],
        compiler_params=params(32),
        name="own_keys",
    )(fresh_slot, positions, new_latent, freqs, own_q)

    def exchange(x, axes, n):
        return lax.all_to_all(x.reshape(n, -1, WIDE), axes, 0, 0, tiled=True).reshape(-1, WIDE)

    def swap(x):
        return lax.ppermute(x, "core", [(0, 1), (1, 0)])

    def turned(x, k, sign):
        pairs = []
        for i in range(copies):
            pairs += [(2 * i, 2 * ((i + sign * k) % copies)), (2 * i + 1, 2 * ((i - sign * k) % copies) + 1)]
        return lax.ppermute(x, ("zx", "core"), pairs)

    new_own = exchange(out_q, ("group", "zx"), slots * copies)
    res_sib = swap(res_q)
    res_both = jnp.concatenate([res_q, res_sib], 0)
    near = [turned(res_both, k, 1) for k in range(1, copies // 2)]
    across = turned(res_q, copies // 2, 1)
    new_own, across, *near = lax.optimization_barrier((new_own, across, *near))
    new_other, across_sib, *far = map(swap, (new_own, across, *near))

    send, keep, stat = pl.pallas_call(
        functools.partial(attend_kernel, piece),
        out_shape=(shape((rows * half, WIDE), BF), shape((rows * half, LAT), F32), shape((rows * half, 128), BF)),
        in_specs=[SMEM] + [ANY] * 2 + [VMEM] * (4 + copies),
        out_specs=[VMEM] * 3,
        scratch_shapes=[pltpu.VMEM((rows, LAT + ROPE, tokens), BF), pltpu.SemaphoreType.DMA((rows,))],
        compiler_params=params(24),
        cost_estimate=cost(rows * 5 * 10**8, rows * 2 * 10**6),
        name="attend",
    )(offset, in_hbm(fresh), in_hbm(cache), new_own, new_other, *far, res_sib, across_sib, *near, res_q, across)

    new_part, *res_parts = pl.pallas_call(
        functools.partial(join_kernel, slots, piece),
        out_shape=(shape((slots * half, WIDE), BF),)
        + (shape((2 * resident * piece, WIDE), BF),) * len(near)
        + (shape((resident * piece, WIDE), BF),) * 2,
        in_specs=[VMEM] * 3,
        out_specs=(VMEM,) * (len(near) + 3),
        compiler_params=params(32),
        name="join_cores",
    )(swap(send), keep, stat)
    new_back = exchange(new_part, ("group", "zx"), slots * copies)
    *near, res_here, across = res_parts
    near = [turned(x, k + 1, -1) for k, x in enumerate(near)]
    across = turned(across, copies // 2, -1)
    res_back = [res_here, across, *near, *map(swap, near)]

    return pl.pallas_call(
        functools.partial(finish_kernel, slots),
        out_shape=shape((rows, 2, heads * 128), BF),
        in_specs=[SMEM] + [VMEM] * (4 + len(res_back)),
        out_specs=VMEM,
        compiler_params=params(32),
        name="finish",
    )(fresh_slot, new_back, own_out, own_stat, w_value_up, *res_back)


def solution(mesh):
    groups, shards = mesh.devices.shape
    split = Mesh(mesh.devices.reshape(groups, shards // 2, 2), ("group", "zx", "core"))
    ctx = ("zx", "core")
    placed = (
        P("group", None, None),
        P(None, ctx),
        P(ctx, None, None),
        P(ctx, None, None),
        P("group", ctx, None),
        P("group", None, ctx, None),
        P("group", None, None),
        P("group"),
        P("group", None),
        P("group", None),
    )
    return jax.shard_map(
        local, mesh=split, in_specs=placed, out_specs=P("group", None, ctx), check_vma=False
    )
```

time: 109 us -> 71.6 us (0.66)
  blocking collectives: 37.1 us -> 0 us
  starting transfers between devices: 9.26 us -> 39 us
  local copies, waits for them, and re-layouts: 22.3 us -> 0.04 us
  Pallas kernels: 19.5 us -> 14.7 us
  waiting for transfers between devices: 20.1 us -> 17.4 us
    all_to_all x2 -> x0, blocking collectives: 37.1 us -> none  [exchange(): lax.all_to_all(x.reshape(n, -1, WIDE), axes, 0, 0, tiled=True)]
    unnamed x25 -> x11, local copies, waits for them, and re-layouts: 22.3 us -> 0.04 us
    all_to_all x2, waiting for transfers between devices: 19 us -> 0.25 us  [exchange(): lax.all_to_all(x.reshape(n, -1, WIDE), axes, 0, 0, tiled=True)]
    ppermute x0 -> x8, starting transfers between devices: none -> 17.8 us  [turned(): return lax.ppermute(x, ('zx', 'core'), pairs)]
    ppermute x0 -> x8, waiting for transfers between devices: none -> 12.5 us  [turned(): return lax.ppermute(x, ('zx', 'core'), pairs)]
    all_to_all x2, starting transfers between devices: 8.15 us -> 18.9 us  [exchange(): lax.all_to_all(x.reshape(n, -1, WIDE), axes, 0, 0, tiled=True)]
    pallas_call x4 -> x2, Pallas kernels: 14.9 us -> 7.8 us  [the longest x1 6.36 us: local(): pl.pallas_call(functools.partial(attend_kernel, piece), out_shape=(shape(...]
    ppermute x4 -> x10, waiting for transfers between devices: 1.04 us -> 4.65 us  [swap(): return lax.ppermute(x, 'core', [(0, 1), (1, 0)])]
  transfers between devices with their start and end apart: 6 -> 20, of which waited for: 3 -> 8; matrix products, arithmetic and copies ran while one was open for 12% -> 0% of each run, Pallas kernels for 7% -> 1%
where the time goes in v2:
time: 71.6 us; the launch traced here: 71.3 us
  starting transfers between devices  39 us (54%)
  waiting for transfers between devices  17.4 us (24%)
  Pallas kernels  14.7 us (21%)
    all_to_all x2, starting transfers between devices, exchange(): lax.all_to_all(x.reshape(n, -1, WIDE), axes, 0, 0, tiled=True)  18.9 us
    ppermute x8, starting transfers between devices, turned(): return lax.ppermute(x, ('zx', 'core'), pairs)  17.8 us
    ppermute x8, waiting for transfers between devices, turned(): return lax.ppermute(x, ('zx', 'core'), pairs)  12.5 us
    pallas_call x1, Pallas kernels, local(): pl.pallas_call(functools.partial(attend_kernel, piece), out_shape=(shape(...  6.36 us
    ppermute x10, waiting for transfers between devices, swap(): return lax.ppermute(x, 'core', [(0, 1), (1, 0)])  4.65 us
    pallas_call x1, Pallas kernels, local(): pl.pallas_call(functools.partial(project_kernel, heads, slots, copies), o...  4 us
    ppermute x10, starting transfers between devices, swap(): return lax.ppermute(x, 'core', [(0, 1), (1, 0)])  2.33 us
    pallas_call x1, Pallas kernels, local(): pl.pallas_call(functools.partial(finish_kernel, slots), out_shape=shape((...  1.86 us
  transfers between devices with their start and end apart: 20, of which 8 were waited for; matrix products, arithmetic and copies ran while one was open for 0% of the time, Pallas kernels for 1%

profile of v2, /device:TPU:0, one launch (start us, length us, event | category | flops | bytes accessed | tf_op | source)
XLA Modules:
  0.0 71.3 jit_solution(6351631396157186027)
XLA Ops:
  0.0 4.0 %project.1 = (bf16[512,640]{1,0:T(8,128)(2,1)}, bf16[16,640]{1,0:T(8,128)(2,1)S(1)}, bf16[80,640]{1,0:T(8,128)(2,1)S(1)}) custom-call(s32[1,8]{1,0:T(1,128)} %slot_ref.5, s32[10]{0:T(128)} %len_ref.1, s32[2,10]{1,0:T(2,128)} %bitcast.13, bf16[10,2,1536]{2,1,0:T(2,128)(2,1)} %ql_ref.1, bf16[1536,768]{1,0:T(8,128)(2,1)} %wq_hbm.1, ...), custom_call_target="tpu_custom_call" | custom-call | tf_op jit(solution)/shard_map/project/pallas_call | solution.py:363
  4.0 11.5 %all-to-all-start = ((bf16[64,8,640]{2,1,0:T(8,128)(2,1)}), bf16[64,8,640]{2,1,0:T(8,128)(2,1)S(1)}, u32[]{:S(2)}, u32[]{:S(2)}) async-start(bf16[64,8,640]{2,1,0:T(8,128)(2,1)} %bitcast.5), calls=%async_computation | async-start | bytes 1310720 | tf_op jit(solution)/shard_map/all_to_all | solution.py:394
  15.5 0.1 collective-permute-start.1
  15.6 1.2 %collective-permute-done.1.refs_3_ = bf16[16,640]{1,0:T(8,128)(2,1)S(1)} collective-permute-done((bf16[16,640]{1,0:T(8,128)(2,1)S(1)}, bf16[16,640]{1,0:T(8,128)(2,1)S(1)}, u32[]{:S(2)}, u32[]{:S(2)}) %collective-permute-start.1) | collective-permute-done | bytes 20512 | tf_op jit(solution)/shard_map/ppermute | solution.py:397
  16.8 3.1 %collective-permute-start.2 = (bf16[32,640]{1,0:T(8,128)(2,1)S(1)}, bf16[32,640]{1,0:T(8,128)(2,1)S(1)}, u32[]{:S(2)}, u32[]{:S(2)}) collective-permute-start(bf16[32,640]{1,0:T(8,128)(2,1)S(1)} %constant_dynamic-update-slice_fusion), channel_id=1, source_target_pairs={{0,2},{1,15},{2,4},{3,1},{4,6},{5,3},{6,8},{7,5},{8,10},{9,7},{10,... | collective-permute-start | bytes 122888 | tf_op jit(solution)/shard_map/ppermute | solution.py:403
  19.9 1.5 %collective-permute-start.3 = (bf16[32,640]{1,0:T(8,128)(2,1)S(1)}, bf16[32,640]{1,0:T(8,128)(2,1)S(1)}, u32[]{:S(2)}, u32[]{:S(2)}) collective-permute-start(bf16[32,640]{1,0:T(8,128)(2,1)S(1)} %constant_dynamic-update-slice_fusion), channel_id=1, source_target_pairs={{0,4},{1,13},{2,6},{3,15},{4,8},{5,1},{6,10},{7,3},{8,12},{9,5},{1... | collective-permute-start | bytes 122888 | tf_op jit(solution)/shard_map/ppermute | solution.py:403
  21.3 2.1 %collective-permute-start.4 = (bf16[32,640]{1,0:T(8,128)(2,1)S(1)}, bf16[32,640]{1,0:T(8,128)(2,1)S(1)}, u32[]{:S(2)}, u32[]{:S(2)}) collective-permute-start(bf16[32,640]{1,0:T(8,128)(2,1)S(1)} %constant_dynamic-update-slice_fusion), channel_id=1, source_target_pairs={{0,6},{1,11},{2,8},{3,13},{4,10},{5,15},{6,12},{7,1},{8,14},{9,3},... | collective-permute-start | bytes 122888 | tf_op jit(solution)/shard_map/ppermute | solution.py:403
  23.4 2.1 %collective-permute-start = (bf16[16,640]{1,0:T(8,128)(2,1)S(1)}, bf16[16,640]{1,0:T(8,128)(2,1)S(1)}, u32[]{:S(2)}, u32[]{:S(2)}) collective-permute-start(bf16[16,640]{1,0:T(8,128)(2,1)S(1)} %get-tuple-element.25.refs_8_), channel_id=1, source_target_pairs={{0,8},{1,9},{2,10},{3,11},{4,12},{5,13},{6,14},{7,15},{8,0},{9,1},... | collective-permute-start | bytes 61448 | tf_op jit(solution)/shard_map/ppermute | solution.py:403
  25.5 4.8 %collective-permute-done.refs_9_ = bf16[16,640]{1,0:T(8,128)(2,1)S(1)} collective-permute-done((bf16[16,640]{1,0:T(8,128)(2,1)S(1)}, bf16[16,640]{1,0:T(8,128)(2,1)S(1)}, u32[]{:S(2)}, u32[]{:S(2)}) %collective-permute-start) | collective-permute-done | bytes 20512 | tf_op jit(solution)/shard_map/ppermute | solution.py:403
  30.3 0.2 all-to-all-done
  30.6 0.5 collective-permute-start.6
  31.1 0.5 collective-permute-start.8
  31.6 1.3 %collective-permute-done.9.refs_4_ = bf16[16,640]{1,0:T(8,128)(2,1)S(1)} collective-permute-done((bf16[16,640]{1,0:T(8,128)(2,1)S(1)}, bf16[16,640]{1,0:T(8,128)(2,1)S(1)}, u32[]{:S(2)}, u32[]{:S(2)}) %collective-permute-start.9) | collective-permute-done | bytes 20512 | tf_op jit(solution)/shard_map/ppermute | solution.py:397
  32.9 6.4 %attend.1 = (bf16[640,640]{1,0:T(8,128)(2,1)S(1)}, f32[640,512]{1,0:T(8,128)S(1)}, bf16[640,128]{1,0:T(8,128)(2,1)S(1)}) custom-call(s32[1]{0:T(128)} %bitcast.offset_ref, bf16[8,576,768]{2,1,0:T(8,128)(2,1)} %bitcast.15, bf16[2,576,768]{2,1,0:T(8,128)(2,1)} %bitcast.16, bf16[512,640]{1,0:T(8,128)(2,1)S(1)} %bitcast.12, ...), custom_call_target="tpu_custom_call" | custom-call | flops 5000000000 | bytes 20000000 | tf_op jit(solution)/shard_map/attend/pallas_call | solution.py:413
  39.3 0.0 copy-start.2
  39.3 0.0 copy-start.3
  39.3 0.0 copy-start.4
  39.3 0.2 collective-permute-start.10
  39.5 2.2 %collective-permute-done.10.got_ref = bf16[640,640]{1,0:T(8,128)(2,1)S(1)} collective-permute-done((bf16[640,640]{1,0:T(8,128)(2,1)S(1)}, bf16[640,640]{1,0:T(8,128)(2,1)S(1)}, u32[]{:S(2)}, u32[]{:S(2)}) %collective-permute-start.10) | collective-permute-done | bytes 819232 | tf_op jit(solution)/shard_map/ppermute | solution.py:397
  41.7 1.4 %join_cores.1 = (bf16[512,640]{1,0:T(8,128)(2,1)}, bf16[32,640]{1,0:T(8,128)(2,1)S(1)}, bf16[32,640]{1,0:T(8,128)(2,1)S(1)}, bf16[32,640]{1,0:T(8,128)(2,1)S(1)}...) custom-call(bf16[640,640]{1,0:T(8,128)(2,1)S(1)} %collective-permute-done.10.got_ref, ...), custom_call_target="tpu_custom_call" | custom-call | tf_op jit(solution)/shard_map/join_cores/pallas_call | solution.py:424
  43.2 7.4 %all-to-all-start.1 = ((bf16[64,8,640]{2,1,0:T(8,128)(2,1)}), bf16[64,8,640]{2,1,0:T(8,128)(2,1)S(1)}, u32[]{:S(2)}, u32[]{:S(2)}) async-start(bf16[64,8,640]{2,1,0:T(8,128)(2,1)} %bitcast.7), calls=%async_computation.1 | async-start | bytes 1310720 | tf_op jit(solution)/shard_map/all_to_all | solution.py:394
  50.6 5.3 %collective-permute-start.12 = (bf16[32,640]{1,0:T(8,128)(2,1)S(1)}, bf16[32,640]{1,0:T(8,128)(2,1)S(1)}, u32[]{:S(2)}, u32[]{:S(2)}) collective-permute-start(bf16[32,640]{1,0:T(8,128)(2,1)S(1)} %get-tuple-element.40), channel_id=1, source_target_pairs={{0,14},{1,3},{2,0},{3,5},{4,2},{5,7},{6,4},{7,9},{8,6},{9,11},{10,... | collective-permute-start | bytes 122888 | tf_op jit(solution)/shard_map/ppermute | solution.py:403
  55.8 0.9 %collective-permute-start.13 = (bf16[32,640]{1,0:T(8,128)(2,1)S(1)}, bf16[32,640]{1,0:T(8,128)(2,1)S(1)}, u32[]{:S(2)}, u32[]{:S(2)}) collective-permute-start(bf16[32,640]{1,0:T(8,128)(2,1)S(1)} %get-tuple-element.41), channel_id=1, source_target_pairs={{0,12},{1,5},{2,14},{3,7},{4,0},{5,9},{6,2},{7,11},{8,4},{9,13},{1... | collective-permute-start | bytes 122888 | tf_op jit(solution)/shard_map/ppermute | solution.py:403
  56.7 0.6 collective-permute-start.14
  57.3 5.0 %collective-permute-done.12.refs_2_ = bf16[32,640]{1,0:T(8,128)(2,1)S(1)} collective-permute-done((bf16[32,640]{1,0:T(8,128)(2,1)S(1)}, bf16[32,640]{1,0:T(8,128)(2,1)S(1)}, u32[]{:S(2)}, u32[]{:S(2)}) %collective-permute-start.12) | collective-permute-done | bytes 40992 | tf_op jit(solution)/shard_map/ppermute | solution.py:403
  62.3 0.7 collective-permute-start.15
  62.9 0.8 %collective-permute-done.14.refs_4_ = bf16[32,640]{1,0:T(8,128)(2,1)S(1)} collective-permute-done((bf16[32,640]{1,0:T(8,128)(2,1)S(1)}, bf16[32,640]{1,0:T(8,128)(2,1)S(1)}, u32[]{:S(2)}, u32[]{:S(2)}) %collective-permute-start.14) | collective-permute-done | bytes 40992 | tf_op jit(solution)/shard_map/ppermute | solution.py:403
  63.8 0.3 collective-permute-start.17
  64.1 2.4 %collective-permute-start.11 = (bf16[16,640]{1,0:T(8,128)(2,1)S(1)}, bf16[16,640]{1,0:T(8,128)(2,1)S(1)}, u32[]{:S(2)}, u32[]{:S(2)}) collective-permute-start(bf16[16,640]{1,0:T(8,128)(2,1)S(1)} %get-tuple-element.39), channel_id=1, source_target_pairs={{0,8},{1,9},{2,10},{3,11},{4,12},{5,13},{6,14},{7,15},{8,0},{9,1},... | collective-permute-start | bytes 61448 | tf_op jit(solution)/shard_map/ppermute | solution.py:403
  66.5 1.0 %own_keys.1 = (f32[80,512]{1,0:T(8,128)S(1)}, f32[80,256]{1,0:T(8,128)S(1)}) custom-call(s32[1,8]{1,0:T(1,128)S(1)} %copy-done.2, s32[2,10]{1,0:T(2,128)S(1)} %bitcast.14, bf16[10,2,576]{2,1,0:T(2,128)(2,1)S(1)} %copy-done.1, f32[1,64]{1,0:T(1,128)S(1)} %copy-done.4, bf16[80,640]{1,0:T(8,128)(2,1)S(1)} %get-tuple-element.35.own_ref), custom_call_target="tpu_custom_call" | custom-call | tf_op jit(solution)/shard_map/own_keys/pallas_call | solution.py:383
  67.6 1.8 %collective-permute-done.11.refs_1_ = bf16[16,640]{1,0:T(8,128)(2,1)S(1)} collective-permute-done((bf16[16,640]{1,0:T(8,128)(2,1)S(1)}, bf16[16,640]{1,0:T(8,128)(2,1)S(1)}, u32[]{:S(2)}, u32[]{:S(2)}) %collective-permute-start.11) | collective-permute-done | bytes 20512 | tf_op jit(solution)/shard_map/ppermute | solution.py:403
  69.4 1.9 %finish.1 = bf16[10,2,512]{2,1,0:T(2,128)(2,1)} custom-call(s32[1,8]{1,0:T(1,128)S(1)} %copy-done.2, bf16[512,640]{1,0:T(8,128)(2,1)S(1)} %bitcast.10, f32[80,512]{1,0:T(8,128)S(1)} %get-tuple-element.36.own_ref, f32[80,256]{1,0:T(8,128)S(1)} %get-tuple-element.37.stat_ref, bf16[4,512,128]{2,1,0:T(8,128)(2,1)S(1)} %copy-done, ...), custom_call_target="tpu_custom_call" | custom-call | tf_op jit(solution)/shard_map/finish/pallas_call | solution.py:440
  (25 shorter events, 0.1 us)
Async XLA Ops:
  4.0 26.5 %all-to-all-start = ((bf16[64,8,640]{2,1,0:T(8,128)(2,1)}), bf16[64,8,640]{2,1,0:T(8,128)(2,1)S(1)}, u32[]{:S(2)}, u32[]{:S(2)}) async-start(bf16[64,8,640]{2,1,0:T(8,128)(2,1)} %bitcast.5), calls=%async_computation | async-start | bytes 1310720 | tf_op jit(solution)/shard_map/all_to_all | solution.py:394
  15.5 1.3 %collective-permute-start.1 = (bf16[16,640]{1,0:T(8,128)(2,1)S(1)}, bf16[16,640]{1,0:T(8,128)(2,1)S(1)}, u32[]{:S(2)}, u32[]{:S(2)}) collective-permute-start(bf16[16,640]{1,0:T(8,128)(2,1)S(1)} %get-tuple-element.25.refs_8_), channel_id=1, source_target_pairs={{0,1},{1,0},{2,3},{3,2},{4,5},{5,4},{6,7},{7,6},{8,9},{9,8},{10,11... | collective-permute-start | bytes 61448 | tf_op jit(solution)/shard_map/ppermute | solution.py:397
  16.8 13.5 %collective-permute-start.2 = (bf16[32,640]{1,0:T(8,128)(2,1)S(1)}, bf16[32,640]{1,0:T(8,128)(2,1)S(1)}, u32[]{:S(2)}, u32[]{:S(2)}) collective-permute-start(bf16[32,640]{1,0:T(8,128)(2,1)S(1)} %constant_dynamic-update-slice_fusion), channel_id=1, source_target_pairs={{0,2},{1,15},{2,4},{3,1},{4,6},{5,3},{6,8},{7,5},{8,10},{9,7},{10,... | collective-permute-start | bytes 122888 | tf_op jit(solution)/shard_map/ppermute | solution.py:403
  19.9 10.4 %collective-permute-start.3 = (bf16[32,640]{1,0:T(8,128)(2,1)S(1)}, bf16[32,640]{1,0:T(8,128)(2,1)S(1)}, u32[]{:S(2)}, u32[]{:S(2)}) collective-permute-start(bf16[32,640]{1,0:T(8,128)(2,1)S(1)} %constant_dynamic-update-slice_fusion), channel_id=1, source_target_pairs={{0,4},{1,13},{2,6},{3,15},{4,8},{5,1},{6,10},{7,3},{8,12},{9,5},{1... | collective-permute-start | bytes 122888 | tf_op jit(solution)/shard_map/ppermute | solution.py:403
  21.3 9.0 %collective-permute-start.4 = (bf16[32,640]{1,0:T(8,128)(2,1)S(1)}, bf16[32,640]{1,0:T(8,128)(2,1)S(1)}, u32[]{:S(2)}, u32[]{:S(2)}) collective-permute-start(bf16[32,640]{1,0:T(8,128)(2,1)S(1)} %constant_dynamic-update-slice_fusion), channel_id=1, source_target_pairs={{0,6},{1,11},{2,8},{3,13},{4,10},{5,15},{6,12},{7,1},{8,14},{9,3},... | collective-permute-start | bytes 122888 | tf_op jit(solution)/shard_map/ppermute | solution.py:403
  23.4 6.9 %collective-permute-start = (bf16[16,640]{1,0:T(8,128)(2,1)S(1)}, bf16[16,640]{1,0:T(8,128)(2,1)S(1)}, u32[]{:S(2)}, u32[]{:S(2)}) collective-permute-start(bf16[16,640]{1,0:T(8,128)(2,1)S(1)} %get-tuple-element.25.refs_8_), channel_id=1, source_target_pairs={{0,8},{1,9},{2,10},{3,11},{4,12},{5,13},{6,14},{7,15},{8,0},{9,1},... | collective-permute-start | bytes 61448 | tf_op jit(solution)/shard_map/ppermute | solution.py:403
  30.6 2.3 %collective-permute-start.5 = (bf16[512,640]{1,0:T(8,128)(2,1)S(1)}, bf16[512,640]{1,0:T(8,128)(2,1)S(1)}, u32[]{:S(2)}, u32[]{:S(2)}) collective-permute-start(bf16[512,640]{1,0:T(8,128)(2,1)S(1)} %bitcast.11), channel_id=1, source_target_pairs={{0,1},{1,0},{2,3},{3,2},{4,5},{5,4},{6,7},{7,6},{8,9},{9,8},{10,11... | collective-permute-start | bytes 1966088 | tf_op jit(solution)/shard_map/ppermute | solution.py:397
  30.6 2.3 %collective-permute-start.6 = (bf16[32,640]{1,0:T(8,128)(2,1)S(1)}, bf16[32,640]{1,0:T(8,128)(2,1)S(1)}, u32[]{:S(2)}, u32[]{:S(2)}) collective-permute-start(bf16[32,640]{1,0:T(8,128)(2,1)S(1)} %collective-permute-done.2.refs_5_), channel_id=1, source_target_pairs={{0,1},{1,0},{2,3},{3,2},{4,5},{5,4},{6,7},{7,6},{8,9},{9,8},{10,11... | collective-permute-start | bytes 122888 | tf_op jit(solution)/shard_map/ppermute | solution.py:397
  31.1 1.8 %collective-permute-start.7 = (bf16[32,640]{1,0:T(8,128)(2,1)S(1)}, bf16[32,640]{1,0:T(8,128)(2,1)S(1)}, u32[]{:S(2)}, u32[]{:S(2)}) collective-permute-start(bf16[32,640]{1,0:T(8,128)(2,1)S(1)} %collective-permute-done.3.refs_6_), channel_id=1, source_target_pairs={{0,1},{1,0},{2,3},{3,2},{4,5},{5,4},{6,7},{7,6},{8,9},{9,8},{10,11... | collective-permute-start | bytes 122888 | tf_op jit(solution)/shard_map/ppermute | solution.py:397
  31.1 1.8 %collective-permute-start.8 = (bf16[32,640]{1,0:T(8,128)(2,1)S(1)}, bf16[32,640]{1,0:T(8,128)(2,1)S(1)}, u32[]{:S(2)}, u32[]{:S(2)}) collective-permute-start(bf16[32,640]{1,0:T(8,128)(2,1)S(1)} %collective-permute-done.4.refs_7_), channel_id=1, source_target_pairs={{0,1},{1,0},{2,3},{3,2},{4,5},{5,4},{6,7},{7,6},{8,9},{9,8},{10,11... | collective-permute-start | bytes 122888 | tf_op jit(solution)/shard_map/ppermute | solution.py:397
  31.6 1.3 %collective-permute-start.9 = (bf16[16,640]{1,0:T(8,128)(2,1)S(1)}, bf16[16,640]{1,0:T(8,128)(2,1)S(1)}, u32[]{:S(2)}, u32[]{:S(2)}) collective-permute-start(bf16[16,640]{1,0:T(8,128)(2,1)S(1)} %collective-permute-done.refs_9_), channel_id=1, source_target_pairs={{0,1},{1,0},{2,3},{3,2},{4,5},{5,4},{6,7},{7,6},{8,9},{9,8},{10,11... | collective-permute-start | bytes 61448 | tf_op jit(solution)/shard_map/ppermute | solution.py:397
  39.2 27.3 %copy-start.1 = (bf16[10,2,576]{2,1,0:T(2,128)(2,1)S(1)}, bf16[10,2,576]{2,1,0:T(2,128)(2,1)}, u32[]{:S(2)}) copy-start(bf16[10,2,576]{2,1,0:T(2,128)(2,1)} %nl_ref.1) | copy-start | bytes 69124
  39.3 27.3 %copy-start.2 = (s32[1,8]{1,0:T(1,128)S(1)}, s32[1,8]{1,0:T(1,128)}, u32[]{:S(2)}) copy-start(s32[1,8]{1,0:T(1,128)} %slot_ref.5) | copy-start | bytes 100
  39.3 27.3 %copy-start.3 = (s32[10,2]{0,1:T(2,128)S(1)}, s32[10,2]{0,1:T(2,128)}, u32[]{:S(2)}) copy-start(s32[10,2]{0,1:T(2,128)} %param.20) | copy-start | bytes 244
  39.3 27.2 %copy-start.4 = (f32[1,64]{1,0:T(1,128)S(1)}, f32[1,64]{1,0:T(1,128)}, u32[]{:S(2)}) copy-start(f32[1,64]{1,0:T(1,128)} %constant.14.clone.freq_ref) | copy-start | bytes 772
  39.3 30.1 %copy-start = (bf16[4,512,128]{2,1,0:T(8,128)(2,1)S(1)}, bf16[4,512,128]{2,1,0:T(8,128)(2,1)}, u32[]{:S(2)}) copy-start(bf16[4,512,128]{2,1,0:T(8,128)(2,1)} %wv_ref.1) | copy-start | bytes 1572868
  39.3 2.4 %collective-permute-start.10 = (bf16[640,640]{1,0:T(8,128)(2,1)S(1)}, bf16[640,640]{1,0:T(8,128)(2,1)S(1)}, u32[]{:S(2)}, u32[]{:S(2)}) collective-permute-start(bf16[640,640]{1,0:T(8,128)(2,1)S(1)} %get-tuple-element.31), channel_id=1, source_target_pairs={{0,1},{1,0},{2,3},{3,2},{4,5},{5,4},{6,7},{7,6},{8,9},{9,8},{10,11... | collective-permute-start | bytes 2457608 | tf_op jit(solution)/shard_map/ppermute | solution.py:397
  43.2 26.3 %all-to-all-start.1 = ((bf16[64,8,640]{2,1,0:T(8,128)(2,1)}), bf16[64,8,640]{2,1,0:T(8,128)(2,1)S(1)}, u32[]{:S(2)}, u32[]{:S(2)}) async-start(bf16[64,8,640]{2,1,0:T(8,128)(2,1)} %bitcast.7), calls=%async_computation.1 | async-start | bytes 1310720 | tf_op jit(solution)/shard_map/all_to_all | solution.py:394
  50.6 11.7 %collective-permute-start.12 = (bf16[32,640]{1,0:T(8,128)(2,1)S(1)}, bf16[32,640]{1,0:T(8,128)(2,1)S(1)}, u32[]{:S(2)}, u32[]{:S(2)}) collective-permute-start(bf16[32,640]{1,0:T(8,128)(2,1)S(1)} %get-tuple-element.40), channel_id=1, source_target_pairs={{0,14},{1,3},{2,0},{3,5},{4,2},{5,7},{6,4},{7,9},{8,6},{9,11},{10,... | collective-permute-start | bytes 122888 | tf_op jit(solution)/shard_map/ppermute | solution.py:403
  55.8 7.1 %collective-permute-start.13 = (bf16[32,640]{1,0:T(8,128)(2,1)S(1)}, bf16[32,640]{1,0:T(8,128)(2,1)S(1)}, u32[]{:S(2)}, u32[]{:S(2)}) collective-permute-start(bf16[32,640]{1,0:T(8,128)(2,1)S(1)} %get-tuple-element.41), channel_id=1, source_target_pairs={{0,12},{1,5},{2,14},{3,7},{4,0},{5,9},{6,2},{7,11},{8,4},{9,13},{1... | collective-permute-start | bytes 122888 | tf_op jit(solution)/shard_map/ppermute | solution.py:403
  56.7 7.1 %collective-permute-start.14 = (bf16[32,640]{1,0:T(8,128)(2,1)S(1)}, bf16[32,640]{1,0:T(8,128)(2,1)S(1)}, u32[]{:S(2)}, u32[]{:S(2)}) collective-permute-start(bf16[32,640]{1,0:T(8,128)(2,1)S(1)} %get-tuple-element.42), channel_id=1, source_target_pairs={{0,10},{1,7},{2,12},{3,9},{4,14},{5,11},{6,0},{7,13},{8,2},{9,15},... | collective-permute-start | bytes 122888 | tf_op jit(solution)/shard_map/ppermute | solution.py:403
  62.3 7.1 %collective-permute-start.15 = (bf16[32,640]{1,0:T(8,128)(2,1)S(1)}, bf16[32,640]{1,0:T(8,128)(2,1)S(1)}, u32[]{:S(2)}, u32[]{:S(2)}) collective-permute-start(bf16[32,640]{1,0:T(8,128)(2,1)S(1)} %collective-permute-done.12.refs_2_), channel_id=1, source_target_pairs={{0,1},{1,0},{2,3},{3,2},{4,5},{5,4},{6,7},{7,6},{8,9},{9,8},{10,11... | collective-permute-start | bytes 122888 | tf_op jit(solution)/shard_map/ppermute | solution.py:397
  62.9 6.5 %collective-permute-start.16 = (bf16[32,640]{1,0:T(8,128)(2,1)S(1)}, bf16[32,640]{1,0:T(8,128)(2,1)S(1)}, u32[]{:S(2)}, u32[]{:S(2)}) collective-permute-start(bf16[32,640]{1,0:T(8,128)(2,1)S(1)} %collective-permute-done.13.refs_3_), channel_id=1, source_target_pairs={{0,1},{1,0},{2,3},{3,2},{4,5},{5,4},{6,7},{7,6},{8,9},{9,8},{10,11... | collective-permute-start | bytes 122888 | tf_op jit(solution)/shard_map/ppermute | solution.py:397
  63.8 5.6 %collective-permute-start.17 = (bf16[32,640]{1,0:T(8,128)(2,1)S(1)}, bf16[32,640]{1,0:T(8,128)(2,1)S(1)}, u32[]{:S(2)}, u32[]{:S(2)}) collective-permute-start(bf16[32,640]{1,0:T(8,128)(2,1)S(1)} %collective-permute-done.14.refs_4_), channel_id=1, source_target_pairs={{0,1},{1,0},{2,3},{3,2},{4,5},{5,4},{6,7},{7,6},{8,9},{9,8},{10,11... | collective-permute-start | bytes 122888 | tf_op jit(solution)/shard_map/ppermute | solution.py:397
  64.1 5.3 %collective-permute-start.11 = (bf16[16,640]{1,0:T(8,128)(2,1)S(1)}, bf16[16,640]{1,0:T(8,128)(2,1)S(1)}, u32[]{:S(2)}, u32[]{:S(2)}) collective-permute-start(bf16[16,640]{1,0:T(8,128)(2,1)S(1)} %get-tuple-element.39), channel_id=1, source_target_pairs={{0,8},{1,9},{2,10},{3,11},{4,12},{5,13},{6,14},{7,15},{8,0},{9,1},... | collective-permute-start | bytes 61448 | tf_op jit(solution)/shard_map/ppermute | solution.py:403

commit v3 on v2

--- a/solution.py
+++ b/solution.py
@@ -83,18 +83,23 @@
     return out
 
 
-def project_kernel(heads, slots, copies, slot_ref, len_ref, pos_ref, ql_ref, wq_hbm, wk_hbm, freq_ref,
-                   out_ref, res_ref, own_ref, rows_ref, all_ref, wq_ref, wk_ref, sems):
+def project_kernel(heads, slots, copies, slot_hbm, len_hbm, pos_hbm, ql_hbm, wq_hbm, wk_hbm, freq_hbm,
+                   out_ref, res_ref, own_ref, rows_ref, all_ref, slot_ref, len_ref, pos_ref, ql_ref, wq_ref, wk_ref,
+                   freq_ref, sems):
     rows = ql_ref.shape[0]
     resident = rows - slots
     chunks = wq_ref.shape[0]
     step = wq_ref.shape[1]
+    small = ((ql_hbm, ql_ref), (slot_hbm, slot_ref), (len_hbm, len_ref), (pos_hbm, pos_ref), (freq_hbm, freq_ref))
+    small = [pltpu.make_async_copy(*pair, sems.at[chunks + 1 + n]) for n, pair in enumerate(small)]
     loads = [
         pltpu.make_async_copy(wq_hbm.at[pl.ds(c * step, step)], wq_ref.at[c], sems.at[c]) for c in range(chunks)
     ]
     loads.append(pltpu.make_async_copy(wk_hbm, wk_ref, sems.at[chunks]))
-    for load in loads:
+    for load in small + loads:
         load.start()
+    for load in small:
+        load.wait()
     rows_ref[...] = jnp.zeros_like(rows_ref)
     for r in range(rows):
         rows_ref[2 * r : 2 * r + 2, :] = ql_ref[r].astype(F32)
@@ -130,7 +135,7 @@
     res_ref[...] = own[slots * piece :].astype(BF)
 
 
-def own_keys_kernel(slots, slot_ref, pos_ref, nl_ref, freq_ref, own_ref, out_ref, stat_ref, keys_ref):
+def own_keys_kernel(slots, slot_ref, pos_ref, nl_ref, freq_ref, own_ref, out_ref, stat_ref, order_ref, keys_ref):
     rows = nl_ref.shape[0]
     resident = rows - slots
     count = own_ref.shape[0]
@@ -154,6 +159,9 @@
     out_ref[...] = dot(weights.astype(BF), latent)
     stat_ref[:, :128] = jnp.broadcast_to(highest, (count, 128))
     stat_ref[:, 128:] = jnp.broadcast_to(total, (count, 128))
+    row = row_of(slot_ref, slots, resident, (1, count), 1, piece)
+    target = 2 * row + iota((1, count), 1) % 2
+    order_ref[...] = jnp.where(iota((32, count), 0) == target, 1.0, 0.0).astype(BF)
 
 
 def parts_of(value):
@@ -188,20 +196,17 @@
     return highest * SCALE, jnp.sum(weights, 1, keepdims=True), weights.astype(BF)
 
 
-def attend_kernel(piece, offset_ref, fresh_hbm, cache_hbm, new_own, new_other, *refs):
+def attend_kernel(piece, fresh_hbm, cache_ref, new_own, new_other, *refs):
     send_ref, keep_ref, stat_ref, keys_ref, sems = refs[-5:]
     blocks = refs[:-5]
     res_other, res_own = blocks[: len(blocks) // 2], blocks[len(blocks) // 2 :]
-    slots, resident = fresh_hbm.shape[0], cache_hbm.shape[0]
+    slots, resident = fresh_hbm.shape[0], cache_ref.shape[0]
     rows = slots + resident
     half = new_own.shape[0] // slots
     loads = [pltpu.make_async_copy(fresh_hbm.at[i], keys_ref.at[i], sems.at[i]) for i in range(slots)]
-    loads += [
-        pltpu.make_async_copy(cache_hbm.at[i], keys_ref.at[slots + i], sems.at[slots + i]) for i in range(resident)
-    ]
     for load in loads:
         load.start()
-    arrived = 0
+    offset = (lax.axis_index("zx") * lax.axis_size("core") + lax.axis_index("core")) * keys_ref.shape[2]
 
     def queries_of(i):
         if i < slots:
@@ -213,26 +218,29 @@
             [ref[k + at : k + at + piece, :] for ref in res_other + res_own for k in range(0, ref.shape[0], step)], 0
         )
 
+    def keys_of(i):
+        return keys_ref.at[i] if i < slots else cache_ref.at[i - slots]
+
     def scores_of(i):
         queries = queries_of(i)
         length = queries[:, LAT + ROPE : LAT + ROPE + 2].astype(F32)
-        length = (length[:, 0:1] * 128.0 + length[:, 1:2]).astype(jnp.int32) - offset_ref[0]
-        return dot(queries[:, : LAT + ROPE], keys_ref[i]), length
-
-    loads[0].wait()
-    arrived = 1
-    ahead = scores_of(0)
-    for i in range(rows):
+        length = (length[:, 0:1] * 128.0 + length[:, 1:2]).astype(jnp.int32) - offset
+        return dot(queries[:, : LAT + ROPE], keys_of(i)[...]), length
+
+    order = [*range(slots, rows), *range(slots)]
+    arrived = 0
+    ahead = scores_of(order[0])
+    for n, i in enumerate(order):
         scores, length = ahead
-        if i + 1 < rows:
-            if i + 1 == arrived:
-                upto = min(rows, arrived + i + 2)
+        if n + 1 < rows:
+            if order[n + 1] == arrived:
+                upto = min(slots, arrived + n + 1)
                 for load in loads[arrived:upto]:
                     load.wait()
                 arrived = upto
-            ahead = scores_of(i + 1)
+            ahead = scores_of(order[n + 1])
         highest, total, weights = softmax_part(scores, length)
-        mean = dot(weights, keys_ref[i, :LAT, :], ((1,), (1,))) * (1.0 / jnp.maximum(total, 1e-30))
+        mean = dot(weights, keys_of(i)[:LAT, :], ((1,), (1,))) * (1.0 / jnp.maximum(total, 1e-30))
         stats = with_stats(highest, total)
         span = slice(i * half, (i + 1) * half)
         send_ref[span, :LAT] = mean[:half].astype(BF)
@@ -253,22 +261,33 @@
     return mean.astype(BF), with_stats(top, both)
 
 
-def join_kernel(slots, piece, got_ref, keep_ref, stat_ref, new_ref, *res_refs):
-    mean, stats = joined(got_ref[...], keep_ref[...], stat_ref[...])
+def join_kernel(slots, piece, got_ref, keep_ref, stat_ref, new_hbm, *refs):
+    res_refs, new_ref, sems = refs[:-2], refs[-2], refs[-1]
     count = new_ref.shape[0]
     half = count // slots
-    new_ref[:, :LAT] = mean[:count]
-    new_ref[:, LAT:] = stats[:count]
     resident = got_ref.shape[0] // half - slots
+    parts = sems.shape[0]
+    stores = []
+    for c in range(parts):
+        span = slice(c * count // parts, (c + 1) * count // parts)
+        mean, stats = joined(got_ref[span, :], keep_ref[span, :], stat_ref[span, :])
+        new_ref[span, :LAT] = mean
+        new_ref[span, LAT:] = stats
+        at = pl.ds(c * count // parts, count // parts)
+        stores.append(pltpu.make_async_copy(new_ref.at[at], new_hbm.at[at], sems.at[c]))
+        stores[c].start()
+    mean, stats = joined(got_ref[count:, :], keep_ref[count:, :], stat_ref[count:, :])
     block = 0
     for ref in res_refs:
         for k in range(0, ref.shape[0], resident * piece):
             for i in range(resident):
-                at = count + i * half + block * piece
+                at = i * half + block * piece
                 span = slice(k + i * piece, k + (i + 1) * piece)
                 ref[span, :LAT] = mean[at : at + piece]
                 ref[span, LAT:] = stats[at : at + piece]
             block += 1
+    for store in stores:
+        store.wait()
 
 
 def merged(means, tails, own, own_highest, own_total):
@@ -285,7 +304,7 @@
     return summed.astype(BF)
 
 
-def finish_kernel(slots, slot_ref, new_ref, own_ref, stat_ref, wv_ref, *refs):
+def finish_kernel(slots, order_ref, new_ref, own_ref, stat_ref, wv_ref, *refs):
     out_ref = refs[-1]
     heads = wv_ref.shape[0]
     piece = 2 * heads
@@ -294,7 +313,8 @@
     n = resident * piece
     copies = new_ref.shape[0] // slots // piece
     mine = copies // 2 + 1
-    parts = [ref[:n, :] for ref in refs[:mine]] + [ref[n:, :] for ref in refs[mine:-1]]
+    far_ref = refs[mine]
+    parts = [ref[:n, :] for ref in refs[:mine]] + [far_ref[k : k + n, :] for k in range(0, far_ref.shape[0], n)]
 
     def own_of(at, n):
         return own_ref[at : at + n, :], stat_ref[at : at + n, :128], stat_ref[at : at + n, 128:]
@@ -314,10 +334,7 @@
         one = dot(latent, wv_ref[h])
         values.append(jnp.where(inner // 2 == h, one, 0.0).astype(BF))
     values = jnp.concatenate(values, 1)
-    row = row_of(slot_ref, slots, resident, (1, count), 1, piece)
-    target = 2 * row + iota((1, count), 1) % 2
-    select = jnp.where(iota((32, count), 0) == target, 1.0, 0.0).astype(BF)
-    out = dot(select, values)
+    out = dot(order_ref[...], values)
     for r in range(rows):
         out_ref[r] = out[2 * r : 2 * r + 2].astype(BF)
 
@@ -348,11 +365,9 @@
     copies = lax.axis_size("zx")
     piece = 2 * heads
     half = copies * piece
-    chunks = 4
+    chunks = 6
     freqs = 50000.0 ** (-np.arange(ROPE // 2, dtype=np.float64) / (ROPE // 2))
     freqs = jnp.asarray(np.concatenate([freqs, freqs]).astype(np.float32)[None])
-    place = lax.axis_index("zx")
-    offset = ((place * lax.axis_size("core") + lax.axis_index("core")) * tokens).reshape(1)
     positions = positions.T
     cache = jnp.swapaxes(cache, 1, 2)
     fresh = jnp.swapaxes(fresh[0], 1, 2)
@@ -367,24 +382,33 @@
             shape((resident * piece, WIDE), BF),
             shape((rows * piece, WIDE), BF),
         ),
-        in_specs=[SMEM] * 3 + [VMEM, ANY, ANY, VMEM],
+        in_specs=[ANY] * 7,
         out_specs=[VMEM] * 3,
         scratch_shapes=[
             pltpu.VMEM((32, depth), F32),
             pltpu.VMEM((heads * 32, WIDE), BF),
+            pltpu.SMEM(fresh_slot.shape, jnp.int32),
+            pltpu.SMEM(lengths.shape, jnp.int32),
+            pltpu.SMEM(positions.shape, jnp.int32),
+            pltpu.VMEM(query_latent.shape, BF),
             pltpu.VMEM((chunks, depth // chunks, heads * HEAD), BF),
             pltpu.VMEM((heads, NOPE, LAT), BF),
-            pltpu.SemaphoreType.DMA((chunks + 1,)),
+            pltpu.VMEM(freqs.shape, F32),
+            pltpu.SemaphoreType.DMA((chunks + 6,)),
         ],
         compiler_params=params(16),
         name="project",
     )(*map(in_hbm, (fresh_slot, lengths, positions, query_latent, w_query, w_key_up, freqs)))
 
-    own_out, own_stat = pl.pallas_call(
+    own_out, own_stat, order = pl.pallas_call(
         functools.partial(own_keys_kernel, slots),
-        out_shape=(shape((rows * piece, LAT), F32), shape((rows * piece, 256), F32)),
+        out_shape=(
+            shape((rows * piece, LAT), F32),
+            shape((rows * piece, 256), F32),
+            shape((32, rows * piece), BF),
+        ),
         in_specs=[SMEM] * 2 + [VMEM] * 3,
-        out_specs=[VMEM] * 2,
+        out_specs=[VMEM] * 3,
         scratch_shapes=[pltpu.VMEM((32, LAT + ROPE), F32)],
         compiler_params=params(32),
         name="own_keys",
@@ -413,13 +437,13 @@
     send, keep, stat = pl.pallas_call(
         functools.partial(attend_kernel, piece),
         out_shape=(shape((rows * half, WIDE), BF), shape((rows * half, LAT), F32), shape((rows * half, 128), BF)),
-        in_specs=[SMEM] + [ANY] * 2 + [VMEM] * (4 + copies),
+        in_specs=[ANY] + [VMEM] * (5 + copies),
         out_specs=[VMEM] * 3,
-        scratch_shapes=[pltpu.VMEM((rows, LAT + ROPE, tokens), BF), pltpu.SemaphoreType.DMA((rows,))],
+        scratch_shapes=[pltpu.VMEM((slots, LAT + ROPE, tokens), BF), pltpu.SemaphoreType.DMA((slots,))],
         compiler_params=params(24),
         cost_estimate=cost(rows * 5 * 10**8, rows * 2 * 10**6),
         name="attend",
-    )(offset, in_hbm(fresh), in_hbm(cache), new_own, new_other, *far, res_sib, across_sib, *near, res_q, across)
+    )(in_hbm(fresh), pltpu.with_memory_space_constraint(cache, pltpu.VMEM), new_own, new_other, *far, res_sib, across_sib, *near, res_q, across)
 
     new_part, *res_parts = pl.pallas_call(
         functools.partial(join_kernel, slots, piece),
@@ -427,7 +451,8 @@
         + (shape((2 * resident * piece, WIDE), BF),) * len(near)
         + (shape((resident * piece, WIDE), BF),) * 2,
         in_specs=[VMEM] * 3,
-        out_specs=(VMEM,) * (len(near) + 3),
+        out_specs=(ANY,) + (VMEM,) * (len(near) + 2),
+        scratch_shapes=[pltpu.VMEM((slots * half, WIDE), BF), pltpu.SemaphoreType.DMA((4,))],
         compiler_params=params(32),
         name="join_cores",
     )(swap(send), keep, stat)
@@ -435,16 +460,18 @@
     *near, res_here, across = res_parts
     near = [turned(x, k + 1, -1) for k, x in enumerate(near)]
     across = turned(across, copies // 2, -1)
-    res_back = [res_here, across, *near, *map(swap, near)]
+    own_out, own_stat, order, across, *near = lax.optimization_barrier((own_out, own_stat, order, across, *near))
+    far = swap(jnp.concatenate([x[resident * piece :] for x in near], 0))
+    res_back = [res_here, across, *near, far]
 
     return pl.pallas_call(
         functools.partial(finish_kernel, slots),
         out_shape=shape((rows, 2, heads * 128), BF),
-        in_specs=[SMEM] + [VMEM] * (4 + len(res_back)),
+        in_specs=[VMEM] * (5 + len(res_back)),
         out_specs=VMEM,
         compiler_params=params(32),
         name="finish",
-    )(fresh_slot, new_back, own_out, own_stat, w_value_up, *res_back)
+    )(order, new_back, own_out, own_stat, w_value_up, *res_back)
 
 
 def solution(mesh):

time: 71.6 us -> 67.1 us (0.937)
  waiting for transfers between devices: 17.4 us -> 14.9 us
  Pallas kernels: 14.7 us -> 12.7 us
    ppermute x8, waiting for transfers between devices: 12.5 us -> 8.23 us  [turned(): return lax.ppermute(x, ('zx', 'core'), pairs)]
    ppermute x10 -> x8, waiting for transfers between devices: 4.65 us -> 5.89 us  [swap(): return lax.ppermute(x, 'core', [(0, 1), (1, 0)])]
    ppermute x10 -> x8, starting transfers between devices: 2.33 us -> 1.4 us  [swap(): return lax.ppermute(x, 'core', [(0, 1), (1, 0)])]
  transfers between devices with their start and end apart: 20 -> 18, of which waited for: 8 -> 8; matrix products, arithmetic and copies ran while one was open for 0% -> 0% of each run, Pallas kernels for 1% -> 2%
where the time goes in v3:
time: 67.1 us; the launch traced here: 66.2 us
  starting transfers between devices  38.4 us (57%)
  waiting for transfers between devices  14.9 us (22%)
  Pallas kernels  12.7 us (19%)
    all_to_all x2, starting transfers between devices, exchange(): lax.all_to_all(x.reshape(n, -1, WIDE), axes, 0, 0, tiled=True)  18.9 us
    ppermute x8, starting transfers between devices, turned(): return lax.ppermute(x, ('zx', 'core'), pairs)  18 us
    ppermute x8, waiting for transfers between devices, turned(): return lax.ppermute(x, ('zx', 'core'), pairs)  8.23 us
    ppermute x8, waiting for transfers between devices, swap(): return lax.ppermute(x, 'core', [(0, 1), (1, 0)])  5.89 us
    pallas_call x1, Pallas kernels, local(): pl.pallas_call(functools.partial(attend_kernel, piece), out_shape=(shape(...  5.7 us
    pallas_call x1, Pallas kernels, local(): pl.pallas_call(functools.partial(project_kernel, heads, slots, copies), o...  3.34 us
    ppermute x8, starting transfers between devices, swap(): return lax.ppermute(x, 'core', [(0, 1), (1, 0)])  1.4 us
  transfers between devices with their start and end apart: 18, of which 8 were waited for; matrix products, arithmetic and copies ran while one was open for 0% of the time, Pallas kernels for 2%

profile of v3, /device:TPU:0, one launch (start us, length us, event | category | flops | bytes accessed | tf_op | source)
XLA Modules:
  0.0 66.2 jit_solution(4736798416773558283)
XLA Ops:
  0.0 3.3 %project.1 = (bf16[512,640]{1,0:T(8,128)(2,1)}, bf16[16,640]{1,0:T(8,128)(2,1)S(1)}, bf16[80,640]{1,0:T(8,128)(2,1)S(1)}) custom-call(s32[1,8]{1,0:T(1,128)} %slot_ref.1, s32[10]{0:T(128)} %len_hbm.1, s32[2,10]{1,0:T(2,128)} %bitcast.12, bf16[10,2,1536]{2,1,0:T(2,128)(2,1)} %ql_hbm.1, bf16[1536,768]{1,0:T(8,128)(2,1)} %wq_hbm.1, ...), custom_call_target="tpu_custom_call" | custom-call | tf_op jit(solution)/shard_map/project/pallas_call | solution.py:378
  3.3 11.5 %all-to-all-start = ((bf16[64,8,640]{2,1,0:T(8,128)(2,1)}), bf16[64,8,640]{2,1,0:T(8,128)(2,1)S(1)}, u32[]{:S(2)}, u32[]{:S(2)}) async-start(bf16[64,8,640]{2,1,0:T(8,128)(2,1)} %bitcast.4), calls=%async_computation | async-start | bytes 1310720 | tf_op jit(solution)/shard_map/all_to_all | solution.py:418
  14.9 0.1 collective-permute-start.1
  15.0 1.2 %collective-permute-done.1.refs_3_ = bf16[16,640]{1,0:T(8,128)(2,1)S(1)} collective-permute-done((bf16[16,640]{1,0:T(8,128)(2,1)S(1)}, bf16[16,640]{1,0:T(8,128)(2,1)S(1)}, u32[]{:S(2)}, u32[]{:S(2)}) %collective-permute-start.1) | collective-permute-done | bytes 20512 | tf_op jit(solution)/shard_map/ppermute | solution.py:421
  16.1 3.1 %collective-permute-start.2 = (bf16[32,640]{1,0:T(8,128)(2,1)S(1)}, bf16[32,640]{1,0:T(8,128)(2,1)S(1)}, u32[]{:S(2)}, u32[]{:S(2)}) collective-permute-start(bf16[32,640]{1,0:T(8,128)(2,1)S(1)} %constant_dynamic-update-slice_fusion), channel_id=1, source_target_pairs={{0,2},{1,15},{2,4},{3,1},{4,6},{5,3},{6,8},{7,5},{8,10},{9,7},{10,... | collective-permute-start | bytes 122888 | tf_op jit(solution)/shard_map/ppermute | solution.py:427
  19.2 1.5 %collective-permute-start.3 = (bf16[32,640]{1,0:T(8,128)(2,1)S(1)}, bf16[32,640]{1,0:T(8,128)(2,1)S(1)}, u32[]{:S(2)}, u32[]{:S(2)}) collective-permute-start(bf16[32,640]{1,0:T(8,128)(2,1)S(1)} %constant_dynamic-update-slice_fusion), channel_id=1, source_target_pairs={{0,4},{1,13},{2,6},{3,15},{4,8},{5,1},{6,10},{7,3},{8,12},{9,5},{1... | collective-permute-start | bytes 122888 | tf_op jit(solution)/shard_map/ppermute | solution.py:427
  20.7 2.1 %collective-permute-start.4 = (bf16[32,640]{1,0:T(8,128)(2,1)S(1)}, bf16[32,640]{1,0:T(8,128)(2,1)S(1)}, u32[]{:S(2)}, u32[]{:S(2)}) collective-permute-start(bf16[32,640]{1,0:T(8,128)(2,1)S(1)} %constant_dynamic-update-slice_fusion), channel_id=1, source_target_pairs={{0,6},{1,11},{2,8},{3,13},{4,10},{5,15},{6,12},{7,1},{8,14},{9,3},... | collective-permute-start | bytes 122888 | tf_op jit(solution)/shard_map/ppermute | solution.py:427
  22.8 2.1 %collective-permute-start = (bf16[16,640]{1,0:T(8,128)(2,1)S(1)}, bf16[16,640]{1,0:T(8,128)(2,1)S(1)}, u32[]{:S(2)}, u32[]{:S(2)}) collective-permute-start(bf16[16,640]{1,0:T(8,128)(2,1)S(1)} %get-tuple-element.37.refs_8_), channel_id=1, source_target_pairs={{0,8},{1,9},{2,10},{3,11},{4,12},{5,13},{6,14},{7,15},{8,0},{9,1},... | collective-permute-start | bytes 61448 | tf_op jit(solution)/shard_map/ppermute | solution.py:427
  24.8 4.8 %collective-permute-done.refs_9_ = bf16[16,640]{1,0:T(8,128)(2,1)S(1)} collective-permute-done((bf16[16,640]{1,0:T(8,128)(2,1)S(1)}, bf16[16,640]{1,0:T(8,128)(2,1)S(1)}, u32[]{:S(2)}, u32[]{:S(2)}) %collective-permute-start) | collective-permute-done | bytes 20512 | tf_op jit(solution)/shard_map/ppermute | solution.py:427
  29.6 0.2 all-to-all-done
  29.9 0.5 collective-permute-start.6
  30.4 0.5 collective-permute-start.8
  30.9 1.3 %collective-permute-done.9.refs_4_ = bf16[16,640]{1,0:T(8,128)(2,1)S(1)} collective-permute-done((bf16[16,640]{1,0:T(8,128)(2,1)S(1)}, bf16[16,640]{1,0:T(8,128)(2,1)S(1)}, u32[]{:S(2)}, u32[]{:S(2)}) %collective-permute-start.9) | collective-permute-done | bytes 20512 | tf_op jit(solution)/shard_map/ppermute | solution.py:421
  32.2 5.7 %attend.1 = (bf16[640,640]{1,0:T(8,128)(2,1)S(1)}, f32[640,512]{1,0:T(8,128)S(1)}, bf16[640,128]{1,0:T(8,128)(2,1)S(1)}) custom-call(bf16[8,576,768]{2,1,0:T(8,128)(2,1)} %bitcast.15, bf16[2,576,768]{2,1,0:T(8,128)(2,1)S(1)} %bitcast.14, bf16[512,640]{1,0:T(8,128)(2,1)S(1)} %bitcast.11, bf16[512,640]{1,0:T(8,128)(2,1)S(1)} %collective-permute-done.5.new_other, ...), custom_call_target="tpu_custom_call" | custom-call | flops 5000000000 | bytes 20000000 | tf_op jit(solution)/shard_map/attend/pallas_call | solution.py:437
  37.9 0.0 copy-start.1
  38.0 0.0 copy-start.2
  38.0 0.0 copy-start.3
  38.0 0.0 copy-start.4
  38.0 0.2 collective-permute-start.10
  38.2 2.2 %collective-permute-done.10.got_ref = bf16[640,640]{1,0:T(8,128)(2,1)S(1)} collective-permute-done((bf16[640,640]{1,0:T(8,128)(2,1)S(1)}, bf16[640,640]{1,0:T(8,128)(2,1)S(1)}, u32[]{:S(2)}, u32[]{:S(2)}) %collective-permute-start.10) | collective-permute-done | bytes 819232 | tf_op jit(solution)/shard_map/ppermute | solution.py:421
  40.4 1.3 %join_cores.1 = (bf16[512,640]{1,0:T(8,128)(2,1)}, bf16[32,640]{1,0:T(8,128)(2,1)S(1)}, bf16[32,640]{1,0:T(8,128)(2,1)S(1)}, bf16[32,640]{1,0:T(8,128)(2,1)S(1)}...) custom-call(bf16[640,640]{1,0:T(8,128)(2,1)S(1)} %collective-permute-done.10.got_ref, ...), custom_call_target="tpu_custom_call" | custom-call | tf_op jit(solution)/shard_map/join_cores/pallas_call | solution.py:448
  41.7 7.4 %all-to-all-start.1 = ((bf16[64,8,640]{2,1,0:T(8,128)(2,1)}), bf16[64,8,640]{2,1,0:T(8,128)(2,1)S(1)}, u32[]{:S(2)}, u32[]{:S(2)}) async-start(bf16[64,8,640]{2,1,0:T(8,128)(2,1)} %bitcast.6), calls=%async_computation.1 | async-start | bytes 1310720 | tf_op jit(solution)/shard_map/all_to_all | solution.py:418
  49.2 5.3 %collective-permute-start.12 = (bf16[32,640]{1,0:T(8,128)(2,1)S(1)}, bf16[32,640]{1,0:T(8,128)(2,1)S(1)}, u32[]{:S(2)}, u32[]{:S(2)}) collective-permute-start(bf16[32,640]{1,0:T(8,128)(2,1)S(1)} %get-tuple-element.47), channel_id=1, source_target_pairs={{0,14},{1,3},{2,0},{3,5},{4,2},{5,7},{6,4},{7,9},{8,6},{9,11},{10,... | collective-permute-start | bytes 122888 | tf_op jit(solution)/shard_map/ppermute | solution.py:427
  54.4 0.9 %collective-permute-start.13 = (bf16[32,640]{1,0:T(8,128)(2,1)S(1)}, bf16[32,640]{1,0:T(8,128)(2,1)S(1)}, u32[]{:S(2)}, u32[]{:S(2)}) collective-permute-start(bf16[32,640]{1,0:T(8,128)(2,1)S(1)} %get-tuple-element.48), channel_id=1, source_target_pairs={{0,12},{1,5},{2,14},{3,7},{4,0},{5,9},{6,2},{7,11},{8,4},{9,13},{1... | collective-permute-start | bytes 122888 | tf_op jit(solution)/shard_map/ppermute | solution.py:427
  55.3 0.6 collective-permute-start.14
  55.8 2.7 %collective-permute-start.11 = (bf16[16,640]{1,0:T(8,128)(2,1)S(1)}, bf16[16,640]{1,0:T(8,128)(2,1)S(1)}, u32[]{:S(2)}, u32[]{:S(2)}) collective-permute-start(bf16[16,640]{1,0:T(8,128)(2,1)S(1)} %get-tuple-element.46), channel_id=1, source_target_pairs={{0,8},{1,9},{2,10},{3,11},{4,12},{5,13},{6,14},{7,15},{8,0},{9,1},... | collective-permute-start | bytes 61448 | tf_op jit(solution)/shard_map/ppermute | solution.py:427
  58.5 1.0 %own_keys.1 = (f32[80,512]{1,0:T(8,128)S(1)}, f32[80,256]{1,0:T(8,128)S(1)}, bf16[32,80]{1,0:T(8,128)(2,1)S(1)}) custom-call(s32[1,8]{1,0:T(1,128)S(1)} %copy-done.3, s32[2,10]{1,0:T(2,128)S(1)} %bitcast.13, bf16[10,2,576]{2,1,0:T(2,128)(2,1)S(1)} %copy-done.1, f32[1,64]{1,0:T(1,128)S(1)} %copy-done.4, bf16[80,640]{1,0:T(8,128)(2,1)S(1)} %get-tuple-element.32.own_ref), custom_call_target="tpu_custom_call" | custom-call | tf_op jit(solution)/shard_map/own_keys/pallas_call | solution.py:403
  59.6 3.4 %collective-permute-done.11.refs_1_ = bf16[16,640]{1,0:T(8,128)(2,1)S(1)} collective-permute-done((bf16[16,640]{1,0:T(8,128)(2,1)S(1)}, bf16[16,640]{1,0:T(8,128)(2,1)S(1)}, u32[]{:S(2)}, u32[]{:S(2)}) %collective-permute-start.11) | collective-permute-done | bytes 20512 | tf_op jit(solution)/shard_map/ppermute | solution.py:427
  63.0 0.1 collective-permute-start.15
  63.1 1.2 %collective-permute-done.15.refs_5_ = bf16[48,640]{1,0:T(8,128)(2,1)S(1)} collective-permute-done((bf16[48,640]{1,0:T(8,128)(2,1)S(1)}, bf16[48,640]{1,0:T(8,128)(2,1)S(1)}, u32[]{:S(2)}, u32[]{:S(2)}) %collective-permute-start.15) | collective-permute-done | bytes 61472 | tf_op jit(solution)/shard_map/ppermute | solution.py:421
  64.4 0.5 all-to-all-done.1
  64.9 1.3 %finish.1 = bf16[10,2,512]{2,1,0:T(2,128)(2,1)} custom-call(bf16[32,80]{1,0:T(8,128)(2,1)S(1)} %get-tuple-element.50.order_ref, bf16[512,640]{1,0:T(8,128)(2,1)S(1)} %bitcast.9, f32[80,512]{1,0:T(8,128)S(1)} %get-tuple-element.52.own_ref, f32[80,256]{1,0:T(8,128)S(1)} %get-tuple-element.53.stat_ref, bf16[4,512,128]{2,1,0:T(8,128)(2,1)S(1)} %copy-done, ...), custom_call_target="tpu_custom_call" | custom-call | tf_op jit(solution)/shard_map/finish/pallas_call | solution.py:467
  (27 shorter events, 0.1 us)
Async XLA Ops:
  0.0 32.2 %copy-start.5 = (bf16[2,768,576]{1,2,0:T(8,128)(2,1)S(1)}, bf16[2,768,576]{1,2,0:T(8,128)(2,1)}, u32[]{:S(2)}) copy-start(bf16[2,768,576]{1,2,0:T(8,128)(2,1)} %param.15) | copy-start | bytes 5308420
  3.3 26.5 %all-to-all-start = ((bf16[64,8,640]{2,1,0:T(8,128)(2,1)}), bf16[64,8,640]{2,1,0:T(8,128)(2,1)S(1)}, u32[]{:S(2)}, u32[]{:S(2)}) async-start(bf16[64,8,640]{2,1,0:T(8,128)(2,1)} %bitcast.4), calls=%async_computation | async-start | bytes 1310720 | tf_op jit(solution)/shard_map/all_to_all | solution.py:418
  14.9 1.3 %collective-permute-start.1 = (bf16[16,640]{1,0:T(8,128)(2,1)S(1)}, bf16[16,640]{1,0:T(8,128)(2,1)S(1)}, u32[]{:S(2)}, u32[]{:S(2)}) collective-permute-start(bf16[16,640]{1,0:T(8,128)(2,1)S(1)} %get-tuple-element.37.refs_8_), channel_id=1, source_target_pairs={{0,1},{1,0},{2,3},{3,2},{4,5},{5,4},{6,7},{7,6},{8,9},{9,8},{10,11... | collective-permute-start | bytes 61448 | tf_op jit(solution)/shard_map/ppermute | solution.py:421
  16.1 13.5 %collective-permute-start.2 = (bf16[32,640]{1,0:T(8,128)(2,1)S(1)}, bf16[32,640]{1,0:T(8,128)(2,1)S(1)}, u32[]{:S(2)}, u32[]{:S(2)}) collective-permute-start(bf16[32,640]{1,0:T(8,128)(2,1)S(1)} %constant_dynamic-update-slice_fusion), channel_id=1, source_target_pairs={{0,2},{1,15},{2,4},{3,1},{4,6},{5,3},{6,8},{7,5},{8,10},{9,7},{10,... | collective-permute-start | bytes 122888 | tf_op jit(solution)/shard_map/ppermute | solution.py:427
  19.2 10.4 %collective-permute-start.3 = (bf16[32,640]{1,0:T(8,128)(2,1)S(1)}, bf16[32,640]{1,0:T(8,128)(2,1)S(1)}, u32[]{:S(2)}, u32[]{:S(2)}) collective-permute-start(bf16[32,640]{1,0:T(8,128)(2,1)S(1)} %constant_dynamic-update-slice_fusion), channel_id=1, source_target_pairs={{0,4},{1,13},{2,6},{3,15},{4,8},{5,1},{6,10},{7,3},{8,12},{9,5},{1... | collective-permute-start | bytes 122888 | tf_op jit(solution)/shard_map/ppermute | solution.py:427
  20.7 9.0 %collective-permute-start.4 = (bf16[32,640]{1,0:T(8,128)(2,1)S(1)}, bf16[32,640]{1,0:T(8,128)(2,1)S(1)}, u32[]{:S(2)}, u32[]{:S(2)}) collective-permute-start(bf16[32,640]{1,0:T(8,128)(2,1)S(1)} %constant_dynamic-update-slice_fusion), channel_id=1, source_target_pairs={{0,6},{1,11},{2,8},{3,13},{4,10},{5,15},{6,12},{7,1},{8,14},{9,3},... | collective-permute-start | bytes 122888 | tf_op jit(solution)/shard_map/ppermute | solution.py:427
  22.8 6.9 %collective-permute-start = (bf16[16,640]{1,0:T(8,128)(2,1)S(1)}, bf16[16,640]{1,0:T(8,128)(2,1)S(1)}, u32[]{:S(2)}, u32[]{:S(2)}) collective-permute-start(bf16[16,640]{1,0:T(8,128)(2,1)S(1)} %get-tuple-element.37.refs_8_), channel_id=1, source_target_pairs={{0,8},{1,9},{2,10},{3,11},{4,12},{5,13},{6,14},{7,15},{8,0},{9,1},... | collective-permute-start | bytes 61448 | tf_op jit(solution)/shard_map/ppermute | solution.py:427
  29.9 2.3 %collective-permute-start.5 = (bf16[512,640]{1,0:T(8,128)(2,1)S(1)}, bf16[512,640]{1,0:T(8,128)(2,1)S(1)}, u32[]{:S(2)}, u32[]{:S(2)}) collective-permute-start(bf16[512,640]{1,0:T(8,128)(2,1)S(1)} %bitcast.10), channel_id=1, source_target_pairs={{0,1},{1,0},{2,3},{3,2},{4,5},{5,4},{6,7},{7,6},{8,9},{9,8},{10,11... | collective-permute-start | bytes 1966088 | tf_op jit(solution)/shard_map/ppermute | solution.py:421
  29.9 2.3 %collective-permute-start.6 = (bf16[32,640]{1,0:T(8,128)(2,1)S(1)}, bf16[32,640]{1,0:T(8,128)(2,1)S(1)}, u32[]{:S(2)}, u32[]{:S(2)}) collective-permute-start(bf16[32,640]{1,0:T(8,128)(2,1)S(1)} %collective-permute-done.2.refs_5_), channel_id=1, source_target_pairs={{0,1},{1,0},{2,3},{3,2},{4,5},{5,4},{6,7},{7,6},{8,9},{9,8},{10,11... | collective-permute-start | bytes 122888 | tf_op jit(solution)/shard_map/ppermute | solution.py:421
  30.4 1.8 %collective-permute-start.7 = (bf16[32,640]{1,0:T(8,128)(2,1)S(1)}, bf16[32,640]{1,0:T(8,128)(2,1)S(1)}, u32[]{:S(2)}, u32[]{:S(2)}) collective-permute-start(bf16[32,640]{1,0:T(8,128)(2,1)S(1)} %collective-permute-done.3.refs_6_), channel_id=1, source_target_pairs={{0,1},{1,0},{2,3},{3,2},{4,5},{5,4},{6,7},{7,6},{8,9},{9,8},{10,11... | collective-permute-start | bytes 122888 | tf_op jit(solution)/shard_map/ppermute | solution.py:421
  30.4 1.8 %collective-permute-start.8 = (bf16[32,640]{1,0:T(8,128)(2,1)S(1)}, bf16[32,640]{1,0:T(8,128)(2,1)S(1)}, u32[]{:S(2)}, u32[]{:S(2)}) collective-permute-start(bf16[32,640]{1,0:T(8,128)(2,1)S(1)} %collective-permute-done.4.refs_7_), channel_id=1, source_target_pairs={{0,1},{1,0},{2,3},{3,2},{4,5},{5,4},{6,7},{7,6},{8,9},{9,8},{10,11... | collective-permute-start | bytes 122888 | tf_op jit(solution)/shard_map/ppermute | solution.py:421
  30.9 1.3 %collective-permute-start.9 = (bf16[16,640]{1,0:T(8,128)(2,1)S(1)}, bf16[16,640]{1,0:T(8,128)(2,1)S(1)}, u32[]{:S(2)}, u32[]{:S(2)}) collective-permute-start(bf16[16,640]{1,0:T(8,128)(2,1)S(1)} %collective-permute-done.refs_9_), channel_id=1, source_target_pairs={{0,1},{1,0},{2,3},{3,2},{4,5},{5,4},{6,7},{7,6},{8,9},{9,8},{10,11... | collective-permute-start | bytes 61448 | tf_op jit(solution)/shard_map/ppermute | solution.py:421
  37.9 20.6 %copy-start.1 = (bf16[10,2,576]{2,1,0:T(2,128)(2,1)S(1)}, bf16[10,2,576]{2,1,0:T(2,128)(2,1)}, u32[]{:S(2)}) copy-start(bf16[10,2,576]{2,1,0:T(2,128)(2,1)} %nl_ref.1) | copy-start | bytes 69124
  38.0 20.6 %copy-start.2 = (s32[10,2]{0,1:T(2,128)S(1)}, s32[10,2]{0,1:T(2,128)}, u32[]{:S(2)}) copy-start(s32[10,2]{0,1:T(2,128)} %param.20) | copy-start | bytes 244
  38.0 20.6 %copy-start.3 = (s32[1,8]{1,0:T(1,128)S(1)}, s32[1,8]{1,0:T(1,128)}, u32[]{:S(2)}) copy-start(s32[1,8]{1,0:T(1,128)} %slot_ref.1) | copy-start | bytes 100
  38.0 20.6 %copy-start.4 = (f32[1,64]{1,0:T(1,128)S(1)}, f32[1,64]{1,0:T(1,128)}, u32[]{:S(2)}) copy-start(f32[1,64]{1,0:T(1,128)} %constant.2.clone.freq_hbm.freq_ref) | copy-start | bytes 772
  38.0 26.9 %copy-start = (bf16[4,512,128]{2,1,0:T(8,128)(2,1)S(1)}, bf16[4,512,128]{2,1,0:T(8,128)(2,1)}, u32[]{:S(2)}) copy-start(bf16[4,512,128]{2,1,0:T(8,128)(2,1)} %wv_ref.1) | copy-start | bytes 1572868
  38.0 2.4 %collective-permute-start.10 = (bf16[640,640]{1,0:T(8,128)(2,1)S(1)}, bf16[640,640]{1,0:T(8,128)(2,1)S(1)}, u32[]{:S(2)}, u32[]{:S(2)}) collective-permute-start(bf16[640,640]{1,0:T(8,128)(2,1)S(1)} %get-tuple-element.43), channel_id=1, source_target_pairs={{0,1},{1,0},{2,3},{3,2},{4,5},{5,4},{6,7},{7,6},{8,9},{9,8},{10,11... | collective-permute-start | bytes 2457608 | tf_op jit(solution)/shard_map/ppermute | solution.py:421
  41.7 23.1 %all-to-all-start.1 = ((bf16[64,8,640]{2,1,0:T(8,128)(2,1)}), bf16[64,8,640]{2,1,0:T(8,128)(2,1)S(1)}, u32[]{:S(2)}, u32[]{:S(2)}) async-start(bf16[64,8,640]{2,1,0:T(8,128)(2,1)} %bitcast.6), calls=%async_computation.1 | async-start | bytes 1310720 | tf_op jit(solution)/shard_map/all_to_all | solution.py:418
  49.2 13.8 %collective-permute-start.12 = (bf16[32,640]{1,0:T(8,128)(2,1)S(1)}, bf16[32,640]{1,0:T(8,128)(2,1)S(1)}, u32[]{:S(2)}, u32[]{:S(2)}) collective-permute-start(bf16[32,640]{1,0:T(8,128)(2,1)S(1)} %get-tuple-element.47), channel_id=1, source_target_pairs={{0,14},{1,3},{2,0},{3,5},{4,2},{5,7},{6,4},{7,9},{8,6},{9,11},{10,... | collective-permute-start | bytes 122888 | tf_op jit(solution)/shard_map/ppermute | solution.py:427
  54.4 8.6 %collective-permute-start.13 = (bf16[32,640]{1,0:T(8,128)(2,1)S(1)}, bf16[32,640]{1,0:T(8,128)(2,1)S(1)}, u32[]{:S(2)}, u32[]{:S(2)}) collective-permute-start(bf16[32,640]{1,0:T(8,128)(2,1)S(1)} %get-tuple-element.48), channel_id=1, source_target_pairs={{0,12},{1,5},{2,14},{3,7},{4,0},{5,9},{6,2},{7,11},{8,4},{9,13},{1... | collective-permute-start | bytes 122888 | tf_op jit(solution)/shard_map/ppermute | solution.py:427
  55.3 7.7 %collective-permute-start.14 = (bf16[32,640]{1,0:T(8,128)(2,1)S(1)}, bf16[32,640]{1,0:T(8,128)(2,1)S(1)}, u32[]{:S(2)}, u32[]{:S(2)}) collective-permute-start(bf16[32,640]{1,0:T(8,128)(2,1)S(1)} %get-tuple-element.49), channel_id=1, source_target_pairs={{0,10},{1,7},{2,12},{3,9},{4,14},{5,11},{6,0},{7,13},{8,2},{9,15},... | collective-permute-start | bytes 122888 | tf_op jit(solution)/shard_map/ppermute | solution.py:427
  55.8 7.1 %collective-permute-start.11 = (bf16[16,640]{1,0:T(8,128)(2,1)S(1)}, bf16[16,640]{1,0:T(8,128)(2,1)S(1)}, u32[]{:S(2)}, u32[]{:S(2)}) collective-permute-start(bf16[16,640]{1,0:T(8,128)(2,1)S(1)} %get-tuple-element.46), channel_id=1, source_target_pairs={{0,8},{1,9},{2,10},{3,11},{4,12},{5,13},{6,14},{7,15},{8,0},{9,1},... | collective-permute-start | bytes 61448 | tf_op jit(solution)/shard_map/ppermute | solution.py:427
  63.0 1.3 %collective-permute-start.15 = (bf16[48,640]{1,0:T(8,128)(2,1)S(1)}, bf16[48,640]{1,0:T(8,128)(2,1)S(1)}, u32[]{:S(2)}, u32[]{:S(2)}) collective-permute-start(bf16[48,640]{1,0:T(8,128)(2,1)S(1)} %pad_maximum_fusion), channel_id=1, source_target_pairs={{0,1},{1,0},{2,3},{3,2},{4,5},{5,4},{6,7},{7,6},{8,9},{9,8},{10,11... | collective-permute-start | bytes 184328 | tf_op jit(solution)/shard_map/ppermute | solution.py:421

commit v4 on v3

--- a/solution.py
+++ b/solution.py
@@ -304,37 +304,36 @@
     return summed.astype(BF)
 
 
-def finish_kernel(slots, order_ref, new_ref, own_ref, stat_ref, wv_ref, *refs):
-    out_ref = refs[-1]
+def raised(latent, wv_ref, order):
     heads = wv_ref.shape[0]
-    piece = 2 * heads
-    rows = out_ref.shape[0]
-    resident = rows - slots
-    n = resident * piece
-    copies = new_ref.shape[0] // slots // piece
-    mine = copies // 2 + 1
-    far_ref = refs[mine]
-    parts = [ref[:n, :] for ref in refs[:mine]] + [far_ref[k : k + n, :] for k in range(0, far_ref.shape[0], n)]
-
-    def own_of(at, n):
-        return own_ref[at : at + n, :], stat_ref[at : at + n, :128], stat_ref[at : at + n, 128:]
-
-    half = copies * piece
+    head = iota((latent.shape[0], 1), 0) % (2 * heads) // 2
+    values = [jnp.where(head == h, dot(latent, wv_ref[h]), 0.0).astype(BF) for h in range(heads)]
+    return dot(order, jnp.concatenate(values, 1))
+
+
+def finish_new_kernel(slots, order_ref, new_ref, own_ref, stat_ref, wv_ref, out_ref):
+    piece = 2 * wv_ref.shape[0]
+    half = new_ref.shape[0] // slots
     latent = []
     for p in range(slots):
-        block = new_ref[p * half : (p + 1) * half, :].reshape(copies, piece, WIDE)
-        latent.append(merged(block[..., :LAT], block[..., LAT:], *own_of(p * piece, piece)))
+        block = new_ref[p * half : (p + 1) * half, :].reshape(half // piece, piece, WIDE)
+        span = slice(p * piece, (p + 1) * piece)
+        own = own_ref[span, :], stat_ref[span, :128], stat_ref[span, 128:]
+        latent.append(merged(block[..., :LAT], block[..., LAT:], *own))
+    out_ref[...] = raised(jnp.concatenate(latent, 0), wv_ref, order_ref[:, : slots * piece])
+
+
+def finish_resident_kernel(slots, order_ref, own_ref, stat_ref, wv_ref, new_ref, *refs):
+    *near_refs, far_ref, out_ref = refs
+    rows = out_ref.shape[0]
+    piece = 2 * wv_ref.shape[0]
+    n = (rows - slots) * piece
+    parts = [ref[:n, :] for ref in near_refs] + [far_ref[k : k + n, :] for k in range(0, far_ref.shape[0], n)]
     block = jnp.stack(parts)
-    latent.append(merged(block[..., :LAT], block[..., LAT:], *own_of(slots * piece, resident * piece)))
-    latent = jnp.concatenate(latent, 0)
-    count = rows * piece
-    inner = iota((count, 1), 0) % piece
-    values = []
-    for h in range(heads):
-        one = dot(latent, wv_ref[h])
-        values.append(jnp.where(inner // 2 == h, one, 0.0).astype(BF))
-    values = jnp.concatenate(values, 1)
-    out = dot(order_ref[...], values)
+    span = slice(slots * piece, rows * piece)
+    own = own_ref[span, :], stat_ref[span, :128], stat_ref[span, 128:]
+    latent = merged(block[..., :LAT], block[..., LAT:], *own)
+    out = new_ref[...] + raised(latent, wv_ref, order_ref[:, slots * piece :])
     for r in range(rows):
         out_ref[r] = out[2 * r : 2 * r + 2].astype(BF)
 
@@ -464,14 +463,24 @@
     far = swap(jnp.concatenate([x[resident * piece :] for x in near], 0))
     res_back = [res_here, across, *near, far]
 
+    new_out = pl.pallas_call(
+        functools.partial(finish_new_kernel, slots),
+        out_shape=shape((32, heads * 128), F32),
+        in_specs=[VMEM] * 5,
+        out_specs=VMEM,
+        compiler_params=params(32),
+        cost_estimate=cost(4 * 10**8, 2 * 10**6),
+        name="finish_new",
+    )(order, new_back, own_out, own_stat, w_value_up)
+
     return pl.pallas_call(
-        functools.partial(finish_kernel, slots),
+        functools.partial(finish_resident_kernel, slots),
         out_shape=shape((rows, 2, heads * 128), BF),
         in_specs=[VMEM] * (5 + len(res_back)),
         out_specs=VMEM,
         compiler_params=params(32),
         name="finish",
-    )(order, new_back, own_out, own_stat, w_value_up, *res_back)
+    )(order, own_out, own_stat, w_value_up, new_out, *res_back)
 
 
 def solution(mesh):

time: 67.1 us -> 67 us (level)
    ppermute x8, waiting for transfers between devices: 5.89 us -> 4.65 us  [swap(): return lax.ppermute(x, 'core', [(0, 1), (1, 0)])]
    all_to_all x2, waiting for transfers between devices: 0.74 us -> 1.97 us  [exchange(): lax.all_to_all(x.reshape(n, -1, WIDE), axes, 0, 0, tiled=True)]
    pallas_call x1 -> x2, Pallas kernels: 1.32 us -> 1.78 us  [the longest x1 1.14 us: local(): pl.pallas_call(functools.partial(finish_resident_kernel, slots), out_shap...]
  transfers between devices with their start and end apart: 18 -> 18, of which waited for: 8 -> 7; matrix products, arithmetic and copies ran while one was open for 0% -> 0% of each run, Pallas kernels for 2% -> 3%
where the time goes in v4:
time: 67 us; the launch traced here: 66.7 us
  starting transfers between devices  38.4 us (57%)
  waiting for transfers between devices  14.9 us (22%)
  Pallas kernels  13.2 us (20%)
    all_to_all x2, starting transfers between devices, exchange(): lax.all_to_all(x.reshape(n, -1, WIDE), axes, 0, 0, tiled=True)  18.9 us
    ppermute x8, starting transfers between devices, turned(): return lax.ppermute(x, ('zx', 'core'), pairs)  18 us
    ppermute x8, waiting for transfers between devices, turned(): return lax.ppermute(x, ('zx', 'core'), pairs)  8.24 us
    pallas_call x1, Pallas kernels, local(): pl.pallas_call(functools.partial(attend_kernel, piece), out_shape=(shape(...  5.75 us
    ppermute x8, waiting for transfers between devices, swap(): return lax.ppermute(x, 'core', [(0, 1), (1, 0)])  4.65 us
    pallas_call x1, Pallas kernels, local(): pl.pallas_call(functools.partial(project_kernel, heads, slots, copies), o...  3.34 us
    all_to_all x2, waiting for transfers between devices, exchange(): lax.all_to_all(x.reshape(n, -1, WIDE), axes, 0, 0, tiled=True)  1.97 us
    ppermute x8, starting transfers between devices, swap(): return lax.ppermute(x, 'core', [(0, 1), (1, 0)])  1.41 us
  transfers between devices with their start and end apart: 18, of which 7 were waited for; matrix products, arithmetic and copies ran while one was open for 0% of the time, Pallas kernels for 3%

profile of v4, /device:TPU:0, one launch (start us, length us, event | category | flops | bytes accessed | tf_op | source)
XLA Modules:
  0.0 66.7 jit_solution(15916372336439995195)
XLA Ops:
  0.0 3.3 %project.1 = (bf16[512,640]{1,0:T(8,128)(2,1)}, bf16[16,640]{1,0:T(8,128)(2,1)S(1)}, bf16[80,640]{1,0:T(8,128)(2,1)S(1)}) custom-call(s32[1,8]{1,0:T(1,128)} %slot_ref.1, s32[10]{0:T(128)} %len_hbm.1, s32[2,10]{1,0:T(2,128)} %bitcast.12, bf16[10,2,1536]{2,1,0:T(2,128)(2,1)} %ql_hbm.1, bf16[1536,768]{1,0:T(8,128)(2,1)} %wq_hbm.1, ...), custom_call_target="tpu_custom_call" | custom-call | tf_op jit(solution)/shard_map/project/pallas_call | solution.py:377
  3.3 11.5 %all-to-all-start = ((bf16[64,8,640]{2,1,0:T(8,128)(2,1)}), bf16[64,8,640]{2,1,0:T(8,128)(2,1)S(1)}, u32[]{:S(2)}, u32[]{:S(2)}) async-start(bf16[64,8,640]{2,1,0:T(8,128)(2,1)} %bitcast.4), calls=%async_computation | async-start | bytes 1310720 | tf_op jit(solution)/shard_map/all_to_all | solution.py:417
  14.9 0.1 collective-permute-start.1
  15.0 1.2 %collective-permute-done.1.refs_3_ = bf16[16,640]{1,0:T(8,128)(2,1)S(1)} collective-permute-done((bf16[16,640]{1,0:T(8,128)(2,1)S(1)}, bf16[16,640]{1,0:T(8,128)(2,1)S(1)}, u32[]{:S(2)}, u32[]{:S(2)}) %collective-permute-start.1) | collective-permute-done | bytes 20512 | tf_op jit(solution)/shard_map/ppermute | solution.py:420
  16.1 3.1 %collective-permute-start.2 = (bf16[32,640]{1,0:T(8,128)(2,1)S(1)}, bf16[32,640]{1,0:T(8,128)(2,1)S(1)}, u32[]{:S(2)}, u32[]{:S(2)}) collective-permute-start(bf16[32,640]{1,0:T(8,128)(2,1)S(1)} %constant_dynamic-update-slice_fusion), channel_id=1, source_target_pairs={{0,2},{1,15},{2,4},{3,1},{4,6},{5,3},{6,8},{7,5},{8,10},{9,7},{10,... | collective-permute-start | bytes 122888 | tf_op jit(solution)/shard_map/ppermute | solution.py:426
  19.2 1.5 %collective-permute-start.3 = (bf16[32,640]{1,0:T(8,128)(2,1)S(1)}, bf16[32,640]{1,0:T(8,128)(2,1)S(1)}, u32[]{:S(2)}, u32[]{:S(2)}) collective-permute-start(bf16[32,640]{1,0:T(8,128)(2,1)S(1)} %constant_dynamic-update-slice_fusion), channel_id=1, source_target_pairs={{0,4},{1,13},{2,6},{3,15},{4,8},{5,1},{6,10},{7,3},{8,12},{9,5},{1... | collective-permute-start | bytes 122888 | tf_op jit(solution)/shard_map/ppermute | solution.py:426
  20.7 2.1 %collective-permute-start.4 = (bf16[32,640]{1,0:T(8,128)(2,1)S(1)}, bf16[32,640]{1,0:T(8,128)(2,1)S(1)}, u32[]{:S(2)}, u32[]{:S(2)}) collective-permute-start(bf16[32,640]{1,0:T(8,128)(2,1)S(1)} %constant_dynamic-update-slice_fusion), channel_id=1, source_target_pairs={{0,6},{1,11},{2,8},{3,13},{4,10},{5,15},{6,12},{7,1},{8,14},{9,3},... | collective-permute-start | bytes 122888 | tf_op jit(solution)/shard_map/ppermute | solution.py:426
  22.8 2.1 %collective-permute-start = (bf16[16,640]{1,0:T(8,128)(2,1)S(1)}, bf16[16,640]{1,0:T(8,128)(2,1)S(1)}, u32[]{:S(2)}, u32[]{:S(2)}) collective-permute-start(bf16[16,640]{1,0:T(8,128)(2,1)S(1)} %get-tuple-element.37.refs_8_), channel_id=1, source_target_pairs={{0,8},{1,9},{2,10},{3,11},{4,12},{5,13},{6,14},{7,15},{8,0},{9,1},... | collective-permute-start | bytes 61448 | tf_op jit(solution)/shard_map/ppermute | solution.py:426
  24.8 4.8 %collective-permute-done.refs_9_ = bf16[16,640]{1,0:T(8,128)(2,1)S(1)} collective-permute-done((bf16[16,640]{1,0:T(8,128)(2,1)S(1)}, bf16[16,640]{1,0:T(8,128)(2,1)S(1)}, u32[]{:S(2)}, u32[]{:S(2)}) %collective-permute-start) | collective-permute-done | bytes 20512 | tf_op jit(solution)/shard_map/ppermute | solution.py:426
  29.6 0.2 all-to-all-done
  29.9 0.5 collective-permute-start.6
  30.4 0.5 collective-permute-start.8
  30.9 1.3 %collective-permute-done.9.refs_4_ = bf16[16,640]{1,0:T(8,128)(2,1)S(1)} collective-permute-done((bf16[16,640]{1,0:T(8,128)(2,1)S(1)}, bf16[16,640]{1,0:T(8,128)(2,1)S(1)}, u32[]{:S(2)}, u32[]{:S(2)}) %collective-permute-start.9) | collective-permute-done | bytes 20512 | tf_op jit(solution)/shard_map/ppermute | solution.py:420
  32.2 5.7 %attend.1 = (bf16[640,640]{1,0:T(8,128)(2,1)S(1)}, f32[640,512]{1,0:T(8,128)S(1)}, bf16[640,128]{1,0:T(8,128)(2,1)S(1)}) custom-call(bf16[8,576,768]{2,1,0:T(8,128)(2,1)} %bitcast.15, bf16[2,576,768]{2,1,0:T(8,128)(2,1)S(1)} %bitcast.14, bf16[512,640]{1,0:T(8,128)(2,1)S(1)} %bitcast.11, bf16[512,640]{1,0:T(8,128)(2,1)S(1)} %collective-permute-done.5.new_other, ...), custom_call_target="tpu_custom_call" | custom-call | flops 5000000000 | bytes 20000000 | tf_op jit(solution)/shard_map/attend/pallas_call | solution.py:436
  38.0 0.0 copy-start.1
  38.0 0.0 copy-start.2
  38.0 0.0 copy-start.4
  38.0 0.0 copy-start
  38.0 0.2 collective-permute-start.10
  38.3 2.2 %collective-permute-done.10.got_ref = bf16[640,640]{1,0:T(8,128)(2,1)S(1)} collective-permute-done((bf16[640,640]{1,0:T(8,128)(2,1)S(1)}, bf16[640,640]{1,0:T(8,128)(2,1)S(1)}, u32[]{:S(2)}, u32[]{:S(2)}) %collective-permute-start.10) | collective-permute-done | bytes 819232 | tf_op jit(solution)/shard_map/ppermute | solution.py:420
  40.5 1.3 %join_cores.1 = (bf16[512,640]{1,0:T(8,128)(2,1)}, bf16[32,640]{1,0:T(8,128)(2,1)S(1)}, bf16[32,640]{1,0:T(8,128)(2,1)S(1)}, bf16[32,640]{1,0:T(8,128)(2,1)S(1)}...) custom-call(bf16[640,640]{1,0:T(8,128)(2,1)S(1)} %collective-permute-done.10.got_ref, ...), custom_call_target="tpu_custom_call" | custom-call | tf_op jit(solution)/shard_map/join_cores/pallas_call | solution.py:447
  41.8 7.4 %all-to-all-start.1 = ((bf16[64,8,640]{2,1,0:T(8,128)(2,1)}), bf16[64,8,640]{2,1,0:T(8,128)(2,1)S(1)}, u32[]{:S(2)}, u32[]{:S(2)}) async-start(bf16[64,8,640]{2,1,0:T(8,128)(2,1)} %bitcast.6), calls=%async_computation.1 | async-start | bytes 1310720 | tf_op jit(solution)/shard_map/all_to_all | solution.py:417
  49.2 5.3 %collective-permute-start.12 = (bf16[32,640]{1,0:T(8,128)(2,1)S(1)}, bf16[32,640]{1,0:T(8,128)(2,1)S(1)}, u32[]{:S(2)}, u32[]{:S(2)}) collective-permute-start(bf16[32,640]{1,0:T(8,128)(2,1)S(1)} %get-tuple-element.47), channel_id=1, source_target_pairs={{0,14},{1,3},{2,0},{3,5},{4,2},{5,7},{6,4},{7,9},{8,6},{9,11},{10,... | collective-permute-start | bytes 122888 | tf_op jit(solution)/shard_map/ppermute | solution.py:426
  54.5 0.9 %collective-permute-start.13 = (bf16[32,640]{1,0:T(8,128)(2,1)S(1)}, bf16[32,640]{1,0:T(8,128)(2,1)S(1)}, u32[]{:S(2)}, u32[]{:S(2)}) collective-permute-start(bf16[32,640]{1,0:T(8,128)(2,1)S(1)} %get-tuple-element.48), channel_id=1, source_target_pairs={{0,12},{1,5},{2,14},{3,7},{4,0},{5,9},{6,2},{7,11},{8,4},{9,13},{1... | collective-permute-start | bytes 122888 | tf_op jit(solution)/shard_map/ppermute | solution.py:426
  55.3 0.6 collective-permute-start.14
  55.9 2.7 %collective-permute-start.11 = (bf16[16,640]{1,0:T(8,128)(2,1)S(1)}, bf16[16,640]{1,0:T(8,128)(2,1)S(1)}, u32[]{:S(2)}, u32[]{:S(2)}) collective-permute-start(bf16[16,640]{1,0:T(8,128)(2,1)S(1)} %get-tuple-element.46), channel_id=1, source_target_pairs={{0,8},{1,9},{2,10},{3,11},{4,12},{5,13},{6,14},{7,15},{8,0},{9,1},... | collective-permute-start | bytes 61448 | tf_op jit(solution)/shard_map/ppermute | solution.py:426
  58.6 1.0 %own_keys.1 = (f32[80,512]{1,0:T(8,128)S(1)}, f32[80,256]{1,0:T(8,128)S(1)}, bf16[32,80]{1,0:T(8,128)(2,1)S(1)}) custom-call(s32[1,8]{1,0:T(1,128)S(1)} %copy-done.3, s32[2,10]{1,0:T(2,128)S(1)} %bitcast.13, bf16[10,2,576]{2,1,0:T(2,128)(2,1)S(1)} %copy-done.1, f32[1,64]{1,0:T(1,128)S(1)} %copy-done.4, bf16[80,640]{1,0:T(8,128)(2,1)S(1)} %get-tuple-element.32.own_ref), custom_call_target="tpu_custom_call" | custom-call | tf_op jit(solution)/shard_map/own_keys/pallas_call | solution.py:402
  59.6 3.4 %collective-permute-done.11.refs_1_ = bf16[16,640]{1,0:T(8,128)(2,1)S(1)} collective-permute-done((bf16[16,640]{1,0:T(8,128)(2,1)S(1)}, bf16[16,640]{1,0:T(8,128)(2,1)S(1)}, u32[]{:S(2)}, u32[]{:S(2)}) %collective-permute-start.11) | collective-permute-done | bytes 20512 | tf_op jit(solution)/shard_map/ppermute | solution.py:426
  63.1 0.1 collective-permute-start.15
  63.2 1.7 %all-to-all-done.1 = bf16[64,8,640]{2,1,0:T(8,128)(2,1)S(1)} async-done(((bf16[64,8,640]{2,1,0:T(8,128)(2,1)}), bf16[64,8,640]{2,1,0:T(8,128)(2,1)S(1)}, u32[]{:S(2)}, u32[]{:S(2)}) %all-to-all-start.1) | async-done | bytes 655392 | tf_op jit(solution)/shard_map/all_to_all | solution.py:417
  64.9 0.6 finish_new.1.new_ref
  65.6 1.1 %finish.1 = bf16[10,2,512]{2,1,0:T(2,128)(2,1)} custom-call(bf16[32,80]{1,0:T(8,128)(2,1)S(1)} %get-tuple-element.50.order_ref, f32[80,512]{1,0:T(8,128)S(1)} %get-tuple-element.51.own_ref, f32[80,256]{1,0:T(8,128)S(1)} %get-tuple-element.52.stat_ref, bf16[4,512,128]{2,1,0:T(8,128)(2,1)S(1)} %copy-done, f32[32,512]{1,0:T(8,128)S(1)} %finish_new.1.new_ref, ...), custom_call_target="tpu_custom_call" | custom-call | tf_op jit(solution)/shard_map/finish/pallas_call | solution.py:476
  (28 shorter events, 0.1 us)
Async XLA Ops:
  0.0 32.2 %copy-start.5 = (bf16[2,768,576]{1,2,0:T(8,128)(2,1)S(1)}, bf16[2,768,576]{1,2,0:T(8,128)(2,1)}, u32[]{:S(2)}) copy-start(bf16[2,768,576]{1,2,0:T(8,128)(2,1)} %param.15) | copy-start | bytes 5308420
  3.3 26.5 %all-to-all-start = ((bf16[64,8,640]{2,1,0:T(8,128)(2,1)}), bf16[64,8,640]{2,1,0:T(8,128)(2,1)S(1)}, u32[]{:S(2)}, u32[]{:S(2)}) async-start(bf16[64,8,640]{2,1,0:T(8,128)(2,1)} %bitcast.4), calls=%async_computation | async-start | bytes 1310720 | tf_op jit(solution)/shard_map/all_to_all | solution.py:417
  14.9 1.3 %collective-permute-start.1 = (bf16[16,640]{1,0:T(8,128)(2,1)S(1)}, bf16[16,640]{1,0:T(8,128)(2,1)S(1)}, u32[]{:S(2)}, u32[]{:S(2)}) collective-permute-start(bf16[16,640]{1,0:T(8,128)(2,1)S(1)} %get-tuple-element.37.refs_8_), channel_id=1, source_target_pairs={{0,1},{1,0},{2,3},{3,2},{4,5},{5,4},{6,7},{7,6},{8,9},{9,8},{10,11... | collective-permute-start | bytes 61448 | tf_op jit(solution)/shard_map/ppermute | solution.py:420
  16.1 13.5 %collective-permute-start.2 = (bf16[32,640]{1,0:T(8,128)(2,1)S(1)}, bf16[32,640]{1,0:T(8,128)(2,1)S(1)}, u32[]{:S(2)}, u32[]{:S(2)}) collective-permute-start(bf16[32,640]{1,0:T(8,128)(2,1)S(1)} %constant_dynamic-update-slice_fusion), channel_id=1, source_target_pairs={{0,2},{1,15},{2,4},{3,1},{4,6},{5,3},{6,8},{7,5},{8,10},{9,7},{10,... | collective-permute-start | bytes 122888 | tf_op jit(solution)/shard_map/ppermute | solution.py:426
  19.2 10.4 %collective-permute-start.3 = (bf16[32,640]{1,0:T(8,128)(2,1)S(1)}, bf16[32,640]{1,0:T(8,128)(2,1)S(1)}, u32[]{:S(2)}, u32[]{:S(2)}) collective-permute-start(bf16[32,640]{1,0:T(8,128)(2,1)S(1)} %constant_dynamic-update-slice_fusion), channel_id=1, source_target_pairs={{0,4},{1,13},{2,6},{3,15},{4,8},{5,1},{6,10},{7,3},{8,12},{9,5},{1... | collective-permute-start | bytes 122888 | tf_op jit(solution)/shard_map/ppermute | solution.py:426
  20.7 9.0 %collective-permute-start.4 = (bf16[32,640]{1,0:T(8,128)(2,1)S(1)}, bf16[32,640]{1,0:T(8,128)(2,1)S(1)}, u32[]{:S(2)}, u32[]{:S(2)}) collective-permute-start(bf16[32,640]{1,0:T(8,128)(2,1)S(1)} %constant_dynamic-update-slice_fusion), channel_id=1, source_target_pairs={{0,6},{1,11},{2,8},{3,13},{4,10},{5,15},{6,12},{7,1},{8,14},{9,3},... | collective-permute-start | bytes 122888 | tf_op jit(solution)/shard_map/ppermute | solution.py:426
  22.8 6.9 %collective-permute-start = (bf16[16,640]{1,0:T(8,128)(2,1)S(1)}, bf16[16,640]{1,0:T(8,128)(2,1)S(1)}, u32[]{:S(2)}, u32[]{:S(2)}) collective-permute-start(bf16[16,640]{1,0:T(8,128)(2,1)S(1)} %get-tuple-element.37.refs_8_), channel_id=1, source_target_pairs={{0,8},{1,9},{2,10},{3,11},{4,12},{5,13},{6,14},{7,15},{8,0},{9,1},... | collective-permute-start | bytes 61448 | tf_op jit(solution)/shard_map/ppermute | solution.py:426
  29.9 2.3 %collective-permute-start.5 = (bf16[512,640]{1,0:T(8,128)(2,1)S(1)}, bf16[512,640]{1,0:T(8,128)(2,1)S(1)}, u32[]{:S(2)}, u32[]{:S(2)}) collective-permute-start(bf16[512,640]{1,0:T(8,128)(2,1)S(1)} %bitcast.10), channel_id=1, source_target_pairs={{0,1},{1,0},{2,3},{3,2},{4,5},{5,4},{6,7},{7,6},{8,9},{9,8},{10,11... | collective-permute-start | bytes 1966088 | tf_op jit(solution)/shard_map/ppermute | solution.py:420
  29.9 2.3 %collective-permute-start.6 = (bf16[32,640]{1,0:T(8,128)(2,1)S(1)}, bf16[32,640]{1,0:T(8,128)(2,1)S(1)}, u32[]{:S(2)}, u32[]{:S(2)}) collective-permute-start(bf16[32,640]{1,0:T(8,128)(2,1)S(1)} %collective-permute-done.2.refs_5_), channel_id=1, source_target_pairs={{0,1},{1,0},{2,3},{3,2},{4,5},{5,4},{6,7},{7,6},{8,9},{9,8},{10,11... | collective-permute-start | bytes 122888 | tf_op jit(solution)/shard_map/ppermute | solution.py:420
  30.4 1.8 %collective-permute-start.7 = (bf16[32,640]{1,0:T(8,128)(2,1)S(1)}, bf16[32,640]{1,0:T(8,128)(2,1)S(1)}, u32[]{:S(2)}, u32[]{:S(2)}) collective-permute-start(bf16[32,640]{1,0:T(8,128)(2,1)S(1)} %collective-permute-done.3.refs_6_), channel_id=1, source_target_pairs={{0,1},{1,0},{2,3},{3,2},{4,5},{5,4},{6,7},{7,6},{8,9},{9,8},{10,11... | collective-permute-start | bytes 122888 | tf_op jit(solution)/shard_map/ppermute | solution.py:420
  30.4 1.8 %collective-permute-start.8 = (bf16[32,640]{1,0:T(8,128)(2,1)S(1)}, bf16[32,640]{1,0:T(8,128)(2,1)S(1)}, u32[]{:S(2)}, u32[]{:S(2)}) collective-permute-start(bf16[32,640]{1,0:T(8,128)(2,1)S(1)} %collective-permute-done.4.refs_7_), channel_id=1, source_target_pairs={{0,1},{1,0},{2,3},{3,2},{4,5},{5,4},{6,7},{7,6},{8,9},{9,8},{10,11... | collective-permute-start | bytes 122888 | tf_op jit(solution)/shard_map/ppermute | solution.py:420
  30.9 1.3 %collective-permute-start.9 = (bf16[16,640]{1,0:T(8,128)(2,1)S(1)}, bf16[16,640]{1,0:T(8,128)(2,1)S(1)}, u32[]{:S(2)}, u32[]{:S(2)}) collective-permute-start(bf16[16,640]{1,0:T(8,128)(2,1)S(1)} %collective-permute-done.refs_9_), channel_id=1, source_target_pairs={{0,1},{1,0},{2,3},{3,2},{4,5},{5,4},{6,7},{7,6},{8,9},{9,8},{10,11... | collective-permute-start | bytes 61448 | tf_op jit(solution)/shard_map/ppermute | solution.py:420
  38.0 20.6 %copy-start.1 = (bf16[10,2,576]{2,1,0:T(2,128)(2,1)S(1)}, bf16[10,2,576]{2,1,0:T(2,128)(2,1)}, u32[]{:S(2)}) copy-start(bf16[10,2,576]{2,1,0:T(2,128)(2,1)} %nl_ref.1) | copy-start | bytes 69124
  38.0 20.6 %copy-start.2 = (s32[10,2]{0,1:T(2,128)S(1)}, s32[10,2]{0,1:T(2,128)}, u32[]{:S(2)}) copy-start(s32[10,2]{0,1:T(2,128)} %param.20) | copy-start | bytes 244
  38.0 20.6 %copy-start.3 = (s32[1,8]{1,0:T(1,128)S(1)}, s32[1,8]{1,0:T(1,128)}, u32[]{:S(2)}) copy-start(s32[1,8]{1,0:T(1,128)} %slot_ref.1) | copy-start | bytes 100
  38.0 20.6 %copy-start.4 = (f32[1,64]{1,0:T(1,128)S(1)}, f32[1,64]{1,0:T(1,128)}, u32[]{:S(2)}) copy-start(f32[1,64]{1,0:T(1,128)} %constant.2.clone.freq_hbm.freq_ref) | copy-start | bytes 772
  38.0 26.9 %copy-start = (bf16[4,512,128]{2,1,0:T(8,128)(2,1)S(1)}, bf16[4,512,128]{2,1,0:T(8,128)(2,1)}, u32[]{:S(2)}) copy-start(bf16[4,512,128]{2,1,0:T(8,128)(2,1)} %wv_ref.3) | copy-start | bytes 1572868
  38.0 2.4 %collective-permute-start.10 = (bf16[640,640]{1,0:T(8,128)(2,1)S(1)}, bf16[640,640]{1,0:T(8,128)(2,1)S(1)}, u32[]{:S(2)}, u32[]{:S(2)}) collective-permute-start(bf16[640,640]{1,0:T(8,128)(2,1)S(1)} %get-tuple-element.43), channel_id=1, source_target_pairs={{0,1},{1,0},{2,3},{3,2},{4,5},{5,4},{6,7},{7,6},{8,9},{9,8},{10,11... | collective-permute-start | bytes 2457608 | tf_op jit(solution)/shard_map/ppermute | solution.py:420
  41.8 23.1 %all-to-all-start.1 = ((bf16[64,8,640]{2,1,0:T(8,128)(2,1)}), bf16[64,8,640]{2,1,0:T(8,128)(2,1)S(1)}, u32[]{:S(2)}, u32[]{:S(2)}) async-start(bf16[64,8,640]{2,1,0:T(8,128)(2,1)} %bitcast.6), calls=%async_computation.1 | async-start | bytes 1310720 | tf_op jit(solution)/shard_map/all_to_all | solution.py:417
  49.2 13.8 %collective-permute-start.12 = (bf16[32,640]{1,0:T(8,128)(2,1)S(1)}, bf16[32,640]{1,0:T(8,128)(2,1)S(1)}, u32[]{:S(2)}, u32[]{:S(2)}) collective-permute-start(bf16[32,640]{1,0:T(8,128)(2,1)S(1)} %get-tuple-element.47), channel_id=1, source_target_pairs={{0,14},{1,3},{2,0},{3,5},{4,2},{5,7},{6,4},{7,9},{8,6},{9,11},{10,... | collective-permute-start | bytes 122888 | tf_op jit(solution)/shard_map/ppermute | solution.py:426
  54.5 8.6 %collective-permute-start.13 = (bf16[32,640]{1,0:T(8,128)(2,1)S(1)}, bf16[32,640]{1,0:T(8,128)(2,1)S(1)}, u32[]{:S(2)}, u32[]{:S(2)}) collective-permute-start(bf16[32,640]{1,0:T(8,128)(2,1)S(1)} %get-tuple-element.48), channel_id=1, source_target_pairs={{0,12},{1,5},{2,14},{3,7},{4,0},{5,9},{6,2},{7,11},{8,4},{9,13},{1... | collective-permute-start | bytes 122888 | tf_op jit(solution)/shard_map/ppermute | solution.py:426
  55.3 7.7 %collective-permute-start.14 = (bf16[32,640]{1,0:T(8,128)(2,1)S(1)}, bf16[32,640]{1,0:T(8,128)(2,1)S(1)}, u32[]{:S(2)}, u32[]{:S(2)}) collective-permute-start(bf16[32,640]{1,0:T(8,128)(2,1)S(1)} %get-tuple-element.49), channel_id=1, source_target_pairs={{0,10},{1,7},{2,12},{3,9},{4,14},{5,11},{6,0},{7,13},{8,2},{9,15},... | collective-permute-start | bytes 122888 | tf_op jit(solution)/shard_map/ppermute | solution.py:426
  55.9 7.1 %collective-permute-start.11 = (bf16[16,640]{1,0:T(8,128)(2,1)S(1)}, bf16[16,640]{1,0:T(8,128)(2,1)S(1)}, u32[]{:S(2)}, u32[]{:S(2)}) collective-permute-start(bf16[16,640]{1,0:T(8,128)(2,1)S(1)} %get-tuple-element.46), channel_id=1, source_target_pairs={{0,8},{1,9},{2,10},{3,11},{4,12},{5,13},{6,14},{7,15},{8,0},{9,1},... | collective-permute-start | bytes 61448 | tf_op jit(solution)/shard_map/ppermute | solution.py:426
  63.1 2.5 %collective-permute-start.15 = (bf16[48,640]{1,0:T(8,128)(2,1)S(1)}, bf16[48,640]{1,0:T(8,128)(2,1)S(1)}, u32[]{:S(2)}, u32[]{:S(2)}) collective-permute-start(bf16[48,640]{1,0:T(8,128)(2,1)S(1)} %pad_maximum_fusion), channel_id=1, source_target_pairs={{0,1},{1,0},{2,3},{3,2},{4,5},{5,4},{6,7},{7,6},{8,9},{9,8},{10,11... | collective-permute-start | bytes 184328 | tf_op jit(solution)/shard_map/ppermute | solution.py:420

commit v5 on v4

--- a/solution.py
+++ b/solution.py
@@ -196,14 +196,21 @@
     return highest * SCALE, jnp.sum(weights, 1, keepdims=True), weights.astype(BF)
 
 
-def attend_kernel(piece, fresh_hbm, cache_ref, new_own, new_other, *refs):
+def fetch_kernel(after_hbm, fresh_hbm, keys_ref, sem):
+    load = pltpu.make_async_copy(fresh_hbm.at[pl.ds(0, keys_ref.shape[0])], keys_ref, sem)
+    load.start()
+    load.wait()
+
+
+def attend_kernel(piece, fresh_hbm, first_ref, cache_ref, new_own, new_other, *refs):
     send_ref, keep_ref, stat_ref, keys_ref, sems = refs[-5:]
     blocks = refs[:-5]
-    res_other, res_own = blocks[: len(blocks) // 2], blocks[len(blocks) // 2 :]
+    res_other, res_own = blocks[:2], blocks[2:]
     slots, resident = fresh_hbm.shape[0], cache_ref.shape[0]
     rows = slots + resident
     half = new_own.shape[0] // slots
-    loads = [pltpu.make_async_copy(fresh_hbm.at[i], keys_ref.at[i], sems.at[i]) for i in range(slots)]
+    here = first_ref.shape[0]
+    loads = [pltpu.make_async_copy(fresh_hbm.at[here + i], keys_ref.at[i], sems.at[i]) for i in range(slots - here)]
     for load in loads:
         load.start()
     offset = (lax.axis_index("zx") * lax.axis_size("core") + lax.axis_index("core")) * keys_ref.shape[2]
@@ -219,7 +226,9 @@
         )
 
     def keys_of(i):
-        return keys_ref.at[i] if i < slots else cache_ref.at[i - slots]
+        if i < here:
+            return first_ref.at[i]
+        return keys_ref.at[i - here] if i < slots else cache_ref.at[i - slots]
 
     def scores_of(i):
         queries = queries_of(i)
@@ -228,14 +237,14 @@
         return dot(queries[:, : LAT + ROPE], keys_of(i)[...]), length
 
     order = [*range(slots, rows), *range(slots)]
-    arrived = 0
+    arrived = here
     ahead = scores_of(order[0])
     for n, i in enumerate(order):
         scores, length = ahead
         if n + 1 < rows:
             if order[n + 1] == arrived:
                 upto = min(slots, arrived + n + 1)
-                for load in loads[arrived:upto]:
+                for load in loads[arrived - here : upto - here]:
                     load.wait()
                 arrived = upto
             ahead = scores_of(order[n + 1])
@@ -371,6 +380,9 @@
     cache = jnp.swapaxes(cache, 1, 2)
     fresh = jnp.swapaxes(fresh[0], 1, 2)
 
+    def in_vmem(x):
+        return pltpu.with_memory_space_constraint(x, pltpu.VMEM)
+
     def in_hbm(x):
         return pltpu.with_memory_space_constraint(x, pltpu.HBM)
 
@@ -428,21 +440,37 @@
     new_own = exchange(out_q, ("group", "zx"), slots * copies)
     res_sib = swap(res_q)
     res_both = jnp.concatenate([res_q, res_sib], 0)
-    near = [turned(res_both, k, 1) for k in range(1, copies // 2)]
+    turns = sorted(range(1, copies // 2), key=lambda k: (k + 1) % 2 * copies - k)
+    near = [turned(res_both, k, 1) for k in turns]
     across = turned(res_q, copies // 2, 1)
     new_own, across, *near = lax.optimization_barrier((new_own, across, *near))
-    new_other, across_sib, *far = map(swap, (new_own, across, *near))
+    new_other = swap(new_own)
+    far = swap(jnp.concatenate([*near, across], 0))
+    first = 2
+    first_keys = pl.pallas_call(
+        fetch_kernel,
+        out_shape=pltpu.VMEM((first, *fresh.shape[1:]), BF),
+        in_specs=[ANY] * 2,
+        out_specs=ANY,
+        scratch_shapes=[pltpu.SemaphoreType.DMA],
+        compiler_params=params(2),
+        cost_estimate=cost(0, 4 * first * fresh[0].size),
+        name="fetch_keys",
+    )(new_own, in_hbm(fresh))
 
     send, keep, stat = pl.pallas_call(
         functools.partial(attend_kernel, piece),
         out_shape=(shape((rows * half, WIDE), BF), shape((rows * half, LAT), F32), shape((rows * half, 128), BF)),
-        in_specs=[ANY] + [VMEM] * (5 + copies),
+        in_specs=[ANY] + [VMEM] * (8 + len(near)),
         out_specs=[VMEM] * 3,
-        scratch_shapes=[pltpu.VMEM((slots, LAT + ROPE, tokens), BF), pltpu.SemaphoreType.DMA((slots,))],
+        scratch_shapes=[
+            pltpu.VMEM((slots - first, LAT + ROPE, tokens), BF),
+            pltpu.SemaphoreType.DMA((slots - first,)),
+        ],
         compiler_params=params(24),
         cost_estimate=cost(rows * 5 * 10**8, rows * 2 * 10**6),
         name="attend",
-    )(in_hbm(fresh), pltpu.with_memory_space_constraint(cache, pltpu.VMEM), new_own, new_other, *far, res_sib, across_sib, *near, res_q, across)
+    )(in_hbm(fresh), in_vmem(first_keys), in_vmem(cache), new_own, new_other, far, res_sib, *near, across, res_q)
 
     new_part, *res_parts = pl.pallas_call(
         functools.partial(join_kernel, slots, piece),
@@ -456,8 +484,8 @@
         name="join_cores",
     )(swap(send), keep, stat)
     new_back = exchange(new_part, ("group", "zx"), slots * copies)
-    *near, res_here, across = res_parts
-    near = [turned(x, k + 1, -1) for k, x in enumerate(near)]
+    *near, across, res_here = res_parts
+    near = [turned(x, k, -1) for k, x in zip(turns, near)]
     across = turned(across, copies // 2, -1)
     own_out, own_stat, order, across, *near = lax.optimization_barrier((own_out, own_stat, order, across, *near))
     far = swap(jnp.concatenate([x[resident * piece :] for x in near], 0))

time: 67 us -> 66.6 us (level)
  Pallas kernels: 13.2 us -> 14.2 us
  starting transfers between devices: 38.4 us -> 37.4 us
  waiting for transfers between devices: 14.9 us -> 14.2 us
    pallas_call x0 -> x1, Pallas kernels: none -> 1.61 us  [local(): pl.pallas_call(fetch_kernel, out_shape=pltpu.VMEM((first, *fresh.shape[1:...]
    ppermute x8 -> x5, waiting for transfers between devices: 4.65 us -> 3.55 us  [swap(): return lax.ppermute(x, 'core', [(0, 1), (1, 0)])]
    ppermute x8 -> x5, starting transfers between devices: 1.41 us -> 0.86 us  [swap(): return lax.ppermute(x, 'core', [(0, 1), (1, 0)])]
  transfers between devices with their start and end apart: 18 -> 15, of which waited for: 7 -> 10; matrix products, arithmetic and copies ran while one was open for 0% -> 0% of each run, Pallas kernels for 3% -> 5%
where the time goes in v5:
time: 66.6 us; the launch traced here: 66.3 us
  starting transfers between devices  37.4 us (56%)
  Pallas kernels  14.2 us (21%)
  waiting for transfers between devices  14.2 us (21%)
    all_to_all x2, starting transfers between devices, exchange(): lax.all_to_all(x.reshape(n, -1, WIDE), axes, 0, 0, tiled=True)  18.5 us
    ppermute x8, starting transfers between devices, turned(): return lax.ppermute(x, ('zx', 'core'), pairs)  18 us
    ppermute x8, waiting for transfers between devices, turned(): return lax.ppermute(x, ('zx', 'core'), pairs)  8.28 us
    pallas_call x1, Pallas kernels, local(): pl.pallas_call(functools.partial(attend_kernel, piece), out_shape=(shape(...  5.23 us
    ppermute x5, waiting for transfers between devices, swap(): return lax.ppermute(x, 'core', [(0, 1), (1, 0)])  3.55 us
    pallas_call x1, Pallas kernels, local(): pl.pallas_call(functools.partial(project_kernel, heads, slots, copies), o...  3.23 us
    all_to_all x2, waiting for transfers between devices, exchange(): lax.all_to_all(x.reshape(n, -1, WIDE), axes, 0, 0, tiled=True)  2.37 us
    pallas_call x1, Pallas kernels, local(): pl.pallas_call(fetch_kernel, out_shape=pltpu.VMEM((first, *fresh.shape[1:...  1.61 us
  transfers between devices with their start and end apart: 15, of which 10 were waited for; matrix products, arithmetic and copies ran while one was open for 0% of the time, Pallas kernels for 5%

profile of v5, /device:TPU:0, one launch (start us, length us, event | category | flops | bytes accessed | tf_op | source)
XLA Modules:
  0.0 66.3 jit_solution(18256224317912741313)
XLA Ops:
  0.0 3.2 %project.1 = (bf16[512,640]{1,0:T(8,128)(2,1)}, bf16[16,640]{1,0:T(8,128)(2,1)S(1)}, bf16[80,640]{1,0:T(8,128)(2,1)S(1)}) custom-call(s32[1,8]{1,0:T(1,128)} %slot_ref.1, s32[10]{0:T(128)} %len_hbm.1, s32[2,10]{1,0:T(2,128)} %bitcast.13, bf16[10,2,1536]{2,1,0:T(2,128)(2,1)} %ql_hbm.1, bf16[1536,768]{1,0:T(8,128)(2,1)} %wq_hbm.1, ...), custom_call_target="tpu_custom_call" | custom-call | tf_op jit(solution)/shard_map/project/pallas_call | solution.py:389
  3.2 11.5 %all-to-all-start = ((bf16[64,8,640]{2,1,0:T(8,128)(2,1)}), bf16[64,8,640]{2,1,0:T(8,128)(2,1)S(1)}, u32[]{:S(2)}, u32[]{:S(2)}) async-start(bf16[64,8,640]{2,1,0:T(8,128)(2,1)} %bitcast.3), calls=%async_computation | async-start | bytes 1310720 | tf_op jit(solution)/shard_map/all_to_all | solution.py:429
  14.8 0.1 collective-permute-start.1
  14.9 1.2 %collective-permute-done.1.refs_1_ = bf16[16,640]{1,0:T(8,128)(2,1)S(1)} collective-permute-done((bf16[16,640]{1,0:T(8,128)(2,1)S(1)}, bf16[16,640]{1,0:T(8,128)(2,1)S(1)}, u32[]{:S(2)}, u32[]{:S(2)}) %collective-permute-start.1) | collective-permute-done | bytes 20512 | tf_op jit(solution)/shard_map/ppermute | solution.py:432
  16.0 4.0 %collective-permute-start.2 = (bf16[32,640]{1,0:T(8,128)(2,1)S(1)}, bf16[32,640]{1,0:T(8,128)(2,1)S(1)}, u32[]{:S(2)}, u32[]{:S(2)}) collective-permute-start(bf16[32,640]{1,0:T(8,128)(2,1)S(1)} %constant_dynamic-update-slice_fusion), channel_id=1, source_target_pairs={{0,6},{1,11},{2,8},{3,13},{4,10},{5,15},{6,12},{7,1},{8,14},{9,3},... | collective-permute-start | bytes 122888 | tf_op jit(solution)/shard_map/ppermute | solution.py:438
  20.0 2.1 %collective-permute-start.3 = (bf16[32,640]{1,0:T(8,128)(2,1)S(1)}, bf16[32,640]{1,0:T(8,128)(2,1)S(1)}, u32[]{:S(2)}, u32[]{:S(2)}) collective-permute-start(bf16[32,640]{1,0:T(8,128)(2,1)S(1)} %constant_dynamic-update-slice_fusion), channel_id=1, source_target_pairs={{0,2},{1,15},{2,4},{3,1},{4,6},{5,3},{6,8},{7,5},{8,10},{9,7},{10,... | collective-permute-start | bytes 122888 | tf_op jit(solution)/shard_map/ppermute | solution.py:438
  22.1 0.6 collective-permute-start.4
  22.6 2.1 %collective-permute-start = (bf16[16,640]{1,0:T(8,128)(2,1)S(1)}, bf16[16,640]{1,0:T(8,128)(2,1)S(1)}, u32[]{:S(2)}, u32[]{:S(2)}) collective-permute-start(bf16[16,640]{1,0:T(8,128)(2,1)S(1)} %get-tuple-element.37.refs_6_), channel_id=1, source_target_pairs={{0,8},{1,9},{2,10},{3,11},{4,12},{5,13},{6,14},{7,15},{8,0},{9,1},... | collective-permute-start | bytes 61448 | tf_op jit(solution)/shard_map/ppermute | solution.py:438
  24.7 3.4 %collective-permute-done.refs_5_ = bf16[16,640]{1,0:T(8,128)(2,1)S(1)} collective-permute-done((bf16[16,640]{1,0:T(8,128)(2,1)S(1)}, bf16[16,640]{1,0:T(8,128)(2,1)S(1)}, u32[]{:S(2)}, u32[]{:S(2)}) %collective-permute-start) | collective-permute-done | bytes 20512 | tf_op jit(solution)/shard_map/ppermute | solution.py:438
  28.1 0.8 %collective-permute-done.2.refs_2_ = bf16[32,640]{1,0:T(8,128)(2,1)S(1)} collective-permute-done((bf16[32,640]{1,0:T(8,128)(2,1)S(1)}, bf16[32,640]{1,0:T(8,128)(2,1)S(1)}, u32[]{:S(2)}, u32[]{:S(2)}) %collective-permute-start.2) | collective-permute-done | bytes 40992 | tf_op jit(solution)/shard_map/ppermute | solution.py:438
  28.9 0.2 collective-permute-done.3.refs_3_
  29.1 0.5 collective-permute-done.4.refs_4_
  29.6 0.6 all-to-all-done
  30.2 0.6 collective-permute-start.6
  30.8 1.6 %fetch_keys.1.first_ref = bf16[2,576,768]{2,1,0:T(8,128)(2,1)S(1)} custom-call(bf16[512,640]{1,0:T(8,128)(2,1)S(1)} %bitcast.10, bf16[8,576,768]{2,1,0:T(8,128)(2,1)} %bitcast.16), custom_call_target="tpu_custom_call" | custom-call | bytes 3538944 | tf_op jit(solution)/shard_map/fetch_keys/pallas_call | solution.py:450
  32.5 0.1 collective-permute-done.6.refs_0_
  32.5 0.3 copy-done.5
  32.8 5.2 %attend.1 = (bf16[640,640]{1,0:T(8,128)(2,1)S(1)}, f32[640,512]{1,0:T(8,128)S(1)}, bf16[640,128]{1,0:T(8,128)(2,1)S(1)}) custom-call(bf16[8,576,768]{2,1,0:T(8,128)(2,1)} %bitcast.17, bf16[2,576,768]{2,1,0:T(8,128)(2,1)S(1)} %fetch_keys.1.first_ref, bf16[2,576,768]{2,1,0:T(8,128)(2,1)S(1)} %bitcast.15, bf16[512,640]{1,0:T(8,128)(2,1)S(1)} %bitcast.11, ...), custom_call_target="tpu_custom_call" | custom-call | flops 5000000000 | bytes 20000000 | tf_op jit(solution)/shard_map/attend/pallas_call | solution.py:461
  38.1 0.1 collective-permute-start.7
  38.2 2.3 %collective-permute-done.7.got_ref = bf16[640,640]{1,0:T(8,128)(2,1)S(1)} collective-permute-done((bf16[640,640]{1,0:T(8,128)(2,1)S(1)}, bf16[640,640]{1,0:T(8,128)(2,1)S(1)}, u32[]{:S(2)}, u32[]{:S(2)}) %collective-permute-start.7) | collective-permute-done | bytes 819232 | tf_op jit(solution)/shard_map/ppermute | solution.py:432
  40.5 1.3 %join_cores.1 = (bf16[512,640]{1,0:T(8,128)(2,1)}, bf16[32,640]{1,0:T(8,128)(2,1)S(1)}, bf16[32,640]{1,0:T(8,128)(2,1)S(1)}, bf16[32,640]{1,0:T(8,128)(2,1)S(1)}...) custom-call(bf16[640,640]{1,0:T(8,128)(2,1)S(1)} %collective-permute-done.7.got_ref, ...), custom_call_target="tpu_custom_call" | custom-call | tf_op jit(solution)/shard_map/join_cores/pallas_call | solution.py:475
  41.8 7.0 %all-to-all-start.1 = ((bf16[64,8,640]{2,1,0:T(8,128)(2,1)}), bf16[64,8,640]{2,1,0:T(8,128)(2,1)S(1)}, u32[]{:S(2)}, u32[]{:S(2)}) async-start(bf16[64,8,640]{2,1,0:T(8,128)(2,1)} %bitcast.7), calls=%async_computation.1 | async-start | bytes 1310720 | tf_op jit(solution)/shard_map/all_to_all | solution.py:429
  48.8 5.3 %collective-permute-start.10 = (bf16[32,640]{1,0:T(8,128)(2,1)S(1)}, bf16[32,640]{1,0:T(8,128)(2,1)S(1)}, u32[]{:S(2)}, u32[]{:S(2)}) collective-permute-start(bf16[32,640]{1,0:T(8,128)(2,1)S(1)} %get-tuple-element.48), channel_id=1, source_target_pairs={{0,14},{1,3},{2,0},{3,5},{4,2},{5,7},{6,4},{7,9},{8,6},{9,11},{10,... | collective-permute-start | bytes 122888 | tf_op jit(solution)/shard_map/ppermute | solution.py:438
  54.1 0.9 %collective-permute-start.11 = (bf16[32,640]{1,0:T(8,128)(2,1)S(1)}, bf16[32,640]{1,0:T(8,128)(2,1)S(1)}, u32[]{:S(2)}, u32[]{:S(2)}) collective-permute-start(bf16[32,640]{1,0:T(8,128)(2,1)S(1)} %get-tuple-element.49), channel_id=1, source_target_pairs={{0,12},{1,5},{2,14},{3,7},{4,0},{5,9},{6,2},{7,11},{8,4},{9,13},{1... | collective-permute-start | bytes 122888 | tf_op jit(solution)/shard_map/ppermute | solution.py:438
  55.0 0.6 collective-permute-start.9
  55.5 2.7 %collective-permute-start.8 = (bf16[16,640]{1,0:T(8,128)(2,1)S(1)}, bf16[16,640]{1,0:T(8,128)(2,1)S(1)}, u32[]{:S(2)}, u32[]{:S(2)}) collective-permute-start(bf16[16,640]{1,0:T(8,128)(2,1)S(1)} %get-tuple-element.46), channel_id=1, source_target_pairs={{0,8},{1,9},{2,10},{3,11},{4,12},{5,13},{6,14},{7,15},{8,0},{9,1},... | collective-permute-start | bytes 61448 | tf_op jit(solution)/shard_map/ppermute | solution.py:438
  58.2 1.0 %own_keys.1 = (f32[80,512]{1,0:T(8,128)S(1)}, f32[80,256]{1,0:T(8,128)S(1)}, bf16[32,80]{1,0:T(8,128)(2,1)S(1)}) custom-call(s32[1,8]{1,0:T(1,128)S(1)} %copy-done.3, s32[2,10]{1,0:T(2,128)S(1)} %bitcast.14, bf16[10,2,576]{2,1,0:T(2,128)(2,1)S(1)} %copy-done.1, f32[1,64]{1,0:T(1,128)S(1)} %copy-done.4, bf16[80,640]{1,0:T(8,128)(2,1)S(1)} %get-tuple-element.32.own_ref), custom_call_target="tpu_custom_call" | custom-call | tf_op jit(solution)/shard_map/own_keys/pallas_call | solution.py:414
  59.3 3.4 %collective-permute-done.8.refs_1_ = bf16[16,640]{1,0:T(8,128)(2,1)S(1)} collective-permute-done((bf16[16,640]{1,0:T(8,128)(2,1)S(1)}, bf16[16,640]{1,0:T(8,128)(2,1)S(1)}, u32[]{:S(2)}, u32[]{:S(2)}) %collective-permute-start.8) | collective-permute-done | bytes 20512 | tf_op jit(solution)/shard_map/ppermute | solution.py:438
  62.7 0.1 collective-permute-start.12
  62.8 1.7 %all-to-all-done.1 = bf16[64,8,640]{2,1,0:T(8,128)(2,1)S(1)} async-done(((bf16[64,8,640]{2,1,0:T(8,128)(2,1)}), bf16[64,8,640]{2,1,0:T(8,128)(2,1)S(1)}, u32[]{:S(2)}, u32[]{:S(2)}) %all-to-all-start.1) | async-done | bytes 655392 | tf_op jit(solution)/shard_map/all_to_all | solution.py:429
  64.5 0.6 finish_new.1.new_ref
  65.2 1.1 %finish.1 = bf16[10,2,512]{2,1,0:T(2,128)(2,1)} custom-call(bf16[32,80]{1,0:T(8,128)(2,1)S(1)} %get-tuple-element.50.order_ref, f32[80,512]{1,0:T(8,128)S(1)} %get-tuple-element.51.own_ref, f32[80,256]{1,0:T(8,128)S(1)} %get-tuple-element.52.stat_ref, bf16[4,512,128]{2,1,0:T(8,128)(2,1)S(1)} %copy-done, f32[32,512]{1,0:T(8,128)S(1)} %finish_new.1.new_ref, ...), custom_call_target="tpu_custom_call" | custom-call | tf_op jit(solution)/shard_map/finish/pallas_call | solution.py:504
  (24 shorter events, 0.1 us)
Async XLA Ops:
  3.2 27.0 %all-to-all-start = ((bf16[64,8,640]{2,1,0:T(8,128)(2,1)}), bf16[64,8,640]{2,1,0:T(8,128)(2,1)S(1)}, u32[]{:S(2)}, u32[]{:S(2)}) async-start(bf16[64,8,640]{2,1,0:T(8,128)(2,1)} %bitcast.3), calls=%async_computation | async-start | bytes 1310720 | tf_op jit(solution)/shard_map/all_to_all | solution.py:429
  14.8 1.3 %collective-permute-start.1 = (bf16[16,640]{1,0:T(8,128)(2,1)S(1)}, bf16[16,640]{1,0:T(8,128)(2,1)S(1)}, u32[]{:S(2)}, u32[]{:S(2)}) collective-permute-start(bf16[16,640]{1,0:T(8,128)(2,1)S(1)} %get-tuple-element.37.refs_6_), channel_id=1, source_target_pairs={{0,1},{1,0},{2,3},{3,2},{4,5},{5,4},{6,7},{7,6},{8,9},{9,8},{10,11... | collective-permute-start | bytes 61448 | tf_op jit(solution)/shard_map/ppermute | solution.py:432
  16.0 12.8 %collective-permute-start.2 = (bf16[32,640]{1,0:T(8,128)(2,1)S(1)}, bf16[32,640]{1,0:T(8,128)(2,1)S(1)}, u32[]{:S(2)}, u32[]{:S(2)}) collective-permute-start(bf16[32,640]{1,0:T(8,128)(2,1)S(1)} %constant_dynamic-update-slice_fusion), channel_id=1, source_target_pairs={{0,6},{1,11},{2,8},{3,13},{4,10},{5,15},{6,12},{7,1},{8,14},{9,3},... | collective-permute-start | bytes 122888 | tf_op jit(solution)/shard_map/ppermute | solution.py:438
  20.0 9.1 %collective-permute-start.3 = (bf16[32,640]{1,0:T(8,128)(2,1)S(1)}, bf16[32,640]{1,0:T(8,128)(2,1)S(1)}, u32[]{:S(2)}, u32[]{:S(2)}) collective-permute-start(bf16[32,640]{1,0:T(8,128)(2,1)S(1)} %constant_dynamic-update-slice_fusion), channel_id=1, source_target_pairs={{0,2},{1,15},{2,4},{3,1},{4,6},{5,3},{6,8},{7,5},{8,10},{9,7},{10,... | collective-permute-start | bytes 122888 | tf_op jit(solution)/shard_map/ppermute | solution.py:438
  22.1 7.5 %collective-permute-start.4 = (bf16[32,640]{1,0:T(8,128)(2,1)S(1)}, bf16[32,640]{1,0:T(8,128)(2,1)S(1)}, u32[]{:S(2)}, u32[]{:S(2)}) collective-permute-start(bf16[32,640]{1,0:T(8,128)(2,1)S(1)} %constant_dynamic-update-slice_fusion), channel_id=1, source_target_pairs={{0,4},{1,13},{2,6},{3,15},{4,8},{5,1},{6,10},{7,3},{8,12},{9,5},{1... | collective-permute-start | bytes 122888 | tf_op jit(solution)/shard_map/ppermute | solution.py:438
  22.6 5.5 %collective-permute-start = (bf16[16,640]{1,0:T(8,128)(2,1)S(1)}, bf16[16,640]{1,0:T(8,128)(2,1)S(1)}, u32[]{:S(2)}, u32[]{:S(2)}) collective-permute-start(bf16[16,640]{1,0:T(8,128)(2,1)S(1)} %get-tuple-element.37.refs_6_), channel_id=1, source_target_pairs={{0,8},{1,9},{2,10},{3,11},{4,12},{5,13},{6,14},{7,15},{8,0},{9,1},... | collective-permute-start | bytes 61448 | tf_op jit(solution)/shard_map/ppermute | solution.py:438
  30.2 2.3 %collective-permute-start.5 = (bf16[512,640]{1,0:T(8,128)(2,1)S(1)}, bf16[512,640]{1,0:T(8,128)(2,1)S(1)}, u32[]{:S(2)}, u32[]{:S(2)}) collective-permute-start(bf16[512,640]{1,0:T(8,128)(2,1)S(1)} %bitcast.9), channel_id=1, source_target_pairs={{0,1},{1,0},{2,3},{3,2},{4,5},{5,4},{6,7},{7,6},{8,9},{9,8},{10,11... | collective-permute-start | bytes 1966088 | tf_op jit(solution)/shard_map/ppermute | solution.py:432
  30.2 2.3 %collective-permute-start.6 = (bf16[112,640]{1,0:T(8,128)(2,1)S(1)}, bf16[112,640]{1,0:T(8,128)(2,1)S(1)}, u32[]{:S(2)}, u32[]{:S(2)}) collective-permute-start(bf16[112,640]{1,0:T(8,128)(2,1)S(1)} %pad_maximum_fusion), channel_id=1, source_target_pairs={{0,1},{1,0},{2,3},{3,2},{4,5},{5,4},{6,7},{7,6},{8,9},{9,8},{10,11... | collective-permute-start | bytes 430088 | tf_op jit(solution)/shard_map/ppermute | solution.py:432
  30.8 2.0 %copy-start.5 = (bf16[2,768,576]{1,2,0:T(8,128)(2,1)S(1)}, bf16[2,768,576]{1,2,0:T(8,128)(2,1)}, u32[]{:S(2)}) copy-start(bf16[2,768,576]{1,2,0:T(8,128)(2,1)} %param.15) | copy-start | bytes 5308420
  38.1 2.4 %collective-permute-start.7 = (bf16[640,640]{1,0:T(8,128)(2,1)S(1)}, bf16[640,640]{1,0:T(8,128)(2,1)S(1)}, u32[]{:S(2)}, u32[]{:S(2)}) collective-permute-start(bf16[640,640]{1,0:T(8,128)(2,1)S(1)} %get-tuple-element.43), channel_id=1, source_target_pairs={{0,1},{1,0},{2,3},{3,2},{4,5},{5,4},{6,7},{7,6},{8,9},{9,8},{10,11... | collective-permute-start | bytes 2457608 | tf_op jit(solution)/shard_map/ppermute | solution.py:432
  40.5 17.7 %copy-start.1 = (bf16[10,2,576]{2,1,0:T(2,128)(2,1)S(1)}, bf16[10,2,576]{2,1,0:T(2,128)(2,1)}, u32[]{:S(2)}) copy-start(bf16[10,2,576]{2,1,0:T(2,128)(2,1)} %nl_ref.1) | copy-start | bytes 69124
  40.5 17.7 %copy-start.2 = (s32[10,2]{0,1:T(2,128)S(1)}, s32[10,2]{0,1:T(2,128)}, u32[]{:S(2)}) copy-start(s32[10,2]{0,1:T(2,128)} %param.20) | copy-start | bytes 244
  40.5 17.7 %copy-start.3 = (s32[1,8]{1,0:T(1,128)S(1)}, s32[1,8]{1,0:T(1,128)}, u32[]{:S(2)}) copy-start(s32[1,8]{1,0:T(1,128)} %slot_ref.1) | copy-start | bytes 100
  40.5 17.7 %copy-start.4 = (f32[1,64]{1,0:T(1,128)S(1)}, f32[1,64]{1,0:T(1,128)}, u32[]{:S(2)}) copy-start(f32[1,64]{1,0:T(1,128)} %constant.2.clone.freq_hbm.freq_ref) | copy-start | bytes 772
  40.5 24.0 %copy-start = (bf16[4,512,128]{2,1,0:T(8,128)(2,1)S(1)}, bf16[4,512,128]{2,1,0:T(8,128)(2,1)}, u32[]{:S(2)}) copy-start(bf16[4,512,128]{2,1,0:T(8,128)(2,1)} %wv_ref.3) | copy-start | bytes 1572868
  41.8 22.7 %all-to-all-start.1 = ((bf16[64,8,640]{2,1,0:T(8,128)(2,1)}), bf16[64,8,640]{2,1,0:T(8,128)(2,1)S(1)}, u32[]{:S(2)}, u32[]{:S(2)}) async-start(bf16[64,8,640]{2,1,0:T(8,128)(2,1)} %bitcast.7), calls=%async_computation.1 | async-start | bytes 1310720 | tf_op jit(solution)/shard_map/all_to_all | solution.py:429
  48.8 13.8 %collective-permute-start.10 = (bf16[32,640]{1,0:T(8,128)(2,1)S(1)}, bf16[32,640]{1,0:T(8,128)(2,1)S(1)}, u32[]{:S(2)}, u32[]{:S(2)}) collective-permute-start(bf16[32,640]{1,0:T(8,128)(2,1)S(1)} %get-tuple-element.48), channel_id=1, source_target_pairs={{0,14},{1,3},{2,0},{3,5},{4,2},{5,7},{6,4},{7,9},{8,6},{9,11},{10,... | collective-permute-start | bytes 122888 | tf_op jit(solution)/shard_map/ppermute | solution.py:438
  54.1 8.6 %collective-permute-start.11 = (bf16[32,640]{1,0:T(8,128)(2,1)S(1)}, bf16[32,640]{1,0:T(8,128)(2,1)S(1)}, u32[]{:S(2)}, u32[]{:S(2)}) collective-permute-start(bf16[32,640]{1,0:T(8,128)(2,1)S(1)} %get-tuple-element.49), channel_id=1, source_target_pairs={{0,12},{1,5},{2,14},{3,7},{4,0},{5,9},{6,2},{7,11},{8,4},{9,13},{1... | collective-permute-start | bytes 122888 | tf_op jit(solution)/shard_map/ppermute | solution.py:438
  55.0 7.7 %collective-permute-start.9 = (bf16[32,640]{1,0:T(8,128)(2,1)S(1)}, bf16[32,640]{1,0:T(8,128)(2,1)S(1)}, u32[]{:S(2)}, u32[]{:S(2)}) collective-permute-start(bf16[32,640]{1,0:T(8,128)(2,1)S(1)} %get-tuple-element.47), channel_id=1, source_target_pairs={{0,10},{1,7},{2,12},{3,9},{4,14},{5,11},{6,0},{7,13},{8,2},{9,15},... | collective-permute-start | bytes 122888 | tf_op jit(solution)/shard_map/ppermute | solution.py:438
  55.5 7.1 %collective-permute-start.8 = (bf16[16,640]{1,0:T(8,128)(2,1)S(1)}, bf16[16,640]{1,0:T(8,128)(2,1)S(1)}, u32[]{:S(2)}, u32[]{:S(2)}) collective-permute-start(bf16[16,640]{1,0:T(8,128)(2,1)S(1)} %get-tuple-element.46), channel_id=1, source_target_pairs={{0,8},{1,9},{2,10},{3,11},{4,12},{5,13},{6,14},{7,15},{8,0},{9,1},... | collective-permute-start | bytes 61448 | tf_op jit(solution)/shard_map/ppermute | solution.py:438
  62.7 2.5 %collective-permute-start.12 = (bf16[48,640]{1,0:T(8,128)(2,1)S(1)}, bf16[48,640]{1,0:T(8,128)(2,1)S(1)}, u32[]{:S(2)}, u32[]{:S(2)}) collective-permute-start(bf16[48,640]{1,0:T(8,128)(2,1)S(1)} %pad_maximum_fusion.1), channel_id=1, source_target_pairs={{0,1},{1,0},{2,3},{3,2},{4,5},{5,4},{6,7},{7,6},{8,9},{9,8},{10,11... | collective-permute-start | bytes 184328 | tf_op jit(solution)/shard_map/ppermute | solution.py:432

commit v6 on v5

--- a/solution.py
+++ b/solution.py
@@ -243,7 +243,7 @@
         scores, length = ahead
         if n + 1 < rows:
             if order[n + 1] == arrived:
-                upto = min(slots, arrived + n + 1)
+                upto = min(slots, arrived + 3)
                 for load in loads[arrived - here : upto - here]:
                     load.wait()
                 arrived = upto

time: 66.6 us -> 66.4 us (level)
  no operation moved by 1% of the time
where the time goes in v6:
time: 66.4 us; the launch traced here: 66.1 us
  starting transfers between devices  37.4 us (56%)
  waiting for transfers between devices  14.2 us (21%)
  Pallas kernels  14 us (21%)
    all_to_all x2, starting transfers between devices, exchange(): lax.all_to_all(x.reshape(n, -1, WIDE), axes, 0, 0, tiled=True)  18.5 us
    ppermute x8, starting transfers between devices, turned(): return lax.ppermute(x, ('zx', 'core'), pairs)  18 us
    ppermute x8, waiting for transfers between devices, turned(): return lax.ppermute(x, ('zx', 'core'), pairs)  8.28 us
    pallas_call x1, Pallas kernels, local(): pl.pallas_call(functools.partial(attend_kernel, piece), out_shape=(shape(...  4.99 us
    ppermute x5, waiting for transfers between devices, swap(): return lax.ppermute(x, 'core', [(0, 1), (1, 0)])  3.55 us
    pallas_call x1, Pallas kernels, local(): pl.pallas_call(functools.partial(project_kernel, heads, slots, copies), o...  3.23 us
    all_to_all x2, waiting for transfers between devices, exchange(): lax.all_to_all(x.reshape(n, -1, WIDE), axes, 0, 0, tiled=True)  2.37 us
    pallas_call x1, Pallas kernels, local(): pl.pallas_call(fetch_kernel, out_shape=pltpu.VMEM((first, *fresh.shape[1:...  1.61 us
  transfers between devices with their start and end apart: 15, of which 10 were waited for; matrix products, arithmetic and copies ran while one was open for 0% of the time, Pallas kernels for 5%

profile of v6, /device:TPU:0, one launch (start us, length us, event | category | flops | bytes accessed | tf_op | source)
XLA Modules:
  0.0 66.1 jit_solution(6659265155709986954)
XLA Ops:
  0.0 3.2 %project.1 = (bf16[512,640]{1,0:T(8,128)(2,1)}, bf16[16,640]{1,0:T(8,128)(2,1)S(1)}, bf16[80,640]{1,0:T(8,128)(2,1)S(1)}) custom-call(s32[1,8]{1,0:T(1,128)} %slot_ref.1, s32[10]{0:T(128)} %len_hbm.1, s32[2,10]{1,0:T(2,128)} %bitcast.13, bf16[10,2,1536]{2,1,0:T(2,128)(2,1)} %ql_hbm.1, bf16[1536,768]{1,0:T(8,128)(2,1)} %wq_hbm.1, ...), custom_call_target="tpu_custom_call" | custom-call | tf_op jit(solution)/shard_map/project/pallas_call | solution.py:389
  3.2 11.5 %all-to-all-start = ((bf16[64,8,640]{2,1,0:T(8,128)(2,1)}), bf16[64,8,640]{2,1,0:T(8,128)(2,1)S(1)}, u32[]{:S(2)}, u32[]{:S(2)}) async-start(bf16[64,8,640]{2,1,0:T(8,128)(2,1)} %bitcast.3), calls=%async_computation | async-start | bytes 1310720 | tf_op jit(solution)/shard_map/all_to_all | solution.py:429
  14.8 0.1 collective-permute-start.1
  14.9 1.2 %collective-permute-done.1.refs_1_ = bf16[16,640]{1,0:T(8,128)(2,1)S(1)} collective-permute-done((bf16[16,640]{1,0:T(8,128)(2,1)S(1)}, bf16[16,640]{1,0:T(8,128)(2,1)S(1)}, u32[]{:S(2)}, u32[]{:S(2)}) %collective-permute-start.1) | collective-permute-done | bytes 20512 | tf_op jit(solution)/shard_map/ppermute | solution.py:432
  16.0 4.0 %collective-permute-start.2 = (bf16[32,640]{1,0:T(8,128)(2,1)S(1)}, bf16[32,640]{1,0:T(8,128)(2,1)S(1)}, u32[]{:S(2)}, u32[]{:S(2)}) collective-permute-start(bf16[32,640]{1,0:T(8,128)(2,1)S(1)} %constant_dynamic-update-slice_fusion), channel_id=1, source_target_pairs={{0,6},{1,11},{2,8},{3,13},{4,10},{5,15},{6,12},{7,1},{8,14},{9,3},... | collective-permute-start | bytes 122888 | tf_op jit(solution)/shard_map/ppermute | solution.py:438
  20.0 2.1 %collective-permute-start.3 = (bf16[32,640]{1,0:T(8,128)(2,1)S(1)}, bf16[32,640]{1,0:T(8,128)(2,1)S(1)}, u32[]{:S(2)}, u32[]{:S(2)}) collective-permute-start(bf16[32,640]{1,0:T(8,128)(2,1)S(1)} %constant_dynamic-update-slice_fusion), channel_id=1, source_target_pairs={{0,2},{1,15},{2,4},{3,1},{4,6},{5,3},{6,8},{7,5},{8,10},{9,7},{10,... | collective-permute-start | bytes 122888 | tf_op jit(solution)/shard_map/ppermute | solution.py:438
  22.1 0.6 collective-permute-start.4
  22.6 2.1 %collective-permute-start = (bf16[16,640]{1,0:T(8,128)(2,1)S(1)}, bf16[16,640]{1,0:T(8,128)(2,1)S(1)}, u32[]{:S(2)}, u32[]{:S(2)}) collective-permute-start(bf16[16,640]{1,0:T(8,128)(2,1)S(1)} %get-tuple-element.37.refs_6_), channel_id=1, source_target_pairs={{0,8},{1,9},{2,10},{3,11},{4,12},{5,13},{6,14},{7,15},{8,0},{9,1},... | collective-permute-start | bytes 61448 | tf_op jit(solution)/shard_map/ppermute | solution.py:438
  24.7 3.4 %collective-permute-done.refs_5_ = bf16[16,640]{1,0:T(8,128)(2,1)S(1)} collective-permute-done((bf16[16,640]{1,0:T(8,128)(2,1)S(1)}, bf16[16,640]{1,0:T(8,128)(2,1)S(1)}, u32[]{:S(2)}, u32[]{:S(2)}) %collective-permute-start) | collective-permute-done | bytes 20512 | tf_op jit(solution)/shard_map/ppermute | solution.py:438
  28.1 0.8 %collective-permute-done.2.refs_2_ = bf16[32,640]{1,0:T(8,128)(2,1)S(1)} collective-permute-done((bf16[32,640]{1,0:T(8,128)(2,1)S(1)}, bf16[32,640]{1,0:T(8,128)(2,1)S(1)}, u32[]{:S(2)}, u32[]{:S(2)}) %collective-permute-start.2) | collective-permute-done | bytes 40992 | tf_op jit(solution)/shard_map/ppermute | solution.py:438
  28.9 0.2 collective-permute-done.3.refs_3_
  29.1 0.5 collective-permute-done.4.refs_4_
  29.6 0.6 all-to-all-done
  30.2 0.6 collective-permute-start.6
  30.8 1.6 %fetch_keys.1.first_ref = bf16[2,576,768]{2,1,0:T(8,128)(2,1)S(1)} custom-call(bf16[512,640]{1,0:T(8,128)(2,1)S(1)} %bitcast.10, bf16[8,576,768]{2,1,0:T(8,128)(2,1)} %bitcast.16), custom_call_target="tpu_custom_call" | custom-call | bytes 3538944 | tf_op jit(solution)/shard_map/fetch_keys/pallas_call | solution.py:450
  32.5 0.1 collective-permute-done.6.refs_0_
  32.5 0.3 copy-done.5
  32.8 5.0 %attend.1 = (bf16[640,640]{1,0:T(8,128)(2,1)S(1)}, f32[640,512]{1,0:T(8,128)S(1)}, bf16[640,128]{1,0:T(8,128)(2,1)S(1)}) custom-call(bf16[8,576,768]{2,1,0:T(8,128)(2,1)} %bitcast.17, bf16[2,576,768]{2,1,0:T(8,128)(2,1)S(1)} %fetch_keys.1.first_ref, bf16[2,576,768]{2,1,0:T(8,128)(2,1)S(1)} %bitcast.15, bf16[512,640]{1,0:T(8,128)(2,1)S(1)} %bitcast.11, ...), custom_call_target="tpu_custom_call" | custom-call | flops 5000000000 | bytes 20000000 | tf_op jit(solution)/shard_map/attend/pallas_call | solution.py:461
  37.8 0.1 collective-permute-start.7
  37.9 2.3 %collective-permute-done.7.got_ref = bf16[640,640]{1,0:T(8,128)(2,1)S(1)} collective-permute-done((bf16[640,640]{1,0:T(8,128)(2,1)S(1)}, bf16[640,640]{1,0:T(8,128)(2,1)S(1)}, u32[]{:S(2)}, u32[]{:S(2)}) %collective-permute-start.7) | collective-permute-done | bytes 819232 | tf_op jit(solution)/shard_map/ppermute | solution.py:432
  40.3 1.3 %join_cores.1 = (bf16[512,640]{1,0:T(8,128)(2,1)}, bf16[32,640]{1,0:T(8,128)(2,1)S(1)}, bf16[32,640]{1,0:T(8,128)(2,1)S(1)}, bf16[32,640]{1,0:T(8,128)(2,1)S(1)}...) custom-call(bf16[640,640]{1,0:T(8,128)(2,1)S(1)} %collective-permute-done.7.got_ref, ...), custom_call_target="tpu_custom_call" | custom-call | tf_op jit(solution)/shard_map/join_cores/pallas_call | solution.py:475
  41.6 7.0 %all-to-all-start.1 = ((bf16[64,8,640]{2,1,0:T(8,128)(2,1)}), bf16[64,8,640]{2,1,0:T(8,128)(2,1)S(1)}, u32[]{:S(2)}, u32[]{:S(2)}) async-start(bf16[64,8,640]{2,1,0:T(8,128)(2,1)} %bitcast.7), calls=%async_computation.1 | async-start | bytes 1310720 | tf_op jit(solution)/shard_map/all_to_all | solution.py:429
  48.6 5.3 %collective-permute-start.10 = (bf16[32,640]{1,0:T(8,128)(2,1)S(1)}, bf16[32,640]{1,0:T(8,128)(2,1)S(1)}, u32[]{:S(2)}, u32[]{:S(2)}) collective-permute-start(bf16[32,640]{1,0:T(8,128)(2,1)S(1)} %get-tuple-element.48), channel_id=1, source_target_pairs={{0,14},{1,3},{2,0},{3,5},{4,2},{5,7},{6,4},{7,9},{8,6},{9,11},{10,... | collective-permute-start | bytes 122888 | tf_op jit(solution)/shard_map/ppermute | solution.py:438
  53.8 0.9 %collective-permute-start.11 = (bf16[32,640]{1,0:T(8,128)(2,1)S(1)}, bf16[32,640]{1,0:T(8,128)(2,1)S(1)}, u32[]{:S(2)}, u32[]{:S(2)}) collective-permute-start(bf16[32,640]{1,0:T(8,128)(2,1)S(1)} %get-tuple-element.49), channel_id=1, source_target_pairs={{0,12},{1,5},{2,14},{3,7},{4,0},{5,9},{6,2},{7,11},{8,4},{9,13},{1... | collective-permute-start | bytes 122888 | tf_op jit(solution)/shard_map/ppermute | solution.py:438
  54.7 0.6 collective-permute-start.9
  55.3 2.7 %collective-permute-start.8 = (bf16[16,640]{1,0:T(8,128)(2,1)S(1)}, bf16[16,640]{1,0:T(8,128)(2,1)S(1)}, u32[]{:S(2)}, u32[]{:S(2)}) collective-permute-start(bf16[16,640]{1,0:T(8,128)(2,1)S(1)} %get-tuple-element.46), channel_id=1, source_target_pairs={{0,8},{1,9},{2,10},{3,11},{4,12},{5,13},{6,14},{7,15},{8,0},{9,1},... | collective-permute-start | bytes 61448 | tf_op jit(solution)/shard_map/ppermute | solution.py:438
  58.0 1.0 %own_keys.1 = (f32[80,512]{1,0:T(8,128)S(1)}, f32[80,256]{1,0:T(8,128)S(1)}, bf16[32,80]{1,0:T(8,128)(2,1)S(1)}) custom-call(s32[1,8]{1,0:T(1,128)S(1)} %copy-done.3, s32[2,10]{1,0:T(2,128)S(1)} %bitcast.14, bf16[10,2,576]{2,1,0:T(2,128)(2,1)S(1)} %copy-done.1, f32[1,64]{1,0:T(1,128)S(1)} %copy-done.4, bf16[80,640]{1,0:T(8,128)(2,1)S(1)} %get-tuple-element.32.own_ref), custom_call_target="tpu_custom_call" | custom-call | tf_op jit(solution)/shard_map/own_keys/pallas_call | solution.py:414
  59.0 3.4 %collective-permute-done.8.refs_1_ = bf16[16,640]{1,0:T(8,128)(2,1)S(1)} collective-permute-done((bf16[16,640]{1,0:T(8,128)(2,1)S(1)}, bf16[16,640]{1,0:T(8,128)(2,1)S(1)}, u32[]{:S(2)}, u32[]{:S(2)}) %collective-permute-start.8) | collective-permute-done | bytes 20512 | tf_op jit(solution)/shard_map/ppermute | solution.py:438
  62.5 0.1 collective-permute-start.12
  62.6 1.7 %all-to-all-done.1 = bf16[64,8,640]{2,1,0:T(8,128)(2,1)S(1)} async-done(((bf16[64,8,640]{2,1,0:T(8,128)(2,1)}), bf16[64,8,640]{2,1,0:T(8,128)(2,1)S(1)}, u32[]{:S(2)}, u32[]{:S(2)}) %all-to-all-start.1) | async-done | bytes 655392 | tf_op jit(solution)/shard_map/all_to_all | solution.py:429
  64.3 0.7 finish_new.1.new_ref
  64.9 1.1 %finish.1 = bf16[10,2,512]{2,1,0:T(2,128)(2,1)} custom-call(bf16[32,80]{1,0:T(8,128)(2,1)S(1)} %get-tuple-element.50.order_ref, f32[80,512]{1,0:T(8,128)S(1)} %get-tuple-element.51.own_ref, f32[80,256]{1,0:T(8,128)S(1)} %get-tuple-element.52.stat_ref, bf16[4,512,128]{2,1,0:T(8,128)(2,1)S(1)} %copy-done, f32[32,512]{1,0:T(8,128)S(1)} %finish_new.1.new_ref, ...), custom_call_target="tpu_custom_call" | custom-call | tf_op jit(solution)/shard_map/finish/pallas_call | solution.py:504
  (24 shorter events, 0.1 us)
Async XLA Ops:
  3.2 27.0 %all-to-all-start = ((bf16[64,8,640]{2,1,0:T(8,128)(2,1)}), bf16[64,8,640]{2,1,0:T(8,128)(2,1)S(1)}, u32[]{:S(2)}, u32[]{:S(2)}) async-start(bf16[64,8,640]{2,1,0:T(8,128)(2,1)} %bitcast.3), calls=%async_computation | async-start | bytes 1310720 | tf_op jit(solution)/shard_map/all_to_all | solution.py:429
  14.8 1.3 %collective-permute-start.1 = (bf16[16,640]{1,0:T(8,128)(2,1)S(1)}, bf16[16,640]{1,0:T(8,128)(2,1)S(1)}, u32[]{:S(2)}, u32[]{:S(2)}) collective-permute-start(bf16[16,640]{1,0:T(8,128)(2,1)S(1)} %get-tuple-element.37.refs_6_), channel_id=1, source_target_pairs={{0,1},{1,0},{2,3},{3,2},{4,5},{5,4},{6,7},{7,6},{8,9},{9,8},{10,11... | collective-permute-start | bytes 61448 | tf_op jit(solution)/shard_map/ppermute | solution.py:432
  16.0 12.8 %collective-permute-start.2 = (bf16[32,640]{1,0:T(8,128)(2,1)S(1)}, bf16[32,640]{1,0:T(8,128)(2,1)S(1)}, u32[]{:S(2)}, u32[]{:S(2)}) collective-permute-start(bf16[32,640]{1,0:T(8,128)(2,1)S(1)} %constant_dynamic-update-slice_fusion), channel_id=1, source_target_pairs={{0,6},{1,11},{2,8},{3,13},{4,10},{5,15},{6,12},{7,1},{8,14},{9,3},... | collective-permute-start | bytes 122888 | tf_op jit(solution)/shard_map/ppermute | solution.py:438
  20.0 9.1 %collective-permute-start.3 = (bf16[32,640]{1,0:T(8,128)(2,1)S(1)}, bf16[32,640]{1,0:T(8,128)(2,1)S(1)}, u32[]{:S(2)}, u32[]{:S(2)}) collective-permute-start(bf16[32,640]{1,0:T(8,128)(2,1)S(1)} %constant_dynamic-update-slice_fusion), channel_id=1, source_target_pairs={{0,2},{1,15},{2,4},{3,1},{4,6},{5,3},{6,8},{7,5},{8,10},{9,7},{10,... | collective-permute-start | bytes 122888 | tf_op jit(solution)/shard_map/ppermute | solution.py:438
  22.1 7.5 %collective-permute-start.4 = (bf16[32,640]{1,0:T(8,128)(2,1)S(1)}, bf16[32,640]{1,0:T(8,128)(2,1)S(1)}, u32[]{:S(2)}, u32[]{:S(2)}) collective-permute-start(bf16[32,640]{1,0:T(8,128)(2,1)S(1)} %constant_dynamic-update-slice_fusion), channel_id=1, source_target_pairs={{0,4},{1,13},{2,6},{3,15},{4,8},{5,1},{6,10},{7,3},{8,12},{9,5},{1... | collective-permute-start | bytes 122888 | tf_op jit(solution)/shard_map/ppermute | solution.py:438
  22.6 5.5 %collective-permute-start = (bf16[16,640]{1,0:T(8,128)(2,1)S(1)}, bf16[16,640]{1,0:T(8,128)(2,1)S(1)}, u32[]{:S(2)}, u32[]{:S(2)}) collective-permute-start(bf16[16,640]{1,0:T(8,128)(2,1)S(1)} %get-tuple-element.37.refs_6_), channel_id=1, source_target_pairs={{0,8},{1,9},{2,10},{3,11},{4,12},{5,13},{6,14},{7,15},{8,0},{9,1},... | collective-permute-start | bytes 61448 | tf_op jit(solution)/shard_map/ppermute | solution.py:438
  30.2 2.3 %collective-permute-start.5 = (bf16[512,640]{1,0:T(8,128)(2,1)S(1)}, bf16[512,640]{1,0:T(8,128)(2,1)S(1)}, u32[]{:S(2)}, u32[]{:S(2)}) collective-permute-start(bf16[512,640]{1,0:T(8,128)(2,1)S(1)} %bitcast.9), channel_id=1, source_target_pairs={{0,1},{1,0},{2,3},{3,2},{4,5},{5,4},{6,7},{7,6},{8,9},{9,8},{10,11... | collective-permute-start | bytes 1966088 | tf_op jit(solution)/shard_map/ppermute | solution.py:432
  30.2 2.3 %collective-permute-start.6 = (bf16[112,640]{1,0:T(8,128)(2,1)S(1)}, bf16[112,640]{1,0:T(8,128)(2,1)S(1)}, u32[]{:S(2)}, u32[]{:S(2)}) collective-permute-start(bf16[112,640]{1,0:T(8,128)(2,1)S(1)} %pad_maximum_fusion), channel_id=1, source_target_pairs={{0,1},{1,0},{2,3},{3,2},{4,5},{5,4},{6,7},{7,6},{8,9},{9,8},{10,11... | collective-permute-start | bytes 430088 | tf_op jit(solution)/shard_map/ppermute | solution.py:432
  30.8 2.0 %copy-start.5 = (bf16[2,768,576]{1,2,0:T(8,128)(2,1)S(1)}, bf16[2,768,576]{1,2,0:T(8,128)(2,1)}, u32[]{:S(2)}) copy-start(bf16[2,768,576]{1,2,0:T(8,128)(2,1)} %param.15) | copy-start | bytes 5308420
  37.8 2.4 %collective-permute-start.7 = (bf16[640,640]{1,0:T(8,128)(2,1)S(1)}, bf16[640,640]{1,0:T(8,128)(2,1)S(1)}, u32[]{:S(2)}, u32[]{:S(2)}) collective-permute-start(bf16[640,640]{1,0:T(8,128)(2,1)S(1)} %get-tuple-element.43), channel_id=1, source_target_pairs={{0,1},{1,0},{2,3},{3,2},{4,5},{5,4},{6,7},{7,6},{8,9},{9,8},{10,11... | collective-permute-start | bytes 2457608 | tf_op jit(solution)/shard_map/ppermute | solution.py:432
  40.3 17.7 %copy-start.1 = (bf16[10,2,576]{2,1,0:T(2,128)(2,1)S(1)}, bf16[10,2,576]{2,1,0:T(2,128)(2,1)}, u32[]{:S(2)}) copy-start(bf16[10,2,576]{2,1,0:T(2,128)(2,1)} %nl_ref.1) | copy-start | bytes 69124
  40.3 17.7 %copy-start.2 = (s32[10,2]{0,1:T(2,128)S(1)}, s32[10,2]{0,1:T(2,128)}, u32[]{:S(2)}) copy-start(s32[10,2]{0,1:T(2,128)} %param.20) | copy-start | bytes 244
  40.3 17.7 %copy-start.3 = (s32[1,8]{1,0:T(1,128)S(1)}, s32[1,8]{1,0:T(1,128)}, u32[]{:S(2)}) copy-start(s32[1,8]{1,0:T(1,128)} %slot_ref.1) | copy-start | bytes 100
  40.3 17.7 %copy-start.4 = (f32[1,64]{1,0:T(1,128)S(1)}, f32[1,64]{1,0:T(1,128)}, u32[]{:S(2)}) copy-start(f32[1,64]{1,0:T(1,128)} %constant.2.clone.freq_hbm.freq_ref) | copy-start | bytes 772
  40.3 24.0 %copy-start = (bf16[4,512,128]{2,1,0:T(8,128)(2,1)S(1)}, bf16[4,512,128]{2,1,0:T(8,128)(2,1)}, u32[]{:S(2)}) copy-start(bf16[4,512,128]{2,1,0:T(8,128)(2,1)} %wv_ref.3) | copy-start | bytes 1572868
  41.6 22.7 %all-to-all-start.1 = ((bf16[64,8,640]{2,1,0:T(8,128)(2,1)}), bf16[64,8,640]{2,1,0:T(8,128)(2,1)S(1)}, u32[]{:S(2)}, u32[]{:S(2)}) async-start(bf16[64,8,640]{2,1,0:T(8,128)(2,1)} %bitcast.7), calls=%async_computation.1 | async-start | bytes 1310720 | tf_op jit(solution)/shard_map/all_to_all | solution.py:429
  48.6 13.8 %collective-permute-start.10 = (bf16[32,640]{1,0:T(8,128)(2,1)S(1)}, bf16[32,640]{1,0:T(8,128)(2,1)S(1)}, u32[]{:S(2)}, u32[]{:S(2)}) collective-permute-start(bf16[32,640]{1,0:T(8,128)(2,1)S(1)} %get-tuple-element.48), channel_id=1, source_target_pairs={{0,14},{1,3},{2,0},{3,5},{4,2},{5,7},{6,4},{7,9},{8,6},{9,11},{10,... | collective-permute-start | bytes 122888 | tf_op jit(solution)/shard_map/ppermute | solution.py:438
  53.8 8.6 %collective-permute-start.11 = (bf16[32,640]{1,0:T(8,128)(2,1)S(1)}, bf16[32,640]{1,0:T(8,128)(2,1)S(1)}, u32[]{:S(2)}, u32[]{:S(2)}) collective-permute-start(bf16[32,640]{1,0:T(8,128)(2,1)S(1)} %get-tuple-element.49), channel_id=1, source_target_pairs={{0,12},{1,5},{2,14},{3,7},{4,0},{5,9},{6,2},{7,11},{8,4},{9,13},{1... | collective-permute-start | bytes 122888 | tf_op jit(solution)/shard_map/ppermute | solution.py:438
  54.7 7.7 %collective-permute-start.9 = (bf16[32,640]{1,0:T(8,128)(2,1)S(1)}, bf16[32,640]{1,0:T(8,128)(2,1)S(1)}, u32[]{:S(2)}, u32[]{:S(2)}) collective-permute-start(bf16[32,640]{1,0:T(8,128)(2,1)S(1)} %get-tuple-element.47), channel_id=1, source_target_pairs={{0,10},{1,7},{2,12},{3,9},{4,14},{5,11},{6,0},{7,13},{8,2},{9,15},... | collective-permute-start | bytes 122888 | tf_op jit(solution)/shard_map/ppermute | solution.py:438
  55.3 7.1 %collective-permute-start.8 = (bf16[16,640]{1,0:T(8,128)(2,1)S(1)}, bf16[16,640]{1,0:T(8,128)(2,1)S(1)}, u32[]{:S(2)}, u32[]{:S(2)}) collective-permute-start(bf16[16,640]{1,0:T(8,128)(2,1)S(1)} %get-tuple-element.46), channel_id=1, source_target_pairs={{0,8},{1,9},{2,10},{3,11},{4,12},{5,13},{6,14},{7,15},{8,0},{9,1},... | collective-permute-start | bytes 61448 | tf_op jit(solution)/shard_map/ppermute | solution.py:438
  62.5 2.5 %collective-permute-start.12 = (bf16[48,640]{1,0:T(8,128)(2,1)S(1)}, bf16[48,640]{1,0:T(8,128)(2,1)S(1)}, u32[]{:S(2)}, u32[]{:S(2)}) collective-permute-start(bf16[48,640]{1,0:T(8,128)(2,1)S(1)} %pad_maximum_fusion.1), channel_id=1, source_target_pairs={{0,1},{1,0},{2,3},{3,2},{4,5},{5,4},{6,7},{7,6},{8,9},{9,8},{10,11... | collective-permute-start | bytes 184328 | tf_op jit(solution)/shard_map/ppermute | solution.py:432

commit v7 on v6

--- a/solution.py
+++ b/solution.py
@@ -479,7 +479,7 @@
         + (shape((resident * piece, WIDE), BF),) * 2,
         in_specs=[VMEM] * 3,
         out_specs=(ANY,) + (VMEM,) * (len(near) + 2),
-        scratch_shapes=[pltpu.VMEM((slots * half, WIDE), BF), pltpu.SemaphoreType.DMA((4,))],
+        scratch_shapes=[pltpu.VMEM((slots * half, WIDE), BF), pltpu.SemaphoreType.DMA((2,))],
         compiler_params=params(32),
         name="join_cores",
     )(swap(send), keep, stat)

time: 66.4 us -> 66.4 us (level)
  no operation moved by 1% of the time
where the time goes in v7:
time: 66.4 us; the launch traced here: 66.1 us
  starting transfers between devices  37.4 us (56%)
  waiting for transfers between devices  14.2 us (21%)
  Pallas kernels  14 us (21%)
    all_to_all x2, starting transfers between devices, exchange(): lax.all_to_all(x.reshape(n, -1, WIDE), axes, 0, 0, tiled=True)  18.5 us
    ppermute x8, starting transfers between devices, turned(): return lax.ppermute(x, ('zx', 'core'), pairs)  18 us
    ppermute x8, waiting for transfers between devices, turned(): return lax.ppermute(x, ('zx', 'core'), pairs)  8.28 us
    pallas_call x1, Pallas kernels, local(): pl.pallas_call(functools.partial(attend_kernel, piece), out_shape=(shape(...  4.99 us
    ppermute x5, waiting for transfers between devices, swap(): return lax.ppermute(x, 'core', [(0, 1), (1, 0)])  3.55 us
    pallas_call x1, Pallas kernels, local(): pl.pallas_call(functools.partial(project_kernel, heads, slots, copies), o...  3.23 us
    all_to_all x2, waiting for transfers between devices, exchange(): lax.all_to_all(x.reshape(n, -1, WIDE), axes, 0, 0, tiled=True)  2.37 us
    pallas_call x1, Pallas kernels, local(): pl.pallas_call(fetch_kernel, out_shape=pltpu.VMEM((first, *fresh.shape[1:...  1.61 us
  transfers between devices with their start and end apart: 15, of which 10 were waited for; matrix products, arithmetic and copies ran while one was open for 0% of the time, Pallas kernels for 5%

profile of v7, /device:TPU:0, one launch (start us, length us, event | category | flops | bytes accessed | tf_op | source)
XLA Modules:
  0.0 66.1 jit_solution(9620398196616117768)
XLA Ops:
  0.0 3.2 %project.1 = (bf16[512,640]{1,0:T(8,128)(2,1)}, bf16[16,640]{1,0:T(8,128)(2,1)S(1)}, bf16[80,640]{1,0:T(8,128)(2,1)S(1)}) custom-call(s32[1,8]{1,0:T(1,128)} %slot_ref.1, s32[10]{0:T(128)} %len_hbm.1, s32[2,10]{1,0:T(2,128)} %bitcast.13, bf16[10,2,1536]{2,1,0:T(2,128)(2,1)} %ql_hbm.1, bf16[1536,768]{1,0:T(8,128)(2,1)} %wq_hbm.1, ...), custom_call_target="tpu_custom_call" | custom-call | tf_op jit(solution)/shard_map/project/pallas_call | solution.py:389
  3.2 11.5 %all-to-all-start = ((bf16[64,8,640]{2,1,0:T(8,128)(2,1)}), bf16[64,8,640]{2,1,0:T(8,128)(2,1)S(1)}, u32[]{:S(2)}, u32[]{:S(2)}) async-start(bf16[64,8,640]{2,1,0:T(8,128)(2,1)} %bitcast.3), calls=%async_computation | async-start | bytes 1310720 | tf_op jit(solution)/shard_map/all_to_all | solution.py:429
  14.8 0.1 collective-permute-start.1
  14.9 1.2 %collective-permute-done.1.refs_1_ = bf16[16,640]{1,0:T(8,128)(2,1)S(1)} collective-permute-done((bf16[16,640]{1,0:T(8,128)(2,1)S(1)}, bf16[16,640]{1,0:T(8,128)(2,1)S(1)}, u32[]{:S(2)}, u32[]{:S(2)}) %collective-permute-start.1) | collective-permute-done | bytes 20512 | tf_op jit(solution)/shard_map/ppermute | solution.py:432
  16.0 4.0 %collective-permute-start.2 = (bf16[32,640]{1,0:T(8,128)(2,1)S(1)}, bf16[32,640]{1,0:T(8,128)(2,1)S(1)}, u32[]{:S(2)}, u32[]{:S(2)}) collective-permute-start(bf16[32,640]{1,0:T(8,128)(2,1)S(1)} %constant_dynamic-update-slice_fusion), channel_id=1, source_target_pairs={{0,6},{1,11},{2,8},{3,13},{4,10},{5,15},{6,12},{7,1},{8,14},{9,3},... | collective-permute-start | bytes 122888 | tf_op jit(solution)/shard_map/ppermute | solution.py:438
  20.0 2.1 %collective-permute-start.3 = (bf16[32,640]{1,0:T(8,128)(2,1)S(1)}, bf16[32,640]{1,0:T(8,128)(2,1)S(1)}, u32[]{:S(2)}, u32[]{:S(2)}) collective-permute-start(bf16[32,640]{1,0:T(8,128)(2,1)S(1)} %constant_dynamic-update-slice_fusion), channel_id=1, source_target_pairs={{0,2},{1,15},{2,4},{3,1},{4,6},{5,3},{6,8},{7,5},{8,10},{9,7},{10,... | collective-permute-start | bytes 122888 | tf_op jit(solution)/shard_map/ppermute | solution.py:438
  22.1 0.6 collective-permute-start.4
  22.6 2.1 %collective-permute-start = (bf16[16,640]{1,0:T(8,128)(2,1)S(1)}, bf16[16,640]{1,0:T(8,128)(2,1)S(1)}, u32[]{:S(2)}, u32[]{:S(2)}) collective-permute-start(bf16[16,640]{1,0:T(8,128)(2,1)S(1)} %get-tuple-element.37.refs_6_), channel_id=1, source_target_pairs={{0,8},{1,9},{2,10},{3,11},{4,12},{5,13},{6,14},{7,15},{8,0},{9,1},... | collective-permute-start | bytes 61448 | tf_op jit(solution)/shard_map/ppermute | solution.py:438
  24.7 3.4 %collective-permute-done.refs_5_ = bf16[16,640]{1,0:T(8,128)(2,1)S(1)} collective-permute-done((bf16[16,640]{1,0:T(8,128)(2,1)S(1)}, bf16[16,640]{1,0:T(8,128)(2,1)S(1)}, u32[]{:S(2)}, u32[]{:S(2)}) %collective-permute-start) | collective-permute-done | bytes 20512 | tf_op jit(solution)/shard_map/ppermute | solution.py:438
  28.1 0.8 %collective-permute-done.2.refs_2_ = bf16[32,640]{1,0:T(8,128)(2,1)S(1)} collective-permute-done((bf16[32,640]{1,0:T(8,128)(2,1)S(1)}, bf16[32,640]{1,0:T(8,128)(2,1)S(1)}, u32[]{:S(2)}, u32[]{:S(2)}) %collective-permute-start.2) | collective-permute-done | bytes 40992 | tf_op jit(solution)/shard_map/ppermute | solution.py:438
  28.9 0.2 collective-permute-done.3.refs_3_
  29.1 0.5 collective-permute-done.4.refs_4_
  29.6 0.6 all-to-all-done
  30.2 0.6 collective-permute-start.6
  30.8 1.6 %fetch_keys.1.first_ref = bf16[2,576,768]{2,1,0:T(8,128)(2,1)S(1)} custom-call(bf16[512,640]{1,0:T(8,128)(2,1)S(1)} %bitcast.10, bf16[8,576,768]{2,1,0:T(8,128)(2,1)} %bitcast.16), custom_call_target="tpu_custom_call" | custom-call | bytes 3538944 | tf_op jit(solution)/shard_map/fetch_keys/pallas_call | solution.py:450
  32.5 0.1 collective-permute-done.6.refs_0_
  32.5 0.3 copy-done.5
  32.8 5.0 %attend.1 = (bf16[640,640]{1,0:T(8,128)(2,1)S(1)}, f32[640,512]{1,0:T(8,128)S(1)}, bf16[640,128]{1,0:T(8,128)(2,1)S(1)}) custom-call(bf16[8,576,768]{2,1,0:T(8,128)(2,1)} %bitcast.17, bf16[2,576,768]{2,1,0:T(8,128)(2,1)S(1)} %fetch_keys.1.first_ref, bf16[2,576,768]{2,1,0:T(8,128)(2,1)S(1)} %bitcast.15, bf16[512,640]{1,0:T(8,128)(2,1)S(1)} %bitcast.11, ...), custom_call_target="tpu_custom_call" | custom-call | flops 5000000000 | bytes 20000000 | tf_op jit(solution)/shard_map/attend/pallas_call | solution.py:461
  37.8 0.1 collective-permute-start.7
  37.9 2.3 %collective-permute-done.7.got_ref = bf16[640,640]{1,0:T(8,128)(2,1)S(1)} collective-permute-done((bf16[640,640]{1,0:T(8,128)(2,1)S(1)}, bf16[640,640]{1,0:T(8,128)(2,1)S(1)}, u32[]{:S(2)}, u32[]{:S(2)}) %collective-permute-start.7) | collective-permute-done | bytes 819232 | tf_op jit(solution)/shard_map/ppermute | solution.py:432
  40.3 1.3 %join_cores.1 = (bf16[512,640]{1,0:T(8,128)(2,1)}, bf16[32,640]{1,0:T(8,128)(2,1)S(1)}, bf16[32,640]{1,0:T(8,128)(2,1)S(1)}, bf16[32,640]{1,0:T(8,128)(2,1)S(1)}...) custom-call(bf16[640,640]{1,0:T(8,128)(2,1)S(1)} %collective-permute-done.7.got_ref, ...), custom_call_target="tpu_custom_call" | custom-call | tf_op jit(solution)/shard_map/join_cores/pallas_call | solution.py:475
  41.6 7.0 %all-to-all-start.1 = ((bf16[64,8,640]{2,1,0:T(8,128)(2,1)}), bf16[64,8,640]{2,1,0:T(8,128)(2,1)S(1)}, u32[]{:S(2)}, u32[]{:S(2)}) async-start(bf16[64,8,640]{2,1,0:T(8,128)(2,1)} %bitcast.7), calls=%async_computation.1 | async-start | bytes 1310720 | tf_op jit(solution)/shard_map/all_to_all | solution.py:429
  48.6 5.3 %collective-permute-start.10 = (bf16[32,640]{1,0:T(8,128)(2,1)S(1)}, bf16[32,640]{1,0:T(8,128)(2,1)S(1)}, u32[]{:S(2)}, u32[]{:S(2)}) collective-permute-start(bf16[32,640]{1,0:T(8,128)(2,1)S(1)} %get-tuple-element.48), channel_id=1, source_target_pairs={{0,14},{1,3},{2,0},{3,5},{4,2},{5,7},{6,4},{7,9},{8,6},{9,11},{10,... | collective-permute-start | bytes 122888 | tf_op jit(solution)/shard_map/ppermute | solution.py:438
  53.9 0.9 %collective-permute-start.11 = (bf16[32,640]{1,0:T(8,128)(2,1)S(1)}, bf16[32,640]{1,0:T(8,128)(2,1)S(1)}, u32[]{:S(2)}, u32[]{:S(2)}) collective-permute-start(bf16[32,640]{1,0:T(8,128)(2,1)S(1)} %get-tuple-element.49), channel_id=1, source_target_pairs={{0,12},{1,5},{2,14},{3,7},{4,0},{5,9},{6,2},{7,11},{8,4},{9,13},{1... | collective-permute-start | bytes 122888 | tf_op jit(solution)/shard_map/ppermute | solution.py:438
  54.7 0.6 collective-permute-start.9
  55.3 2.7 %collective-permute-start.8 = (bf16[16,640]{1,0:T(8,128)(2,1)S(1)}, bf16[16,640]{1,0:T(8,128)(2,1)S(1)}, u32[]{:S(2)}, u32[]{:S(2)}) collective-permute-start(bf16[16,640]{1,0:T(8,128)(2,1)S(1)} %get-tuple-element.46), channel_id=1, source_target_pairs={{0,8},{1,9},{2,10},{3,11},{4,12},{5,13},{6,14},{7,15},{8,0},{9,1},... | collective-permute-start | bytes 61448 | tf_op jit(solution)/shard_map/ppermute | solution.py:438
  58.0 1.0 %own_keys.1 = (f32[80,512]{1,0:T(8,128)S(1)}, f32[80,256]{1,0:T(8,128)S(1)}, bf16[32,80]{1,0:T(8,128)(2,1)S(1)}) custom-call(s32[1,8]{1,0:T(1,128)S(1)} %copy-done.3, s32[2,10]{1,0:T(2,128)S(1)} %bitcast.14, bf16[10,2,576]{2,1,0:T(2,128)(2,1)S(1)} %copy-done.1, f32[1,64]{1,0:T(1,128)S(1)} %copy-done.4, bf16[80,640]{1,0:T(8,128)(2,1)S(1)} %get-tuple-element.32.own_ref), custom_call_target="tpu_custom_call" | custom-call | tf_op jit(solution)/shard_map/own_keys/pallas_call | solution.py:414
  59.0 3.4 %collective-permute-done.8.refs_1_ = bf16[16,640]{1,0:T(8,128)(2,1)S(1)} collective-permute-done((bf16[16,640]{1,0:T(8,128)(2,1)S(1)}, bf16[16,640]{1,0:T(8,128)(2,1)S(1)}, u32[]{:S(2)}, u32[]{:S(2)}) %collective-permute-start.8) | collective-permute-done | bytes 20512 | tf_op jit(solution)/shard_map/ppermute | solution.py:438
  62.5 0.1 collective-permute-start.12
  62.6 1.7 %all-to-all-done.1 = bf16[64,8,640]{2,1,0:T(8,128)(2,1)S(1)} async-done(((bf16[64,8,640]{2,1,0:T(8,128)(2,1)}), bf16[64,8,640]{2,1,0:T(8,128)(2,1)S(1)}, u32[]{:S(2)}, u32[]{:S(2)}) %all-to-all-start.1) | async-done | bytes 655392 | tf_op jit(solution)/shard_map/all_to_all | solution.py:429
  64.3 0.7 finish_new.1.new_ref
  65.0 1.1 %finish.1 = bf16[10,2,512]{2,1,0:T(2,128)(2,1)} custom-call(bf16[32,80]{1,0:T(8,128)(2,1)S(1)} %get-tuple-element.50.order_ref, f32[80,512]{1,0:T(8,128)S(1)} %get-tuple-element.51.own_ref, f32[80,256]{1,0:T(8,128)S(1)} %get-tuple-element.52.stat_ref, bf16[4,512,128]{2,1,0:T(8,128)(2,1)S(1)} %copy-done, f32[32,512]{1,0:T(8,128)S(1)} %finish_new.1.new_ref, ...), custom_call_target="tpu_custom_call" | custom-call | tf_op jit(solution)/shard_map/finish/pallas_call | solution.py:504
  (24 shorter events, 0.1 us)
Async XLA Ops:
  3.2 27.0 %all-to-all-start = ((bf16[64,8,640]{2,1,0:T(8,128)(2,1)}), bf16[64,8,640]{2,1,0:T(8,128)(2,1)S(1)}, u32[]{:S(2)}, u32[]{:S(2)}) async-start(bf16[64,8,640]{2,1,0:T(8,128)(2,1)} %bitcast.3), calls=%async_computation | async-start | bytes 1310720 | tf_op jit(solution)/shard_map/all_to_all | solution.py:429
  14.8 1.3 %collective-permute-start.1 = (bf16[16,640]{1,0:T(8,128)(2,1)S(1)}, bf16[16,640]{1,0:T(8,128)(2,1)S(1)}, u32[]{:S(2)}, u32[]{:S(2)}) collective-permute-start(bf16[16,640]{1,0:T(8,128)(2,1)S(1)} %get-tuple-element.37.refs_6_), channel_id=1, source_target_pairs={{0,1},{1,0},{2,3},{3,2},{4,5},{5,4},{6,7},{7,6},{8,9},{9,8},{10,11... | collective-permute-start | bytes 61448 | tf_op jit(solution)/shard_map/ppermute | solution.py:432
  16.0 12.8 %collective-permute-start.2 = (bf16[32,640]{1,0:T(8,128)(2,1)S(1)}, bf16[32,640]{1,0:T(8,128)(2,1)S(1)}, u32[]{:S(2)}, u32[]{:S(2)}) collective-permute-start(bf16[32,640]{1,0:T(8,128)(2,1)S(1)} %constant_dynamic-update-slice_fusion), channel_id=1, source_target_pairs={{0,6},{1,11},{2,8},{3,13},{4,10},{5,15},{6,12},{7,1},{8,14},{9,3},... | collective-permute-start | bytes 122888 | tf_op jit(solution)/shard_map/ppermute | solution.py:438
  20.0 9.1 %collective-permute-start.3 = (bf16[32,640]{1,0:T(8,128)(2,1)S(1)}, bf16[32,640]{1,0:T(8,128)(2,1)S(1)}, u32[]{:S(2)}, u32[]{:S(2)}) collective-permute-start(bf16[32,640]{1,0:T(8,128)(2,1)S(1)} %constant_dynamic-update-slice_fusion), channel_id=1, source_target_pairs={{0,2},{1,15},{2,4},{3,1},{4,6},{5,3},{6,8},{7,5},{8,10},{9,7},{10,... | collective-permute-start | bytes 122888 | tf_op jit(solution)/shard_map/ppermute | solution.py:438
  22.1 7.5 %collective-permute-start.4 = (bf16[32,640]{1,0:T(8,128)(2,1)S(1)}, bf16[32,640]{1,0:T(8,128)(2,1)S(1)}, u32[]{:S(2)}, u32[]{:S(2)}) collective-permute-start(bf16[32,640]{1,0:T(8,128)(2,1)S(1)} %constant_dynamic-update-slice_fusion), channel_id=1, source_target_pairs={{0,4},{1,13},{2,6},{3,15},{4,8},{5,1},{6,10},{7,3},{8,12},{9,5},{1... | collective-permute-start | bytes 122888 | tf_op jit(solution)/shard_map/ppermute | solution.py:438
  22.6 5.5 %collective-permute-start = (bf16[16,640]{1,0:T(8,128)(2,1)S(1)}, bf16[16,640]{1,0:T(8,128)(2,1)S(1)}, u32[]{:S(2)}, u32[]{:S(2)}) collective-permute-start(bf16[16,640]{1,0:T(8,128)(2,1)S(1)} %get-tuple-element.37.refs_6_), channel_id=1, source_target_pairs={{0,8},{1,9},{2,10},{3,11},{4,12},{5,13},{6,14},{7,15},{8,0},{9,1},... | collective-permute-start | bytes 61448 | tf_op jit(solution)/shard_map/ppermute | solution.py:438
  30.2 2.3 %collective-permute-start.5 = (bf16[512,640]{1,0:T(8,128)(2,1)S(1)}, bf16[512,640]{1,0:T(8,128)(2,1)S(1)}, u32[]{:S(2)}, u32[]{:S(2)}) collective-permute-start(bf16[512,640]{1,0:T(8,128)(2,1)S(1)} %bitcast.9), channel_id=1, source_target_pairs={{0,1},{1,0},{2,3},{3,2},{4,5},{5,4},{6,7},{7,6},{8,9},{9,8},{10,11... | collective-permute-start | bytes 1966088 | tf_op jit(solution)/shard_map/ppermute | solution.py:432
  30.2 2.3 %collective-permute-start.6 = (bf16[112,640]{1,0:T(8,128)(2,1)S(1)}, bf16[112,640]{1,0:T(8,128)(2,1)S(1)}, u32[]{:S(2)}, u32[]{:S(2)}) collective-permute-start(bf16[112,640]{1,0:T(8,128)(2,1)S(1)} %pad_maximum_fusion), channel_id=1, source_target_pairs={{0,1},{1,0},{2,3},{3,2},{4,5},{5,4},{6,7},{7,6},{8,9},{9,8},{10,11... | collective-permute-start | bytes 430088 | tf_op jit(solution)/shard_map/ppermute | solution.py:432
  30.8 2.0 %copy-start.5 = (bf16[2,768,576]{1,2,0:T(8,128)(2,1)S(1)}, bf16[2,768,576]{1,2,0:T(8,128)(2,1)}, u32[]{:S(2)}) copy-start(bf16[2,768,576]{1,2,0:T(8,128)(2,1)} %param.15) | copy-start | bytes 5308420
  37.8 2.4 %collective-permute-start.7 = (bf16[640,640]{1,0:T(8,128)(2,1)S(1)}, bf16[640,640]{1,0:T(8,128)(2,1)S(1)}, u32[]{:S(2)}, u32[]{:S(2)}) collective-permute-start(bf16[640,640]{1,0:T(8,128)(2,1)S(1)} %get-tuple-element.43), channel_id=1, source_target_pairs={{0,1},{1,0},{2,3},{3,2},{4,5},{5,4},{6,7},{7,6},{8,9},{9,8},{10,11... | collective-permute-start | bytes 2457608 | tf_op jit(solution)/shard_map/ppermute | solution.py:432
  40.3 17.7 %copy-start.1 = (bf16[10,2,576]{2,1,0:T(2,128)(2,1)S(1)}, bf16[10,2,576]{2,1,0:T(2,128)(2,1)}, u32[]{:S(2)}) copy-start(bf16[10,2,576]{2,1,0:T(2,128)(2,1)} %nl_ref.1) | copy-start | bytes 69124
  40.3 17.7 %copy-start.2 = (s32[10,2]{0,1:T(2,128)S(1)}, s32[10,2]{0,1:T(2,128)}, u32[]{:S(2)}) copy-start(s32[10,2]{0,1:T(2,128)} %param.20) | copy-start | bytes 244
  40.3 17.7 %copy-start.3 = (s32[1,8]{1,0:T(1,128)S(1)}, s32[1,8]{1,0:T(1,128)}, u32[]{:S(2)}) copy-start(s32[1,8]{1,0:T(1,128)} %slot_ref.1) | copy-start | bytes 100
  40.3 17.7 %copy-start.4 = (f32[1,64]{1,0:T(1,128)S(1)}, f32[1,64]{1,0:T(1,128)}, u32[]{:S(2)}) copy-start(f32[1,64]{1,0:T(1,128)} %constant.2.clone.freq_hbm.freq_ref) | copy-start | bytes 772
  40.3 24.1 %copy-start = (bf16[4,512,128]{2,1,0:T(8,128)(2,1)S(1)}, bf16[4,512,128]{2,1,0:T(8,128)(2,1)}, u32[]{:S(2)}) copy-start(bf16[4,512,128]{2,1,0:T(8,128)(2,1)} %wv_ref.3) | copy-start | bytes 1572868
  41.6 22.7 %all-to-all-start.1 = ((bf16[64,8,640]{2,1,0:T(8,128)(2,1)}), bf16[64,8,640]{2,1,0:T(8,128)(2,1)S(1)}, u32[]{:S(2)}, u32[]{:S(2)}) async-start(bf16[64,8,640]{2,1,0:T(8,128)(2,1)} %bitcast.7), calls=%async_computation.1 | async-start | bytes 1310720 | tf_op jit(solution)/shard_map/all_to_all | solution.py:429
  48.6 13.8 %collective-permute-start.10 = (bf16[32,640]{1,0:T(8,128)(2,1)S(1)}, bf16[32,640]{1,0:T(8,128)(2,1)S(1)}, u32[]{:S(2)}, u32[]{:S(2)}) collective-permute-start(bf16[32,640]{1,0:T(8,128)(2,1)S(1)} %get-tuple-element.48), channel_id=1, source_target_pairs={{0,14},{1,3},{2,0},{3,5},{4,2},{5,7},{6,4},{7,9},{8,6},{9,11},{10,... | collective-permute-start | bytes 122888 | tf_op jit(solution)/shard_map/ppermute | solution.py:438
  53.9 8.6 %collective-permute-start.11 = (bf16[32,640]{1,0:T(8,128)(2,1)S(1)}, bf16[32,640]{1,0:T(8,128)(2,1)S(1)}, u32[]{:S(2)}, u32[]{:S(2)}) collective-permute-start(bf16[32,640]{1,0:T(8,128)(2,1)S(1)} %get-tuple-element.49), channel_id=1, source_target_pairs={{0,12},{1,5},{2,14},{3,7},{4,0},{5,9},{6,2},{7,11},{8,4},{9,13},{1... | collective-permute-start | bytes 122888 | tf_op jit(solution)/shard_map/ppermute | solution.py:438
  54.7 7.7 %collective-permute-start.9 = (bf16[32,640]{1,0:T(8,128)(2,1)S(1)}, bf16[32,640]{1,0:T(8,128)(2,1)S(1)}, u32[]{:S(2)}, u32[]{:S(2)}) collective-permute-start(bf16[32,640]{1,0:T(8,128)(2,1)S(1)} %get-tuple-element.47), channel_id=1, source_target_pairs={{0,10},{1,7},{2,12},{3,9},{4,14},{5,11},{6,0},{7,13},{8,2},{9,15},... | collective-permute-start | bytes 122888 | tf_op jit(solution)/shard_map/ppermute | solution.py:438
  55.3 7.1 %collective-permute-start.8 = (bf16[16,640]{1,0:T(8,128)(2,1)S(1)}, bf16[16,640]{1,0:T(8,128)(2,1)S(1)}, u32[]{:S(2)}, u32[]{:S(2)}) collective-permute-start(bf16[16,640]{1,0:T(8,128)(2,1)S(1)} %get-tuple-element.46), channel_id=1, source_target_pairs={{0,8},{1,9},{2,10},{3,11},{4,12},{5,13},{6,14},{7,15},{8,0},{9,1},... | collective-permute-start | bytes 61448 | tf_op jit(solution)/shard_map/ppermute | solution.py:438
  62.5 2.5 %collective-permute-start.12 = (bf16[48,640]{1,0:T(8,128)(2,1)S(1)}, bf16[48,640]{1,0:T(8,128)(2,1)S(1)}, u32[]{:S(2)}, u32[]{:S(2)}) collective-permute-start(bf16[48,640]{1,0:T(8,128)(2,1)S(1)} %pad_maximum_fusion.1), channel_id=1, source_target_pairs={{0,1},{1,0},{2,3},{3,2},{4,5},{5,4},{6,7},{7,6},{8,9},{9,8},{10,11... | collective-permute-start | bytes 184328 | tf_op jit(solution)/shard_map/ppermute | solution.py:432
